TPU v7x, 32 devices: a whole 2x2x4 slice. The times are simulated.
32 devices in a mesh: rows: 16 (over z, y, x), seq: 2 (over core).
Axes of the slice: x: 2, y: 2, z: 4, core: 2. Of those that a mesh axis runs over, the one named last changes fastest.
Arguments:
- tokens_a: bfloat16 [64, 512, 768], P('rows', 'seq'), may hold values from -6 to 6
- lengths_a: int32 [64], P('rows'), may hold values from 128 to 512, as said below
- cotangent_a: bfloat16 [64, 512, 768], P('rows', 'seq'), may hold values from -6 to 6
- tokens_b: bfloat16 [128, 256, 768], P('rows', 'seq'), may hold values from -6 to 6
- lengths_b: int32 [128], P('rows'), may hold values from 64 to 256, as said below
- cotangent_b: bfloat16 [128, 256, 768], P('rows', 'seq'), may hold values from -6 to 6
- gain_attn: float32 [768], replicated, may hold values from 0.25 to 1.75
- w_query: bfloat16 [768, 768], replicated, may hold values from -0.0546875 to 0.0546875
- w_key: bfloat16 [768, 768], replicated, may hold values from -0.21875 to 0.21875
- w_value: bfloat16 [768, 768], replicated, may hold values from -0.21875 to 0.21875
- w_out: bfloat16 [768, 768], replicated, may hold values from -0.875 to 0.875
- relative_bias_table: float32 [32, 12], replicated, may hold values from -4 to 4
- gain_ffn: float32 [768], replicated, may hold values from 0.25 to 1.75
- w_in: bfloat16 [768, 3072], replicated, may hold values from -0.21875 to 0.21875
- w_back: bfloat16 [3072, 768], replicated, may hold values from -0.15625 to 0.15625
Outputs:
- out_a: bfloat16 [64, 512, 768], P('rows', 'seq')
- out_b: bfloat16 [128, 256, 768], P('rows', 'seq')
- grad_tokens_a: bfloat16 [64, 512, 768], P('rows', 'seq')
- grad_tokens_b: bfloat16 [128, 256, 768], P('rows', 'seq')
- grad_gain_attn: float32 [768], replicated
- grad_query: float32 [768, 768], P('rows', 'seq')
- grad_key: float32 [768, 768], P('rows', 'seq')
- grad_value: float32 [768, 768], P('rows', 'seq')
- grad_out: float32 [768, 768], P('rows', 'seq')
- grad_table: float32 [32, 12], replicated
- grad_gain_ffn: float32 [768], replicated
- grad_in: float32 [768, 3072], P('rows', 'seq')
- grad_back: float32 [3072, 768], P('rows', 'seq')
Inputs may be any that keep to these rules, and one draw needn't show every extreme that they name: `lengths_a`: real tokens of each sequence; keys at positions at or beyond it are padding. In every draw some sequence has exactly 512. `lengths_b`: real tokens of each sequence; keys at positions at or beyond it are padding. In every draw some sequence has exactly 256.
All inputs are finite; a program needn't handle non-finite values.
Results may differ from a plain program's by a relative error of at most 0.015.
Values may be sent and summed in bfloat16 or wider, within the bound.
No kernel may reach another device: no remote copies, remote signals or barrier semaphores. Data moves between devices by JAX's collectives and lax.ppermute only.
A program may use at most 384 MiB of HBM per device.

v0:
```python
import functools

import jax
import jax.numpy as jnp
from jax import lax
from jax.experimental import pallas as pl
from jax.experimental.pallas import tpu as pltpu
from jax.sharding import PartitionSpec as P

EPS = 1e-06
EDGES = (12, 16, 23, 32, 46, 64, 91)
MASKED = -1e30
C1 = 0.7978845608
C3 = 0.044715
BF = jnp.bfloat16
F32 = jnp.float32
HEAD = 64
PAIR = 2 * HEAD
MIB = 1 << 20


def dot(a, b, ca, cb):
    return lax.dot_general(a, b, (((ca,), (cb,)), ((), ())), preferred_element_type=F32)


def exact(a, b):
    return lax.dot_general(
        a, b, (((1,), (0,)), ((), ())), precision=lax.Precision.HIGHEST, preferred_element_type=F32
    )


def sds(shape, dtype):
    return jax.ShapeDtypeStruct(shape, dtype)


def call(kernel, grid, in_specs, out_specs, out_shape, scratch=(), flops=0, nbytes=0, vmem=60, after=(), free=(), aliases=None):
    count, extra = len(in_specs), len(after)

    def run(meta, *refs):
        kernel(meta, *refs[:count], *refs[count + extra :])

    def large(x):
        return x.size * x.dtype.itemsize >= MIB

    def put(x):
        return pltpu.HBM(x.shape, x.dtype) if large(x) else x

    in_specs = list(in_specs) + [pl.BlockSpec(memory_space=pl.ANY)] * extra
    made = pl.pallas_call(
        run,
        grid_spec=pltpu.PrefetchScalarGridSpec(
            num_scalar_prefetch=1,
            grid=grid,
            in_specs=in_specs,
            out_specs=out_specs,
            scratch_shapes=list(scratch),
        ),
        out_shape=[put(x) for x in out_shape] if isinstance(out_shape, list) else put(out_shape),
        input_output_aliases=aliases or {},
        compiler_params=pltpu.CompilerParams(vmem_limit_bytes=vmem * MIB),
        cost_estimate=pl.CostEstimate(flops=int(flops), bytes_accessed=int(nbytes), transcendentals=0),
    )

    def place(i, x):
        return pltpu.with_memory_space_constraint(x, pltpu.HBM) if large(x) and i not in free else x

    return lambda *args: made(*(place(i, x) for i, x in enumerate((*args, *after))))


def whole(shape):
    return pl.BlockSpec(shape, lambda *_: (0,) * len(shape))


def bucket_of(rel, buckets):
    n = jnp.abs(rel)
    far = jnp.full(rel.shape, 8, jnp.int32)
    for edge in EDGES:
        far = far + (n >= edge).astype(jnp.int32)
    return jnp.where(n < 8, n, far) + jnp.where(rel > 0, buckets // 2, 0)


def strip_kernel(meta, table, hot, strip, *, base, buckets):
    near0, near1 = base - 96, base + 224
    heads = strip.shape[0]
    lines = lax.dot_general(
        table[0], hot[...], (((1,), (1,)), ((), ())), precision=lax.Precision.HIGHEST, preferred_element_type=F32
    )
    shape = (near1 - near0, 128)
    rel = near0 - base + lax.broadcasted_iota(jnp.int32, shape, 0) - lax.broadcasted_iota(jnp.int32, shape, 1)
    for h in range(heads):
        wide = jnp.broadcast_to(lines[h : h + 1], (near1 - near0, 256))
        near = pltpu.roll(wide, 0, 1, stride=1, stride_axis=0)[:, :128]
        minus = table[0, h : h + 1, buckets // 2 - 1 : buckets // 2]
        plus = table[0, h : h + 1, buckets - 1 : buckets]
        strip[h, near0:near1, :] = jnp.where(rel >= EDGES[-1], plus, jnp.where(rel <= -EDGES[-1], minus, near))
        strip[h, :near0, :] = jnp.broadcast_to(minus, (near0, 128))
        strip[h, near1:, :] = jnp.broadcast_to(plus, (strip.shape[1] - near1, 128))


def pick_kernel(meta, a, b, out):
    @pl.when(pl.program_id(0) == 0)
    def _():
        out[...] = flat(a)

    @pl.when(pl.program_id(0) == 1)
    def _():
        out[...] = flat(b)


def place_kernel(meta, out_got, grad_got, a0, b0, a1, b1, out_a, out_b, grad_a, grad_b):
    @pl.when(pl.program_id(0) == 0)
    def _():
        out_a[...] = out_got[...].reshape(out_a.shape)
        grad_a[...] = grad_got[...].reshape(grad_a.shape)

    @pl.when(pl.program_id(0) == 1)
    def _():
        out_b[...] = out_got[...].reshape(out_b.shape)
        grad_b[...] = grad_got[...].reshape(grad_b.shape)


def gathered(i, a, b, rest, out):
    @pl.when(i == 0)
    def _():
        out[...] = flat(a)

    @pl.when(i == 1)
    def _():
        out[...] = flat(b)

    @pl.when(i > 1)
    def _():
        out[...] = rest[...]


def qkv_kernel(meta, xa, xb, xr, gain, wq, wk, wv, x_ref, normed, q, k, v):
    gathered(pl.program_id(0), xa, xb, xr, x_ref.at[0])
    x = x_ref[0].astype(F32)
    r = lax.rsqrt(jnp.mean(x * x, axis=-1, keepdims=True) + EPS)
    n = (x * r * gain[...]).astype(BF)
    normed[0] = n
    q[0] = dot(n, wq[...], 1, 0).astype(BF)
    k[0] = dot(n, wk[...], 1, 0).astype(BF)
    v[0] = dot(n, wv[...], 1, 0).astype(BF)


def units_of(na, la, nb, lb):
    out = [(0, s, la, s * la // 2) for s in range(na)]
    return out + [(1, s, lb, na * la // 2 + s * lb // 2) for s in range(nb)]


def joined(ref, off, half):
    return jnp.concatenate([ref[0, off : off + half, :], ref[1, off : off + half, :]], axis=0)


def strip_rows(flip, base, size, cb, kh):
    half = size // 2
    plain = base - 128 * cb + half * kh
    if flip is None:
        return plain
    moved = (128 * cb + half) % size
    return pl.multiple_of(jnp.where(flip == 0, plain, base - moved + half * (1 - kh)), 128)


def lanes_of(shape, high):
    lane = lax.broadcasted_iota(jnp.int32, shape, len(shape) - 1)
    return (lane >= HEAD) == high


def half_mask(high):
    return jnp.where(lanes_of((1, PAIR), high), 1.0, 0.0).astype(BF)


def attn_kernel(meta, q, k, v, strip, pa, pb, attn, linv, kaug, *, dims, base):
    na, la, nb, lb = dims
    flip = meta[0]

    @pl.when(pl.program_id(0) == 0)
    def _():
        for kind, s, size, off in units_of(*dims):
            half = size // 2
            for kh in range(2):
                row = lax.broadcasted_iota(jnp.int32, (half, 128), 0)
                start = jnp.where(flip == 0, half * kh, half * (1 - kh))
                length = meta[3 + (s if kind == 0 else na + s)]
                lane = lax.broadcasted_iota(jnp.int32, (half, 128), 1)
                gone = jnp.logical_and(row + start >= length, lane == 0)
                kaug[kh, off : off + half, :] = jnp.where(gone, MASKED, 0.0).astype(BF)

    low_lanes = lax.broadcasted_iota(jnp.int32, (1, PAIR), 1) < HEAD
    for kind, s, size, off in units_of(*dims):
        half = size // 2
        pref = pa if kind == 0 else pb
        q2, k2, v2 = joined(q, off, half), joined(k, off, half), joined(v, off, half)
        first = jnp.where(lax.broadcasted_iota(jnp.int32, (size, 128), 1) == 0, 1.0, 0.0).astype(BF)
        ones = jnp.ones((size, 128), BF)
        qa = jnp.concatenate([q2, first], axis=1)
        ka = joined(kaug, off, half)
        mixed, inverse = [], []
        for h in range(2):
            kk = jnp.concatenate([k2 * half_mask(h == 1), ka], axis=1)
            for c2 in range(size // 256):
                scores = dot(kk, qa[256 * c2 : 256 * c2 + 256], 1, 1)
                for sub in range(2):
                    cb = 2 * c2 + sub
                    bias = jnp.concatenate(
                        [strip[h, pl.ds(strip_rows(flip, base, size, cb, kh), half), :] for kh in range(2)], axis=0
                    )
                    one = scores[:, 128 * sub : 128 * sub + 128] + bias
                    e = jnp.exp(one - jnp.max(one, axis=0, keepdims=True))
                    pref[h, s, :, 128 * cb : 128 * cb + 128] = e.astype(BF)
            va = jnp.concatenate([v2 * half_mask(h == 1), ones], axis=1)
            both = dot(pref[h, s], va, 0, 0)
            inv = 1.0 / both[:, PAIR:]
            mixed.append(both[:, :PAIR] * inv)
            inverse.append(inv)
        o = (mixed[0] + mixed[1]).astype(BF)
        inv = jnp.where(low_lanes, inverse[0], inverse[1]).astype(BF)
        attn[0, off : off + half, :] = o[:half]
        attn[1, off : off + half, :] = o[half:]
        linv[0, off : off + half, :] = inv[:half]
        linv[1, off : off + half, :] = inv[half:]


def ffn_kernel(
    meta, attn, x, w_out, gain, ga, gb, gr, w_in, w_back,
    hidden, g_out, low, back_send, back_keep, in_send, in_keep, d_normed, normed, d_inner, acc, g, *, mixes, chunk,
):
    i = pl.program_id(0)
    th, tile = g.shape[1], x.shape[1]
    per = th // tile

    @pl.when(i < mixes)
    def _():
        h = x[0].astype(F32) + dot(attn[0], w_out[...], 1, 0)
        r = lax.rsqrt(jnp.mean(h * h, axis=-1, keepdims=True) + EPS)
        hidden[0] = h.astype(BF)
        at = pl.ds(pl.multiple_of((i % per) * tile, tile), tile)
        normed[i // per, at, :] = (h * r * gain[...]).astype(BF)
        gathered(i, ga, gb, gr, g_out.at[0])
        g[i // per, at, :] = g_out[0]

    @pl.when(i == mixes)
    def _():
        acc[...] = jnp.zeros_like(acc)

    @pl.when(i >= mixes)
    def _():
        for part in range(2):
            for lo in range(0, th, chunk):
                rows = slice(lo, lo + chunk)
                v = dot(normed[part, rows, :], w_in[...], 1, 0)
                gw = dot(g[part, rows, :], w_back[...], 1, 1)
                u = v * v
                up = 0.5 + 0.5 * jnp.tanh(v * (C1 + (C1 * C3) * u))
                low[part, rows, :] = (v * up).astype(BF)
                slope = up + up * ((1.0 - up) * (v * (2.0 * C1 + (6.0 * C1 * C3) * u)))
                inner = (gw * slope).astype(BF)
                d_inner[part, rows, :] = inner
                acc[part, rows, :] += dot(inner, w_in[...], 1, 1)
        split_columns(meta, dot(flat(low), flat(g), 0, 0), back_send, back_keep)
        value = dot(flat(normed), flat(d_inner), 0, 0).astype(BF)
        sending = i < mixes + (pl.num_programs(0) - mixes) // 2

        @pl.when(sending)
        def _():
            in_send[...] = value

        @pl.when(jnp.logical_not(sending))
        def _():
            in_keep[...] = value

    @pl.when(i == pl.num_programs(0) - 1)
    def _():
        d_normed[...] = acc[...].astype(BF)


def flat(ref):
    a = ref[...]
    return a.reshape(a.shape[0] * a.shape[1], a.shape[2])


def split_columns(meta, value, send, keep):
    half = value.shape[1] // 2
    lo, hi = value[:, :half].astype(BF), value[:, half:].astype(BF)
    first = meta[1] == 0

    @pl.when(first)
    def _():
        keep[...] = lo
        send[...] = hi

    @pl.when(jnp.logical_not(first))
    def _():
        keep[...] = hi
        send[...] = lo


def rows8(value):
    return jnp.sum(value.reshape(value.shape[0] // 8, 8, value.shape[1]), axis=0)


def hidden_kernel(meta, d_normed, hidden, g, gain, w_out, attn, linv, d_hidden, d_attn, small, send, keep, acc):
    i, last = pl.program_id(0), pl.num_programs(0) - 1
    dn = d_normed[0].astype(F32)
    h = hidden[0].astype(F32)
    r = lax.rsqrt(jnp.mean(h * h, axis=-1, keepdims=True) + EPS)
    gained = dn * gain[...]
    mean = jnp.mean(gained * h, axis=-1, keepdims=True)
    dh = (g[0].astype(F32) + r * gained - h * (r * r * r * mean)).astype(BF)
    d_hidden[0] = dh
    d_attn[0] = (dot(dh, w_out[...], 1, 1) * linv[0].astype(F32)).astype(BF)
    part = rows8(dn * h * r)
    product = dot(attn[0], dh, 0, 0)

    @pl.when(i == 0)
    def _():
        small[...] = part
        acc[...] = product

    @pl.when(i > 0)
    def _():
        small[...] += part
        acc[...] += product

    @pl.when(i == last)
    def _():
        split_columns(meta, acc[...], send, keep)


def table_sums(strip, hot, base, buckets):
    near0, near1 = base - 96, base + 224
    lines, ends = [], []
    for h in range(strip.shape[0]):
        near = strip[h, near0:near1, :]
        rel = (
            near0 - base + lax.broadcasted_iota(jnp.int32, near.shape, 0) - lax.broadcasted_iota(jnp.int32, near.shape, 1)
        )
        plus = rows8(strip[h, near1:, :]) + rows8(jnp.where(rel >= 128, near, 0.0))
        minus = rows8(strip[h, :near0, :]) + rows8(jnp.where(rel <= -128, near, 0.0))
        wide = jnp.where(jnp.abs(rel) < 128, near, 0.0)
        wide = jnp.concatenate([wide, jnp.zeros_like(wide)], axis=1)
        line = jnp.zeros((8, 256), F32)
        for r in range(0, near1 - near0, 8):
            line = line + pltpu.roll(wide[r : r + 8], -r % 256, 1)
        one = jnp.zeros((8, 256), F32)
        row = lax.broadcasted_iota(jnp.int32, (8, 256), 0)
        for r in range(8):
            one = one + pltpu.roll(jnp.where(row == r, line, 0.0), -r % 256, 1)
        lines.append(jnp.sum(one, axis=0, keepdims=True))
        ends.append((jnp.sum(plus, keepdims=True), jnp.sum(minus, keepdims=True)))
    fill = [jnp.zeros((8 - len(lines), 256), F32)]
    sums = exact(jnp.concatenate(lines + fill, axis=0), hot[...])
    lane = lax.broadcasted_iota(jnp.int32, (8, 128), 1)
    row = lax.broadcasted_iota(jnp.int32, (8, 128), 0)
    for h, (plus, minus) in enumerate(ends):
        here = row == h
        sums = sums + jnp.where(jnp.logical_and(here, lane == buckets - 1), plus, 0.0)
        sums = sums + jnp.where(jnp.logical_and(here, lane == buckets // 2 - 1), minus, 0.0)
    return sums


def attn_back_kernel(
    meta, q, k, v, do, at_ref, pa, pb, normed, wqs, wks, wvs, wqk, wkk, wvk, hot,
    dq, dk, dv, table, send, keep, gain, strip, dsa, dsb, cat, *, dims, base, buckets
):
    flip = meta[0]
    step = pl.program_id(0)
    th = normed.shape[1]
    strip[...] = jnp.zeros_like(strip)
    lane = lax.broadcasted_iota(jnp.int32, (1, PAIR), 1)
    minus = jnp.where(lane < 2, -1.0, 0.0).astype(BF)
    for kind, s, size, off in units_of(*dims):
        half = size // 2
        pref = pa if kind == 0 else pb
        ds_ref = dsa if kind == 0 else dsb
        q2, k2, v2, o2, a2 = (joined(ref, off, half) for ref in (q, k, v, do, at_ref))
        prod = o2.astype(F32) * a2.astype(F32)
        dvs, dks, dqs = [], [], []
        for h in range(2):
            mask = half_mask(h == 1)
            delta = jnp.sum(jnp.where((lane >= HEAD) == (h == 1), prod, 0.0), axis=1, keepdims=True)
            high = delta.astype(BF).astype(F32)
            cols = jnp.where(lane == 0, high, jnp.where(lane == 1, delta - high, 0.0)).astype(BF)
            va = jnp.concatenate([v2 * mask, jnp.broadcast_to(minus, (size, PAIR))], axis=1)
            oa = jnp.concatenate([o2, cols], axis=1)
            for c2 in range(size // 256):
                dp = dot(va, oa[256 * c2 : 256 * c2 + 256], 1, 1)
                for sub in range(2):
                    cb = 2 * c2 + sub
                    cs = slice(128 * cb, 128 * cb + 128)
                    ds = pref[h, s, :, cs].astype(F32) * dp[:, 128 * sub : 128 * sub + 128]
                    for kh in range(2):
                        at = pl.ds(strip_rows(flip, base, size, cb, kh), half)
                        strip[h, at, :] += ds[half * kh : half * kh + half]
                    ds_ref[h, :, cs] = ds.astype(BF)
            dvs.append(dot(pref[h, s], o2 * mask, 1, 0))
            dks.append(dot(ds_ref[h], q2 * mask, 1, 0))
            dqs.append(dot(ds_ref[h], k2 * mask, 0, 0))
        d_v = (dvs[0] + dvs[1]).astype(BF)
        d_k = (dks[0] + dks[1]).astype(BF)
        d_q = (dqs[0] + dqs[1]).astype(BF)
        for part in range(2):
            rows = slice(off, off + half)
            got = slice(part * half, part * half + half)
            dq[part, rows, :] = d_q[got]
            dk[part, rows, :] = d_k[got]
            dv[part, rows, :] = d_v[got]
            at = slice(part * th + off, part * th + off + half)
            cat[step, at, 0:128] = d_q[got]
            cat[step, at, 128:256] = d_k[got]
            cat[step, at, 256:384] = d_v[got]
    table[0] = table_sums(strip, hot, base, buckets)

    @pl.when(step == 1)
    def _():
        both = jnp.concatenate([cat[0], cat[1]], axis=1)
        value = dot(flat(normed), both, 0, 0)
        send[...] = value[:, :384].astype(BF)
        keep[...] = value[:, 384:].astype(BF)
        gain[...] = sum(
            value[:, 128 * i : 128 * i + 128] * w[...].astype(F32) for i, w in enumerate((wqs, wks, wvs, wqk, wkk, wvk))
        )


def spread(i, value, first, second):
    @pl.when(i == 0)
    def _():
        first[...] = value.reshape(first.shape)

    @pl.when(i == 1)
    def _():
        second[...] = value.reshape(second.shape)


def out_kernel(meta, low, w_back, hidden, give, out_a, out_b):
    i = pl.program_id(0)
    value = (hidden[0].astype(F32) + dot(low[0], w_back[...], 1, 0)).astype(BF)

    @pl.when(i < 2)
    def _():
        give[...] = value

    spread(i - 2, value, out_a, out_b)


def tokens_kernel(meta, *refs):
    wq, wk, wv, x_ref, d_hidden, gain = refs[9:15]
    outs = refs[15:]

    def columns(of):
        return jnp.concatenate([r[0, :, :PAIR] for r in of] + [r[0, :, PAIR:] for r in of], axis=1)

    dq, dk, dv = columns(refs[0:3]), columns(refs[3:6]), columns(refs[6:9])
    dn = dot(dq, wq[...], 1, 1) + dot(dk, wk[...], 1, 1) + dot(dv, wv[...], 1, 1)
    x = x_ref[0].astype(F32)
    r = lax.rsqrt(jnp.mean(x * x, axis=-1, keepdims=True) + EPS)
    gained = dn * gain[...]
    mean = jnp.mean(gained * x, axis=-1, keepdims=True)
    value = (d_hidden[0].astype(F32) + r * gained - x * (r * r * r * mean)).astype(BF)
    if len(outs) == 1:
        outs[0][...] = value
    else:
        spread(pl.program_id(0), value, *outs)


def swap(x, axis, bit):
    n = lax.axis_size(axis)
    return lax.ppermute(x, axis, [(i, i ^ bit) for i in range(n)])


TAIL = 16


class Piece:
    def __init__(self, parts, bits_left, carrier=False):
        self.parts, self.left, self.carrier, self.flat = parts, bits_left, carrier, 0

    def rows(self, cols):
        return self.flat or sum(t[0].shape[-2] * t[0].shape[-1] // cols for t in self.parts)

    def count(self, bits):
        return 1 << (len(self.left) - len(bits))


def blocks(x, bits):
    return x.reshape((2,) * bits + (x.shape[0] >> bits, x.shape[1]))


def masks_of(bits):
    return [tuple((m >> i) & 1 for i in range(len(bits))) for m in range(1 << len(bits))]


def shuttle(meta, cols, work, finals, after, small=((), ()), through=()):
    pieces, results = finals
    ins = []

    def slot(x):
        for i, y in enumerate(ins):
            if y is x:
                return i
        ins.append(x)
        return len(ins) - 1

    every = [piece for piece, _ in work] + pieces
    slots = []
    for piece in every:
        slots.append([[(slot(t[0]), t[1]) if piece.flat else (slot(t), 0) for t in terms] for terms in piece.parts])
    small_at, tail_at = [slot(x) for x in small[0]], [slot(x) for x in small[1]]
    messages = {}
    for number, (piece, bits) in enumerate(work):
        for mask in masks_of(bits):
            wide = sum(flip << b for flip, b in zip(mask, bits))
            entry = messages.setdefault(wide, [0, False, []])
            entry[2].append((number, mask, entry[0]))
            entry[0] += piece.count(bits) * piece.rows(cols)
            entry[1] |= piece.carrier and wide > 0
    outs = [sds((rows + (TAIL if tail else 0), cols), BF) for rows, tail, _ in messages.values()]
    outs += [sds((spans[0][2], sum(s[4] for s in spans)), F32) for spans in results]
    if small_at:
        outs.append(sds(small[0][0].shape, F32))

    def kernel(meta, *refs):
        got, put = refs[: len(ins)], list(refs[len(ins) + len(through) : len(ins) + len(through) + len(outs)])
        row = meta[2]
        if small_at:
            total = sum(got[i][...] for i in small_at)
            for i in tail_at:
                end = got[i].shape[0]
                tail = got[i][end - TAIL : end, :].astype(F32)
                total = total + tail[: TAIL // 2] + tail[TAIL // 2 :]
            put[-1][...] = total
            high = total.astype(BF).astype(F32)
            tail = jnp.concatenate([high, total - high], axis=0).astype(BF)

        def take(piece, terms, index):
            if not piece.flat:
                return sum(got[i][index].astype(F32) for i, _ in terms)
            at = 0
            for bit in index:
                at = 2 * at + bit
            value = 0.0
            for i, low in terms:
                start = low + at * piece.flat
                value = value + got[i][pl.ds(pl.multiple_of(start, 16) if index else start, piece.flat), :].astype(F32)
            return value

        for (rows, tailed, entries), out in zip(messages.values(), put):
            for number, mask, low in entries:
                piece, bits = work[number]
                rest = [b for b in piece.left if b not in bits]
                for m in range(1 << len(rest)):
                    chosen = {b: (m >> i) & 1 for i, b in enumerate(rest)}
                    for b, flip in zip(bits, mask):
                        chosen[b] = ((row >> b) & 1) ^ flip
                    index = tuple(chosen[b] for b in reversed(piece.left))
                    for terms in slots[number]:
                        value = take(piece, terms, index).astype(BF)
                        high = value.shape[0]
                        for c in range(0, value.shape[1], cols):
                            out[low : low + high, :] = value[:, c : c + cols]
                            low += high
            if tailed:
                out[rows : rows + TAIL, :] = tail
        sums = [take(piece, slots[len(work) + i][0], ()) for i, piece in enumerate(pieces)]
        for spans, out in zip(results, put[len(messages) :]):
            low = 0
            for piece, r0, r, c0, c in spans:
                out[:, low : low + c] = sums[piece][r0 : r0 + r, c0 : c0 + c]
                low += c

    made = call(
        kernel,
        (1,),
        [whole(x.shape) for x in ins] + [pl.BlockSpec(memory_space=pl.ANY)] * len(through),
        [whole(x.shape) for x in outs] + [pl.BlockSpec(memory_space=pl.ANY)] * len(through),
        outs + [sds(x.shape, x.dtype) for x in through],
        nbytes=sum(x.size * 2 for x in ins),
        vmem=30,
        after=after,
        aliases={1 + len(ins) + i: len(outs) + i for i in range(len(through))},
    )(meta, *ins, *through)
    made, passed = list(made[: len(outs)]), made[len(outs) :]
    got = {wide: swap(x, "rows", wide) if wide else x for wide, x in zip(messages, made)}
    tails = []
    for number, (piece, bits) in enumerate(work):
        rows = piece.rows(cols)
        terms = []
        for wide, (_, tailed, entries) in messages.items():
            for other, _, low in entries:
                if other == number:
                    terms.append((got[wide], low))
                    if piece.carrier and tailed:
                        tails.append(got[wide])
        piece.parts, piece.flat = [terms], rows
        piece.left = tuple(b for b in piece.left if b not in bits)
    ends = len(messages) + len(results)
    return made[len(messages) : ends], (made[ends:], tails), [*made, *passed]


def body(
    tokens_a, lengths_a, cotangent_a, tokens_b, lengths_b, cotangent_b,
    gain_attn, w_query, w_key, w_value, w_out, relative_bias_table, gain_ffn, w_in, w_back,
):
    nseq, nrows = lax.axis_size("seq"), lax.axis_size("rows")
    c = lax.axis_index("seq")
    width = tokens_a.shape[2]
    ff = w_in.shape[1]
    buckets, head_count = relative_bias_table.shape
    la, lb = tokens_a.shape[1] * nseq, tokens_b.shape[1] * nseq
    na, nb = tokens_a.shape[0] // nseq, tokens_b.shape[0] // nseq
    dims = (na, la, nb, lb)
    th = (na * la + nb * lb) // 2
    tokens = 2 * th
    base = la - 128
    strip_len = 2 * la - 128
    pairs = head_count // 2
    paired = nseq == 2 and nrows == 16

    me = c if paired else jnp.int32(0)
    flip = me
    own_a = lax.dynamic_slice_in_dim(lengths_a, c * na, na, 0)
    own_b = lax.dynamic_slice_in_dim(lengths_b, c * nb, nb, 0)
    meta = jnp.concatenate([jnp.stack([flip, me, lax.axis_index("rows")]).astype(jnp.int32), own_a, own_b])
    gain1, gain2 = gain_attn[None], gain_ffn[None]

    tile = th // 2
    per = 2
    row_grid = (2 * per,)
    by_row = lambda w: pl.BlockSpec((1, tile, w), lambda i, m: (i // per, i % per, 0))
    dense = 2 * tokens * width
    shape_a, shape_b = (na, la // 2, width), (nb, lb // 2, width)
    of_core = lambda shape: pl.BlockSpec(shape, lambda i, m: (m[1], 0, 0))
    of_other = lambda shape: pl.BlockSpec(shape, lambda i, m: (1 - m[1], 0, 0))
    cores = 2 if paired else 1
    all_a, all_b = (cores * na,) + shape_a[1:], (cores * nb,) + shape_b[1:]
    cut = na * la // 2

    def regroup(a, b):
        if paired:
            give = call(
                pick_kernel,
                (2,),
                [of_other(shape_a), of_other(shape_b)],
                pl.BlockSpec((tile, width), lambda i, m: (i, 0)),
                sds((th, width), BF),
                nbytes=4 * th * width,
                vmem=16,
            )(meta, a, b)
            return a, b, swap(give, "seq", 1)

        def one(x):
            got = lax.all_to_all(x, "seq", 0, 1, tiled=True)
            n, size, _ = got.shape
            return got.reshape(n, 2, size // 2, width).transpose(1, 0, 2, 3)

        whole_a, whole_b = one(a), one(b)
        rest = jnp.concatenate([whole_a[1].reshape(-1, width), whole_b[1].reshape(-1, width)], axis=0)
        return whole_a[0], whole_b[0], rest

    def ungroup(own_a, own_b, rest):
        def one(own, other, n, size):
            y = jnp.stack([own, other.reshape(own.shape)], axis=1).reshape(n, size, width)
            return lax.all_to_all(y, "seq", 1, 0, tiled=True)

        return one(own_a, rest[:cut], na, la), one(own_b, rest[cut:], nb, lb)

    received = pl.BlockSpec((tile, width), lambda i, m: (jnp.clip(i - per, 0, per - 1), 0))
    x_in = regroup(tokens_a, tokens_b)
    g_in3 = regroup(cotangent_a, cotangent_b)
    lane = jnp.arange(256, dtype=jnp.int32)
    back_rel = ((-96 - lane + 128 + 512) & 255) - 128
    hot = jnp.logical_and(
        bucket_of(back_rel, buckets)[:, None] == jnp.arange(128, dtype=jnp.int32)[None], back_rel[:, None] > -128
    ).astype(F32)

    at_once = 4
    rows_of_table = jnp.pad(
        relative_bias_table.T.reshape(head_count // at_once, at_once, buckets), ((0, 0), (0, 4), (0, 128 - buckets))
    )
    strip = call(
        functools.partial(strip_kernel, base=base, buckets=buckets),
        (head_count // at_once,),
        [pl.BlockSpec((1, 8, 128), lambda h, m: (h, 0, 0)), whole((256, 128))],
        pl.BlockSpec((at_once, strip_len, 128), lambda h, m: (h, 0, 0)),
        sds((head_count, strip_len, 128), F32),
        vmem=16,
        nbytes=4 * head_count * strip_len * 128,
    )(meta, rows_of_table, hot)

    tok = sds((2, th, width), BF)
    x, normed, q, k, v = call(
        qkv_kernel,
        row_grid,
        [of_core(shape_a), of_core(shape_b), received, whole((1, width))] + [whole((width, width))] * 3,
        [by_row(width)] * 5,
        [tok] * 5,
        vmem=30,
        free=(5, 6, 7),
        flops=3 * dense * width,
        nbytes=10 * tokens * width,
        after=[strip],
    )(meta, *x_in, gain1, w_query, w_key, w_value)

    by_pair = pl.BlockSpec((2, th, PAIR), lambda p, m: (0, 0, p))
    pa_shape, pb_shape = (head_count, na, la, la), (head_count, nb, lb, lb)
    score_macs = head_count * (na * la * la + nb * lb * lb)
    pa, pb, attn, linv = call(
        functools.partial(attn_kernel, dims=dims, base=base),
        (pairs,),
        [by_pair] * 3 + [pl.BlockSpec((2, strip_len, 128), lambda p, m: (p, 0, 0))],
        [
            pl.BlockSpec((2, na, la, la), lambda p, m: (p, 0, 0, 0)),
            pl.BlockSpec((2, nb, lb, lb), lambda p, m: (p, 0, 0, 0)),
            by_pair,
            by_pair,
        ],
        [sds(pa_shape, BF), sds(pb_shape, BF), tok, tok],
        scratch=[pltpu.VMEM((2, th, 128), BF)],
        vmem=34,
        flops=score_macs * 256 * 4,
        nbytes=2 * score_macs,
    )(meta, q, k, v, strip)

    all_tok = whole((2, th, width))
    fb = 512
    half_w, half_f, nf, mixes = width // 2, ff // 2, ff // fb, 2 * per

    def unit_at(i, m):
        return (jnp.maximum(i - mixes, 0) + (1 - m[1]) * (nf // 2)) % nf

    def mix_at(i):
        return jnp.minimum(i, mixes - 1)

    mix_rows = pl.BlockSpec((1, tile, width), lambda i, m: (mix_at(i) // per, mix_at(i) % per, 0))
    unit_rows = pl.BlockSpec((fb, half_w), lambda i, m: (unit_at(i, m), 0))
    hidden, g, low, back_send, back_keep, in_send, in_keep, d_normed2 = call(
        functools.partial(ffn_kernel, mixes=mixes, chunk=min(512, th)),
        (mixes + nf,),
        [
            mix_rows,
            mix_rows,
            whole((width, width)),
            whole((1, width)),
            of_core(shape_a),
            of_core(shape_b),
            received,
            pl.BlockSpec((width, fb), lambda i, m: (0, unit_at(i, m))),
            pl.BlockSpec((fb, width), lambda i, m: (unit_at(i, m), 0)),
        ],
        [
            mix_rows,
            mix_rows,
            pl.BlockSpec((2, th, fb), lambda i, m: (0, 0, unit_at(i, m))),
            unit_rows,
            unit_rows,
            pl.BlockSpec((width, fb), lambda i, m: (0, jnp.clip(i - mixes, 0, nf // 2 - 1))),
            pl.BlockSpec((width, fb), lambda i, m: (0, jnp.maximum(i - mixes - nf // 2, 0))),
            all_tok,
        ],
        [tok, tok, sds((2, th, ff), BF)]
        + [sds((ff, half_w), BF)] * 2
        + [sds((width, half_f), BF)] * 2
        + [tok],
        scratch=[
            pltpu.VMEM((2, th, width), BF),
            pltpu.VMEM((2, th, fb), BF),
            pltpu.VMEM((2, th, width), F32),
            pltpu.VMEM((2, th, width), BF),
        ],
        flops=dense * (5 * ff + width),
        nbytes=2 * tokens * ff,
        vmem=60,
        free=(3, 8, 9),
    )(meta, attn, x, w_out, gain2, *g_in3, w_in, w_back)

    bit_count = nrows.bit_length() - 1
    low_bits, high_bits = (0, 1), tuple(range(2, bit_count))
    every_bit = tuple(range(bit_count))

    def pair_sum(keep, send):
        return [blocks(keep, bit_count), blocks(swap(send, "seq", 1), bit_count)]

    hold = []
    if paired:
        back = Piece([pair_sum(back_keep, back_send)], every_bit)
        inner = Piece([pair_sum(in_keep, in_send)], every_bit)
        hold = [back_send, in_send]

    small = sds((8, width), F32)
    none = ([], [])
    d_hidden, d_attn, small_ffn, out_send, out_keep = call(
        hidden_kernel,
        row_grid,
        [
            by_row(width),
            by_row(width),
            by_row(width),
            whole((1, width)),
            whole((width, width)),
            by_row(width),
            by_row(width),
        ],
        [by_row(width), by_row(width), whole((8, width)), whole((width, half_w)), whole((width, half_w))],
        [tok, tok, small, sds((width, half_w), BF), sds((width, half_w), BF)],
        scratch=[pltpu.VMEM((width, width), F32)],
        free=(2, 6),
        vmem=44,
        flops=dense * (ff + 2 * width),
        nbytes=2 * tokens * ff,
        after=hold,
    )(meta, d_normed2, hidden, g, gain2, w_out, attn, linv)

    group_count = pairs // 2
    groups, dqs, tables, gains = [], [], [], []
    for gi in range(group_count):
        if paired:
            if gi == 0:
                out_sum = pair_sum(out_keep, out_send)
                _, _, hold = shuttle(meta, half_w, [(back, (0,)), (inner, (1,))], none, [d_attn])
                hold.append(out_send)
            elif gi == 1:
                first = [out_sum, pair_sum(*groups[0])]
                hold = [groups[0][1]]
            else:
                first = Piece(first, every_bit)
                _, _, hold = shuttle(
                    meta, half_w, [(back, (1,)), (inner, (0,)), (first, (2,))], none, [dqs[1][0]]
                )
                second = pair_sum(*groups[1])
                hold.append(groups[1][1])

        def pair_at(s, m, gi=gi):
            return jnp.where(s == 0, 1 - m[1], m[1]) * group_count + gi

        def half_at(s, m):
            return jnp.where(s == 0, 1 - m[1], m[1])

        by_cols = pl.BlockSpec((2, th, PAIR), lambda s, m, f=pair_at: (0, 0, f(s, m)))
        to_cols = pl.BlockSpec((2, th, PAIR), lambda s, m: (0, 0, half_at(s, m)))
        weight_cols = [
            pl.BlockSpec((width, PAIR), lambda s, m, f=pair_at, at=at: (0, f(at, m))) for at in (0, 0, 0, 1, 1, 1)
        ]
        dq, dk, dv, table, send, keep, gain = call(
            functools.partial(attn_back_kernel, dims=dims, base=base, buckets=buckets),
            (2,),
            [by_cols] * 5
            + [
                pl.BlockSpec((2, na, la, la), lambda s, m, f=pair_at: (f(s, m), 0, 0, 0)),
                pl.BlockSpec((2, nb, lb, lb), lambda s, m, f=pair_at: (f(s, m), 0, 0, 0)),
                all_tok,
            ]
            + weight_cols
            + [whole((256, 128))],
            [to_cols] * 3
            + [
                pl.BlockSpec((1, 8, 128), lambda s, m: (half_at(s, m), 0, 0)),
                whole((width, 3 * PAIR)),
                whole((width, 3 * PAIR)),
                whole((width, 128)),
            ],
            [sds((2, th, 2 * PAIR), BF)] * 3
            + [
                sds((2, 8, 128), F32),
                sds((width, 3 * PAIR), BF),
                sds((width, 3 * PAIR), BF),
                sds((width, 128), F32),
            ],
            scratch=[
                pltpu.VMEM((2, strip_len, 128), F32),
                pltpu.VMEM((2, la, la), BF),
                pltpu.VMEM((2, lb, lb), BF),
                pltpu.VMEM((2, tokens, 3 * PAIR), BF),
            ],
            vmem=44,
        flops=score_macs * 256 * 8 // 3 + dense * width,
            nbytes=2 * score_macs // 3,
            after=hold,
        )(meta, q, k, v, d_attn, attn, pa, pb, normed, *([w_query, w_key, w_value] * 2), hot)
        dqs.append((dq, dk, dv))
        tables.append(table)
        gains.append(gain)
        groups.append((keep, send))

    table_local = jnp.stack([t[:, :2, :buckets] for t in tables], axis=1).reshape(head_count, buckets).T
    gain_local = jnp.sum(sum(gains), axis=1) / gain_attn
    small_sum = jnp.concatenate([gain_local, jnp.sum(small_ffn, axis=0), table_local.reshape(-1)])
    small_sum = jnp.pad(small_sum, (0, 8 * half_w - small_sum.size)).reshape(8, half_w)
    if paired:
        last = Piece([second, pair_sum(*groups[2])], every_bit, carrier=True)
        smalls = [small_sum, swap(small_sum, "seq", 1)]
        _, _, hold = shuttle(meta, half_w, [(back, (2,)), (inner, (2,)), (first, (0,))], none, [dqs[2][0]])
        hold += [groups[2][1], small_sum]

    def token_grads(part):
        of_part = lambda w: pl.BlockSpec((1, tile, w), lambda i, m: (part, i, 0))
        own = [of_core(shape_a), of_core(shape_b)]
        return call(
            tokens_kernel,
            (per,),
            [of_part(2 * PAIR)] * 9
            + [whole((width, width))] * 3
            + [of_part(width), of_part(width), whole((1, width))],
            [pl.BlockSpec((tile, width), lambda i, m: (i, 0))] if part else own,
            [sds((th, width), BF)] if part else [sds(all_a, BF), sds(all_b, BF)],
            vmem=28,
            free=(10, 11, 12),
            flops=3 * dense * width // 2,
            nbytes=7 * tokens * width,
            after=hold,
        )(meta, *(d[i] for i in range(3) for d in dqs), w_query, w_key, w_value, x, d_hidden, gain1)

    (grads1,) = token_grads(1)
    if paired:
        _, small_state, hold = shuttle(
            meta,
            half_w,
            [(back, (3,)), (inner, (3,)), (first, (1,)), (last, low_bits)],
            none,
            [grads1],
            (smalls, ()),
        )
        hold.append(grads1)
    out_rows = lambda w: pl.BlockSpec((1, tile, w), lambda i, m: (1 - i // per, i % per, 0))
    outs1, out_a, out_b = call(
        out_kernel,
        row_grid,
        [out_rows(ff), whole((ff, width)), out_rows(width)],
        [pl.BlockSpec((tile, width), lambda i, m: (jnp.minimum(i, per - 1), 0)), of_core(shape_a), of_core(shape_b)],
        [sds((th, width), BF), sds(all_a, BF), sds(all_b, BF)],
        vmem=34,
        free=(2,),
        flops=dense * ff,
        nbytes=2 * tokens * ff,
        after=hold,
    )(meta, low, w_back, hidden)
    if paired:
        r = width // nrows
        in_back = [(0, 0, ff // nrows, 0, half_w)]
        in_in = [(1, r * j, r, 0, half_w) for j in range(half_f // half_w)]
        (g_back, g_in), small_state, hold = shuttle(
            meta,
            half_w,
            [(first, (3,)), (last, high_bits)],
            ([back, inner], [in_back, in_in]),
            [],
            small_state,
            [grads1, outs1],
        )
        grads1_got, outs1_got = (swap(y, "seq", 1) for y in hold[-2:])
    grad_a, grad_b = token_grads(0)

    if paired:
        def of(col):
            at = [(0, r), (1, 0), (1, r)]
            return [(piece, row, r, PAIR * col, PAIR) for piece, row in at]

        (g_out, g_q, g_k, g_v), ((small_all,), _), _ = shuttle(
            meta,
            half_w,
            [],
            ([first, last], [[(0, 0, r, 0, half_w)], of(0), of(1), of(2)]),
            [grad_a],
            small_state,
        )
        anywhere = pl.BlockSpec(memory_space=pl.ANY)
        out_a, out_b, grad_a, grad_b = call(
            place_kernel,
            (2,),
            [pl.BlockSpec((tile, width), lambda i, m: (i, 0))] * 2 + [anywhere] * 4,
            [of_other(shape_a), of_other(shape_b)] * 2,
            [sds(all_a, BF), sds(all_b, BF)] * 2,
            vmem=24,
            aliases={3: 0, 4: 1, 5: 2, 6: 3},
        )(meta, outs1_got, grads1_got, out_a, out_b, grad_a, grad_b)
    else:
        out_a, out_b = ungroup(out_a, out_b, outs1)
        grad_a, grad_b = ungroup(grad_a, grad_b, grads1)
        small_all = lax.psum(small_sum, ("rows", "seq"))

        def reduce(x):
            x = lax.psum_scatter(x.astype(F32), "rows", scatter_dimension=0, tiled=True)
            return lax.psum_scatter(x.astype(BF), "seq", scatter_dimension=1, tiled=True).astype(F32)

        def both(keep, send):
            return reduce(jnp.concatenate([keep, send], axis=1))

        g_back, g_in, g_out = both(back_keep, back_send), both(in_keep, in_send), both(out_keep, out_send)
        g_q, g_k, g_v = (
            reduce(
                jnp.concatenate([part[s][:, PAIR * i : PAIR * i + PAIR] for s in range(2) for part in groups], axis=1)
            )
            for i in range(3)
        )
    small_all = small_all.reshape(-1)
    gain_one, gain_two = small_all[:width], small_all[width : 2 * width]
    table_sum = small_all[2 * width : 2 * width + buckets * head_count].reshape(buckets, head_count)
    return (
        out_a, out_b, grad_a, grad_b, gain_one, g_q, g_k, g_v, g_out, table_sum, gain_two, g_in, g_back,
    )


def solution(mesh):
    split = P("rows", "seq", None)
    placed = (split, P("rows"), split, split, P("rows"), split) + (P(),) * 9
    shard = P("rows", "seq")
    return jax.shard_map(
        body,
        mesh=mesh,
        in_specs=placed,
        out_specs=(split, split, split, split, P(), shard, shard, shard, shard, P(), P(), shard, shard),
        check_vma=False,
    )
```

profile of v0, /device:TPU:0, one launch (start us, length us, event | category | flops | bytes accessed | tf_op | source)
XLA Modules:
  0.0 302.7 jit_solution(14501429945319316350)
XLA Ops:
  2.2 3.1 %shard_map.246 = bf16[1024,768]{1,0:T(8,128)(2,1)} custom-call(s32[9]{0:T(128)S(1)} %concatenate.6.meta, bf16[4,256,768]{2,1,0:T(8,128)(2,1)} %refs_0_.4, bf16[8,128,768]{2,1,0:T(8,128)(2,1)} %refs_1_.5), custom_call_target="tpu_custom_call" | custom-call | bytes 3145728 | tf_op jit(solution)/shard_map/pallas_call | solution.py:67
  5.9 3.1 %shard_map.250 = bf16[1024,768]{1,0:T(8,128)(2,1)} custom-call(s32[9]{0:T(128)S(1)} %concatenate.6.meta, bf16[4,256,768]{2,1,0:T(8,128)(2,1)} %refs_4_.4, bf16[8,128,768]{2,1,0:T(8,128)(2,1)} %refs_5_.3), custom_call_target="tpu_custom_call" | custom-call | bytes 3145728 | tf_op jit(solution)/shard_map/pallas_call | solution.py:67
  9.9 3.9 %shard_map.247.refs_7_.refs_3_ = f32[12,896,128]{2,1,0:T(8,128)} custom-call(s32[9]{0:T(128)S(1)} %concatenate.6.meta, f32[3,8,128]{2,1,0:T(8,128)S(1)} %pad.8.refs_0_, f32[256,128]{1,0:T(8,128)S(1)} %fusion.1.refs_1_.refs_14_), custom_call_target="tpu_custom_call" | custom-call | bytes 5505024 | tf_op jit(solution)/shard_map/pallas_call | solution.py:67
  15.0 12.7 %shard_map.248 = (bf16[2,1024,768]{2,1,0:T(8,128)(2,1)}, bf16[2,1024,768]{2,1,0:T(8,128)(2,1)}, bf16[2,1024,768]{2,1,0:T(8,128)(2,1)}, bf16[2,1024,768]{2,1,0:T(8,128)(2,1)}, bf16[2,1024,768]{2,1,0:T(8,128)(2,1)}) custom-call(s32[9]{0:T(128)S(1)} %concatenate.6.meta, bf16[4,256,768]{2,1,0:T(8,128)(2,1)} %refs_0_.4, bf16[8,128,768]{2,1,0:T(8,128)(2,1)} %refs_1_.5, ...), custom_call_target="tpu_custom_call" | custom-call | flops 7247757312 | bytes 15728640 | tf_op jit(solution)/shard_map/pallas_call | solution.py:67
  27.7 22.2 %shard_map.249 = (bf16[12,2,512,512]{3,2,1,0:T(8,128)(2,1)}, bf16[12,4,256,256]{3,2,1,0:T(8,128)(2,1)}, bf16[2,1024,768]{2,1,0:T(8,128)(2,1)}, bf16[2,1024,768]{2,1,0:T(8,128)(2,1)}) custom-call(s32[9]{0:T(128)S(1)} %concatenate.6.meta, bf16[2,1024,768]{2,1,0:T(8,128)(2,1)} %get-tuple-element.95.refs_0_, bf16[2,1024,768]{2,1,0:T(8,128)(2,1)} %get-tuple-element.96.refs_1_, ...), custom_call_target="tpu_custom_call" | custom-call | flops 9663676416 | bytes 18874368 | tf_op jit(solution)/shard_map/pallas_call | solution.py:67
  51.0 75.2 %shard_map.251 = (bf16[2,1024,768]{2,1,0:T(8,128)(2,1)}, bf16[2,1024,768]{2,1,0:T(8,128)(2,1)}, bf16[2,1024,3072]{2,1,0:T(8,128)(2,1)}, bf16[3072,384]{1,0:T(8,1...) custom-call(s32[9]{0:T(128)} %copy-done.22, ...), custom_call_target="tpu_custom_call" | custom-call | flops 50734301184 | bytes 12582912 | tf_op jit(solution)/shard_map/pallas_call | solution.py:67
  126.9 1.9 copy-done.29
  128.8 13.5 %shard_map.252 = (bf16[2,1024,768]{2,1,0:T(8,128)(2,1)}, bf16[2,1024,768]{2,1,0:T(8,128)(2,1)}, f32[8,768]{1,0:T(8,128)S(1)}, bf16[768,384]{1,0:T(8,128)(2,1)}, bf16[768,384]{1,0:T(8,128)(2,1)S(1)}) custom-call(s32[9]{0:T(128)S(1)} %copy-done.23, bf16[2,1024,768]{2,1,0:T(8,128)(2,1)} %get-tuple-element.104.refs_0_, bf16[2,1024,768]{2,1,0:T(8,128)(2,1)S(1)} %copy-done.29, ...), custom_call_target="tpu_custom_call" | custom-call | flops 14495514624 | bytes 12582912 | tf_op jit(solution)/shard_map/pallas_call | solution.py:67
  143.5 6.9 %shard_map.253 = (bf16[3072,384]{1,0:T(8,128)(2,1)}, bf16[1536,384]{1,0:T(8,128)(2,1)}, bf16[1536,384]{1,0:T(8,128)(2,1)}) custom-call(s32[9]{0:T(128)S(1)} %copy-done.23, bf16[2,2,2,2,192,384]{5,4,3,2,1,0:T(8,128)(2,1)} %bitcast.28, bf16[2,2,2,2,192,384]{5,4,3,2,1,0:T(8,128)(2,1)} %bitcast.4.refs_1_, bf16[2,2,2,2,48,1536]{5,4,3,2,1,0:T(8,128)(2,1)} %bitcast.29, ...), custom_call_target="tpu_custom_call" | custom-call | bytes 9437184 | tf_op jit(solution)/shard_map/pallas_call | solution.py:67
  150.4 2.6 collective-permute-start.4
  153.0 1.5 collective-permute-start.5
  154.6 20.8 %shard_map.254 = (bf16[2,1024,256]{2,1,0:T(8,128)(2,1)}, bf16[2,1024,256]{2,1,0:T(8,128)(2,1)}, bf16[2,1024,256]{2,1,0:T(8,128)(2,1)}, f32[2,8,128]{2,1,0:T(8,12...) custom-call(s32[9]{0:T(128)S(1)} %copy-done.23, ...), custom_call_target="tpu_custom_call" | custom-call | flops 8858370048 | bytes 6291456 | tf_op jit(solution)/shard_map/pallas_call | solution.py:67
  175.5 21.3 %shard_map.255 = (bf16[2,1024,256]{2,1,0:T(8,128)(2,1)}, bf16[2,1024,256]{2,1,0:T(8,128)(2,1)}, bf16[2,1024,256]{2,1,0:T(8,128)(2,1)}, f32[2,8,128]{2,1,0:T(8,12...) custom-call(s32[9]{0:T(128)S(1)} %copy-done.23, ...), custom_call_target="tpu_custom_call" | custom-call | flops 8858370048 | bytes 6291456 | tf_op jit(solution)/shard_map/pallas_call | solution.py:67
  198.8 4.8 %shard_map.256 = (bf16[2304,384]{1,0:T(8,128)(2,1)}, bf16[768,384]{1,0:T(8,128)(2,1)S(1)}, bf16[768,384]{1,0:T(8,128)(2,1)S(1)}, bf16[768,384]{1,0:T(8,128)(2,1)S(1)}) custom-call(s32[9]{0:T(128)S(1)} %copy-done.23, bf16[3072,384]{1,0:T(8,128)(2,1)} %get-tuple-element.109.refs_15_.refs_0_, bf16[1536,384]{1,0:T(8,128)(2,1)} %copy-done.30, ...), custom_call_target="tpu_custom_call" | custom-call | bytes 7077888 | tf_op jit(solution)/shard_map/pallas_call | solution.py:67
  203.6 1.6 collective-permute-start.10
  206.2 21.5 %shard_map.257 = (bf16[2,1024,256]{2,1,0:T(8,128)(2,1)}, bf16[2,1024,256]{2,1,0:T(8,128)(2,1)}, bf16[2,1024,256]{2,1,0:T(8,128)(2,1)}, f32[2,8,128]{2,1,0:T(8,12...) custom-call(s32[9]{0:T(128)S(1)} %copy-done.23, ...), custom_call_target="tpu_custom_call" | custom-call | flops 8858370048 | bytes 6291456 | tf_op jit(solution)/shard_map/pallas_call | solution.py:67
  227.9 3.4 %shard_map.258 = (bf16[1152,384]{1,0:T(8,128)(2,1)S(1)}, bf16[768,384]{1,0:T(8,128)(2,1)}, bf16[384,384]{1,0:T(8,128)(2,1)S(1)}) custom-call(s32[9]{0:T(128)S(1)} %copy-done.23, bf16[2304,384]{1,0:T(8,128)(2,1)} %get-tuple-element.120.refs_15_.refs_0_, bf16[768,384]{1,0:T(8,128)(2,1)S(1)} %collective-permute-done.8.refs_1_, ...), custom_call_target="tpu_custom_call" | custom-call | bytes 3538944 | tf_op jit(solution)/shard_map/pallas_call | solution.py:67
  236.4 1.3 select_maximum_fusion
  238.8 1.5 collective-permute-start.12
  243.1 8.4 %shard_map.259.refs_9_.refs_6_ = bf16[1024,768]{1,0:T(8,128)(2,1)} custom-call(s32[9]{0:T(128)S(1)} %copy-done.23, bf16[2,1024,256]{2,1,0:T(8,128)(2,1)} %get-tuple-element.139.refs_0_, bf16[2,1024,256]{2,1,0:T(8,128)(2,1)} %get-tuple-element.119.refs_7_.refs_1_, bf16[2,1024,256]{2,1,0:T(8,128)(2,1)} %get-tuple-element.125.refs_4_.refs_2_, ...), custom_call_target="tpu_custom_call" | custom-call | flops 3623878656 | bytes 11010048 | tf_op jit(solution)/shard_map/pallas_call | solution.py:67
  251.6 2.5 shard_map.260
  254.1 1.6 collective-permute-start.16
  256.2 1.4 collective-permute-start.18
  257.6 2.6 collective-permute-start.19
  260.2 2.3 copy-done.28
  262.5 15.4 %shard_map.261 = (bf16[1024,768]{1,0:T(8,128)(2,1)}, bf16[4,256,768]{2,1,0:T(8,128)(2,1)}, bf16[8,128,768]{2,1,0:T(8,128)(2,1)}) custom-call(s32[9]{0:T(128)S(1)} %copy-done.23, bf16[2,1024,3072]{2,1,0:T(8,128)(2,1)} %get-tuple-element.153.refs_0_, bf16[3072,768]{1,0:T(8,128)(2,1)S(1)} %copy-done.28, ...), custom_call_target="tpu_custom_call" | custom-call | flops 9663676416 | bytes 12582912 | tf_op jit(solution)/shard_map/pallas_call | solution.py:67
  278.0 1.5 shard_map.262
  280.4 1.2 collective-permute-start.23
  281.6 2.8 collective-permute-start.24
  286.4 8.7 %shard_map.263 = (bf16[4,256,768]{2,1,0:T(8,128)(2,1)}, bf16[8,128,768]{2,1,0:T(8,128)(2,1)}) custom-call(s32[9]{0:T(128)S(1)} %copy-done.23, bf16[2,1024,256]{2,1,0:T(8,128)(2,1)} %get-tuple-element.139.refs_0_, bf16[2,1024,256]{2,1,0:T(8,128)(2,1)} %get-tuple-element.119.refs_7_.refs_1_, bf16[2,1024,256]{2,1,0:T(8,128)(2,1)} %get-tuple-element.125.refs_4_.refs_2_, ...), custom_call_target="tpu_custom_call" | custom-call | flops 3623878656 | bytes 11010048 | tf_op jit(solution)/shard_map/pallas_call | solution.py:67
  295.1 1.3 shard_map.265
  298.4 4.2 %shard_map.264 = (bf16[4,256,768]{2,1,0:T(8,128)(2,1)}, bf16[8,128,768]{2,1,0:T(8,128)(2,1)}, bf16[4,256,768]{2,1,0:T(8,128)(2,1)}, bf16[8,128,768]{2,1,0:T(8,128)(2,1)}) custom-call(s32[9]{0:T(128)S(1)} %copy-done.23, bf16[1024,768]{1,0:T(8,128)(2,1)} %collective-permute-done.20.refs_0_, ...), custom_call_target="tpu_custom_call", output_to_operand_aliasing={{0}: (3, {}), {1}: (4, {}), {2}: (5, {}), {3}: (6, {})} | custom-call | tf_op jit(solution)/shard_map/pallas_call | solution.py:67
  (141 shorter events, 24.5 us)
Async XLA Ops:
  2.2 25.5 %copy-start.22 = (s32[9]{0:T(128)}, s32[9]{0:T(128)S(1)}, u32[]{:S(2)}) copy-start(s32[9]{0:T(128)S(1)} %concatenate.6.meta) | copy-start | bytes 112
  5.3 8.5 %collective-permute-start = (bf16[1024,768]{1,0:T(8,128)(2,1)}, bf16[1024,768]{1,0:T(8,128)(2,1)S(1)}, u32[]{:S(2)}, u32[]{:S(2)}) collective-permute-start(bf16[1024,768]{1,0:T(8,128)(2,1)} %shard_map.246), channel_id=1, source_target_pairs={{0,1},{1,0},{2,3},{3,2},{4,5},{5,4},{6,7},{7,6},{8,9},{9,8},{10,11... | collective-permute-start | bytes 4718600 | tf_op jit(solution)/shard_map/ppermute | solution.py:469
  9.0 40.9 %collective-permute-start.1 = (bf16[1024,768]{1,0:T(8,128)(2,1)}, bf16[1024,768]{1,0:T(8,128)(2,1)S(1)}, u32[]{:S(2)}, u32[]{:S(2)}) collective-permute-start(bf16[1024,768]{1,0:T(8,128)(2,1)} %shard_map.250), channel_id=1, source_target_pairs={{0,1},{1,0},{2,3},{3,2},{4,5},{5,4},{6,7},{7,6},{8,9},{9,8},{10,11... | collective-permute-start | bytes 4718600 | tf_op jit(solution)/shard_map/ppermute | solution.py:469
  51.0 75.8 %copy-start.6 = (bf16[2,1024,768]{2,1,0:T(8,128)(2,1)S(1)}, bf16[2,1024,768]{2,1,0:T(8,128)(2,1)}, u32[]{:S(2)}) copy-start(bf16[2,1024,768]{2,1,0:T(8,128)(2,1)} %get-tuple-element.98.refs_0_.refs_5_.refs_4_) | copy-start | bytes 9437188
  51.0 75.8 %copy-start.23 = (s32[9]{0:T(128)S(1)}, s32[9]{0:T(128)}, u32[]{:S(2)}) copy-start(s32[9]{0:T(128)} %copy-done.22) | copy-start | bytes 112
  51.0 75.8 %copy-start.27 = (f32[1,768]{1,0:T(1,128)S(1)}, f32[1,768]{1,0:T(1,128)}, u32[]{:S(2)}) copy-start(f32[1,768]{1,0:T(1,128)} %broadcast_in_dim.14.refs_3_) | copy-start | bytes 9220
  126.3 17.2 %collective-permute-start.2 = (bf16[3072,384]{1,0:T(8,128)(2,1)}, bf16[3072,384]{1,0:T(8,128)(2,1)}, u32[]{:S(2)}, u32[]{:S(2)}) collective-permute-start(bf16[3072,384]{1,0:T(8,128)(2,1)} %get-tuple-element.101.refs_7_), channel_id=1, source_target_pairs={{0,1},{1,0},{2,3},{3,2},{4,5},{5,4},{6,7},{7,6},{8,9},{9,8},{10,11... | collective-permute-start | bytes 7077896 | tf_op jit(solution)/shard_map/ppermute | solution.py:469
  126.8 16.7 %collective-permute-start.3 = (bf16[768,1536]{1,0:T(8,128)(2,1)}, bf16[768,1536]{1,0:T(8,128)(2,1)}, u32[]{:S(2)}, u32[]{:S(2)}) collective-permute-start(bf16[768,1536]{1,0:T(8,128)(2,1)} %get-tuple-element.103.refs_8_), channel_id=1, source_target_pairs={{0,1},{1,0},{2,3},{3,2},{4,5},{5,4},{6,7},{7,6},{8,9},{9,8},{10,11... | collective-permute-start | bytes 7077896 | tf_op jit(solution)/shard_map/ppermute | solution.py:469
  143.0 54.4 %collective-permute-start.6 = (bf16[768,384]{1,0:T(8,128)(2,1)}, bf16[768,384]{1,0:T(8,128)(2,1)S(1)}, u32[]{:S(2)}, u32[]{:S(2)}) collective-permute-start(bf16[768,384]{1,0:T(8,128)(2,1)} %get-tuple-element.113.refs_18_), channel_id=1, source_target_pairs={{0,1},{1,0},{2,3},{3,2},{4,5},{5,4},{6,7},{7,6},{8,9},{9,8},{10,11... | collective-permute-start | bytes 1769480 | tf_op jit(solution)/shard_map/ppermute | solution.py:469
  150.4 47.0 %collective-permute-start.4 = (bf16[1536,384]{1,0:T(8,128)(2,1)}, bf16[1536,384]{1,0:T(8,128)(2,1)S(1)}, u32[]{:S(2)}, u32[]{:S(2)}) collective-permute-start(bf16[1536,384]{1,0:T(8,128)(2,1)} %get-tuple-element.110.refs_16_), channel_id=1, source_target_pairs={{0,2},{2,0},{4,6},{6,4},{8,10},{10,8},{12,14},{14,12},{16,18},{18,... | collective-permute-start | bytes 3538952 | tf_op jit(solution)/shard_map/ppermute | solution.py:469
  153.0 44.4 %collective-permute-start.5 = (bf16[1536,384]{1,0:T(8,128)(2,1)}, bf16[1536,384]{1,0:T(8,128)(2,1)S(1)}, u32[]{:S(2)}, u32[]{:S(2)}) collective-permute-start(bf16[1536,384]{1,0:T(8,128)(2,1)} %get-tuple-element.111.refs_17_), channel_id=1, source_target_pairs={{0,4},{2,6},{4,0},{6,2},{8,12},{10,14},{12,8},{14,10},{16,20},{18,... | collective-permute-start | bytes 3538952 | tf_op jit(solution)/shard_map/ppermute | solution.py:469
  175.4 23.4 %copy-start.17 = (bf16[768,384]{1,0:T(8,128)(2,1)S(1)}, bf16[768,384]{1,0:T(8,128)(2,1)}, u32[]{:S(2)}) copy-start(bf16[768,384]{1,0:T(8,128)(2,1)} %copy-done.16) | copy-start | bytes 1769476
  175.4 22.0 %collective-permute-start.7 = (bf16[768,384]{1,0:T(8,128)(2,1)S(1)}, bf16[768,384]{1,0:T(8,128)(2,1)S(1)}, u32[]{:S(2)}, u32[]{:S(2)}) collective-permute-start(bf16[768,384]{1,0:T(8,128)(2,1)S(1)} %get-tuple-element.118.refs_15_), channel_id=1, source_target_pairs={{0,1},{1,0},{2,3},{3,2},{4,5},{5,4},{6,7},{7,6},{8,9},{9,8},{10,11... | collective-permute-start | bytes 1769480 | tf_op jit(solution)/shard_map/ppermute | solution.py:469
  196.8 54.7 %collective-permute-start.13 = (bf16[768,384]{1,0:T(8,128)(2,1)}, bf16[768,384]{1,0:T(8,128)(2,1)}, u32[]{:S(2)}, u32[]{:S(2)}) collective-permute-start(bf16[768,384]{1,0:T(8,128)(2,1)} %get-tuple-element.124.refs_19_), channel_id=1, source_target_pairs={{0,1},{1,0},{2,3},{3,2},{4,5},{5,4},{6,7},{7,6},{8,9},{9,8},{10,11... | collective-permute-start | bytes 1769480 | tf_op jit(solution)/shard_map/ppermute | solution.py:469
  203.6 24.2 %collective-permute-start.10 = (bf16[768,384]{1,0:T(8,128)(2,1)S(1)}, bf16[768,384]{1,0:T(8,128)(2,1)S(1)}, u32[]{:S(2)}, u32[]{:S(2)}) collective-permute-start(bf16[768,384]{1,0:T(8,128)(2,1)S(1)} %get-tuple-element.123.refs_18_), channel_id=1, source_target_pairs={{0,8},{2,10},{4,12},{6,14},{8,0},{10,2},{12,4},{14,6},{16,24},{18,... | collective-permute-start | bytes 1769480 | tf_op jit(solution)/shard_map/ppermute | solution.py:469
  205.2 22.7 %collective-permute-start.8 = (bf16[768,384]{1,0:T(8,128)(2,1)S(1)}, bf16[768,384]{1,0:T(8,128)(2,1)S(1)}, u32[]{:S(2)}, u32[]{:S(2)}) collective-permute-start(bf16[768,384]{1,0:T(8,128)(2,1)S(1)} %get-tuple-element.121.refs_16_), channel_id=1, source_target_pairs={{0,4},{2,6},{4,0},{6,2},{8,12},{10,14},{12,8},{14,10},{16,20},{18,... | collective-permute-start | bytes 1769480 | tf_op jit(solution)/shard_map/ppermute | solution.py:469
  205.7 22.2 %collective-permute-start.9 = (bf16[768,384]{1,0:T(8,128)(2,1)S(1)}, bf16[768,384]{1,0:T(8,128)(2,1)S(1)}, u32[]{:S(2)}, u32[]{:S(2)}) collective-permute-start(bf16[768,384]{1,0:T(8,128)(2,1)S(1)} %get-tuple-element.122.refs_17_), channel_id=1, source_target_pairs={{0,2},{2,0},{4,6},{6,4},{8,10},{10,8},{12,14},{14,12},{16,18},{18,... | collective-permute-start | bytes 1769480 | tf_op jit(solution)/shard_map/ppermute | solution.py:469
  227.8 23.7 %collective-permute-start.14 = (bf16[768,384]{1,0:T(8,128)(2,1)}, bf16[768,384]{1,0:T(8,128)(2,1)}, u32[]{:S(2)}, u32[]{:S(2)}) collective-permute-start(bf16[768,384]{1,0:T(8,128)(2,1)} %get-tuple-element.131.refs_18_), channel_id=1, source_target_pairs={{0,1},{1,0},{2,3},{3,2},{4,5},{5,4},{6,7},{7,6},{8,9},{9,8},{10,11... | collective-permute-start | bytes 1769480 | tf_op jit(solution)/shard_map/ppermute | solution.py:469
  227.9 12.4 %copy-start.3 = (bf16[768,768]{1,0:T(8,128)(2,1)S(1)}, bf16[768,768]{1,0:T(8,128)(2,1)}, u32[]{:S(2)}) copy-start(bf16[768,768]{1,0:T(8,128)(2,1)} %refs_10_.9) | copy-start | bytes 3538948
  227.9 12.4 %copy-start.5 = (bf16[768,768]{1,0:T(8,128)(2,1)S(1)}, bf16[768,768]{1,0:T(8,128)(2,1)}, u32[]{:S(2)}) copy-start(bf16[768,768]{1,0:T(8,128)(2,1)} %refs_11_.9) | copy-start | bytes 3538948
  232.3 19.3 %collective-permute-start.11 = (bf16[768,384]{1,0:T(8,128)(2,1)}, bf16[768,384]{1,0:T(8,128)(2,1)}, u32[]{:S(2)}, u32[]{:S(2)}) collective-permute-start(bf16[768,384]{1,0:T(8,128)(2,1)} %get-tuple-element.127.refs_16_), channel_id=1, source_target_pairs={{0,8},{2,10},{4,12},{6,14},{8,0},{10,2},{12,4},{14,6},{16,24},{18,... | collective-permute-start | bytes 1769480 | tf_op jit(solution)/shard_map/ppermute | solution.py:469
  238.4 13.1 %collective-permute-start.15 = (f32[8,384]{1,0:T(8,128)S(1)}, f32[8,384]{1,0:T(8,128)S(1)}, u32[]{:S(2)}, u32[]{:S(2)}) collective-permute-start(f32[8,384]{1,0:T(8,128)S(1)} %reshape.134.refs_19_.refs_7_), channel_id=1, source_target_pairs={{0,1},{1,0},{2,3},{3,2},{4,5},{5,4},{6,7},{7,6},{8,9},{9,8},{10,11... | collective-permute-start | bytes 36872 | tf_op jit(solution)/shard_map/ppermute | solution.py:469
  238.8 12.7 %collective-permute-start.12 = (bf16[384,384]{1,0:T(8,128)(2,1)}, bf16[384,384]{1,0:T(8,128)(2,1)S(1)}, u32[]{:S(2)}, u32[]{:S(2)}) collective-permute-start(bf16[384,384]{1,0:T(8,128)(2,1)} %copy-done.20), channel_id=1, source_target_pairs={{0,2},{2,0},{4,6},{6,4},{8,10},{10,8},{12,14},{14,12},{16,18},{18,... | collective-permute-start | bytes 884744 | tf_op jit(solution)/shard_map/ppermute | solution.py:469
  254.1 23.9 %collective-permute-start.16 = (bf16[592,384]{1,0:T(8,128)(2,1)S(1)}, bf16[592,384]{1,0:T(8,128)(2,1)S(1)}, u32[]{:S(2)}, u32[]{:S(2)}) collective-permute-start(bf16[592,384]{1,0:T(8,128)(2,1)S(1)} %get-tuple-element.148.refs_5_), channel_id=1, source_target_pairs={{0,4},{2,6},{4,0},{6,2},{8,12},{10,14},{12,8},{14,10},{16,20},{18,... | collective-permute-start | bytes 1363976 | tf_op jit(solution)/shard_map/ppermute | solution.py:469
  255.6 22.3 %collective-permute-start.17 = (bf16[400,384]{1,0:T(8,128)(2,1)S(1)}, bf16[400,384]{1,0:T(8,128)(2,1)S(1)}, u32[]{:S(2)}, u32[]{:S(2)}) collective-permute-start(bf16[400,384]{1,0:T(8,128)(2,1)S(1)} %get-tuple-element.149.refs_6_), channel_id=1, source_target_pairs={{0,2},{2,0},{4,6},{6,4},{8,10},{10,8},{12,14},{14,12},{16,18},{18,... | collective-permute-start | bytes 921608 | tf_op jit(solution)/shard_map/ppermute | solution.py:469
  256.2 21.8 %collective-permute-start.18 = (bf16[400,384]{1,0:T(8,128)(2,1)S(1)}, bf16[400,384]{1,0:T(8,128)(2,1)S(1)}, u32[]{:S(2)}, u32[]{:S(2)}) collective-permute-start(bf16[400,384]{1,0:T(8,128)(2,1)S(1)} %get-tuple-element.150.refs_7_), channel_id=1, source_target_pairs={{0,6},{2,4},{4,2},{6,0},{8,14},{10,12},{12,10},{14,8},{16,22},{18,... | collective-permute-start | bytes 921608 | tf_op jit(solution)/shard_map/ppermute | solution.py:469
  257.6 20.3 %collective-permute-start.19 = (bf16[384,384]{1,0:T(8,128)(2,1)S(1)}, bf16[384,384]{1,0:T(8,128)(2,1)S(1)}, u32[]{:S(2)}, u32[]{:S(2)}) collective-permute-start(bf16[384,384]{1,0:T(8,128)(2,1)S(1)} %get-tuple-element.151.refs_4_), channel_id=1, source_target_pairs={{0,16},{2,18},{4,20},{6,22},{8,24},{10,26},{12,28},{14,30},{16,0},... | collective-permute-start | bytes 884744 | tf_op jit(solution)/shard_map/ppermute | solution.py:469
  279.5 18.8 %collective-permute-start.20 = (bf16[1024,768]{1,0:T(8,128)(2,1)}, bf16[1024,768]{1,0:T(8,128)(2,1)}, u32[]{:S(2)}, u32[]{:S(2)}) collective-permute-start(bf16[1024,768]{1,0:T(8,128)(2,1)} %get-tuple-element.155.refs_23_), channel_id=1, source_target_pairs={{0,1},{1,0},{2,3},{3,2},{4,5},{5,4},{6,7},{7,6},{8,9},{9,8},{10,11... | collective-permute-start | bytes 4718600 | tf_op jit(solution)/shard_map/ppermute | solution.py:469
  279.6 18.8 %collective-permute-start.21 = (bf16[1024,768]{1,0:T(8,128)(2,1)}, bf16[1024,768]{1,0:T(8,128)(2,1)}, u32[]{:S(2)}, u32[]{:S(2)}) collective-permute-start(bf16[1024,768]{1,0:T(8,128)(2,1)} %get-tuple-element.156.refs_22_), channel_id=1, source_target_pairs={{0,1},{1,0},{2,3},{3,2},{4,5},{5,4},{6,7},{7,6},{8,9},{9,8},{10,11... | collective-permute-start | bytes 4718600 | tf_op jit(solution)/shard_map/ppermute | solution.py:469
  280.1 15.0 %collective-permute-start.22 = (bf16[208,384]{1,0:T(8,128)(2,1)S(1)}, bf16[208,384]{1,0:T(8,128)(2,1)S(1)}, u32[]{:S(2)}, u32[]{:S(2)}) collective-permute-start(bf16[208,384]{1,0:T(8,128)(2,1)S(1)} %get-tuple-element.160.refs_16_), channel_id=1, source_target_pairs={{0,16},{2,18},{4,20},{6,22},{8,24},{10,26},{12,28},{14,30},{16,0},... | collective-permute-start | bytes 479240 | tf_op jit(solution)/shard_map/ppermute | solution.py:469
  280.4 14.7 %collective-permute-start.23 = (bf16[112,384]{1,0:T(8,128)(2,1)S(1)}, bf16[112,384]{1,0:T(8,128)(2,1)S(1)}, u32[]{:S(2)}, u32[]{:S(2)}) collective-permute-start(bf16[112,384]{1,0:T(8,128)(2,1)S(1)} %get-tuple-element.161.refs_17_), channel_id=1, source_target_pairs={{0,8},{2,10},{4,12},{6,14},{8,0},{10,2},{12,4},{14,6},{16,24},{18,... | collective-permute-start | bytes 258056 | tf_op jit(solution)/shard_map/ppermute | solution.py:469
  281.6 13.4 %collective-permute-start.24 = (bf16[112,384]{1,0:T(8,128)(2,1)S(1)}, bf16[112,384]{1,0:T(8,128)(2,1)S(1)}, u32[]{:S(2)}, u32[]{:S(2)}) collective-permute-start(bf16[112,384]{1,0:T(8,128)(2,1)S(1)} %get-tuple-element.162.refs_18_), channel_id=1, source_target_pairs={{0,24},{2,26},{4,28},{6,30},{8,16},{10,18},{12,20},{14,22},{16,8},... | collective-permute-start | bytes 258056 | tf_op jit(solution)/shard_map/ppermute | solution.py:469
  (30 other events, 112.8 us)
where the time goes:
time: 308 us; the launch traced here: 303 us
  Pallas kernels  255 us (83%)
  local copies, waits for them, and re-layouts  22.6 us (7%)
  starting transfers between devices  22 us (7%)
    pallas_call x20, Pallas kernels, call(): made(*(place(i, x) for i, x in enumerate((*args, *after))))  255 us
    ppermute x25, starting transfers between devices, swap(): return lax.ppermute(x, axis, [(i, i ^ bit) for i in range(n)])  22 us
    unnamed x75, local copies, waits for them, and re-layouts  15.6 us
  transfers between devices with their start and end apart: 25, of which 0 were waited for; matrix products, arithmetic and copies ran while one was open for 3% of the time, Pallas kernels for 55%

commit v1 on v0

--- a/solution.py
+++ b/solution.py
@@ -97,26 +97,52 @@
         strip[h, near1:, :] = jnp.broadcast_to(plus, (strip.shape[1] - near1, 128))
 
 
-def pick_kernel(meta, a, b, out):
-    @pl.when(pl.program_id(0) == 0)
-    def _():
-        out[...] = flat(a)
-
-    @pl.when(pl.program_id(0) == 1)
-    def _():
-        out[...] = flat(b)
-
-
-def place_kernel(meta, out_got, grad_got, a0, b0, a1, b1, out_a, out_b, grad_a, grad_b):
-    @pl.when(pl.program_id(0) == 0)
-    def _():
-        out_a[...] = out_got[...].reshape(out_a.shape)
-        grad_a[...] = grad_got[...].reshape(grad_a.shape)
-
-    @pl.when(pl.program_id(0) == 1)
-    def _():
-        out_b[...] = out_got[...].reshape(out_b.shape)
-        grad_b[...] = grad_got[...].reshape(grad_b.shape)
+def moved(copies, held, arrive, leave):
+    first = [pltpu.make_async_copy(src, held.at[at], arrive.at[i]) for i, (src, at, _) in enumerate(copies)]
+    then = [pltpu.make_async_copy(held.at[at], dst, leave.at[i]) for i, (_, at, dst) in enumerate(copies)]
+    for one in first:
+        one.start()
+    for one, two in zip(first, then):
+        one.wait()
+        two.start()
+    for two in then:
+        two.wait()
+
+
+def flat_rows(dims):
+    na, la, nb, lb = dims
+    first = [(0, s, pl.ds(s * la // 2, la // 2)) for s in range(na)]
+    return first + [(1, s, pl.ds(na * la // 2 + s * lb // 2, lb // 2)) for s in range(nb)]
+
+
+def pick_kernel(meta, ta, tb, ca, cb, out_x, out_g, held, arrive, leave, *, dims):
+    first = [(1 - meta[1]) * n for n in (dims[0], dims[2])]
+    moved(
+        [
+            (pair[kind].at[first[kind] + s], (i, rows), out.at[rows])
+            for i, (pair, out) in enumerate((((ta, tb), out_x), ((ca, cb), out_g)))
+            for kind, s, rows in flat_rows(dims)
+        ],
+        held,
+        arrive,
+        leave,
+    )
+
+
+def place_kernel(
+    meta, out_got, grad_got, a0, b0, a1, b1, out_a, out_b, grad_a, grad_b, held, arrive, leave, *, dims
+):
+    first = [(1 - meta[1]) * n for n in (dims[0], dims[2])]
+    moved(
+        [
+            (got.at[rows], (i, rows), pair[kind].at[first[kind] + s])
+            for i, (got, pair) in enumerate(((out_got, (out_a, out_b)), (grad_got, (grad_a, grad_b))))
+            for kind, s, rows in flat_rows(dims)
+        ],
+        held,
+        arrive,
+        leave,
+    )
 
 
 def gathered(i, a, b, rest, out):
@@ -171,7 +197,7 @@
     return jnp.where(lanes_of((1, PAIR), high), 1.0, 0.0).astype(BF)
 
 
-def attn_kernel(meta, q, k, v, strip, pa, pb, attn, linv, kaug, *, dims, base):
+def attn_kernel(meta, q, k, v, strip, pa, pb, attn, linv, kaug, *, dims, base, seqs_a):
     na, la, nb, lb = dims
     flip = meta[0]
 
@@ -182,7 +208,7 @@
             for kh in range(2):
                 row = lax.broadcasted_iota(jnp.int32, (half, 128), 0)
                 start = jnp.where(flip == 0, half * kh, half * (1 - kh))
-                length = meta[3 + (s if kind == 0 else na + s)]
+                length = meta[4 + (meta[3] * na if kind == 0 else seqs_a + meta[3] * nb) + s]
                 lane = lax.broadcasted_iota(jnp.int32, (half, 128), 1)
                 gone = jnp.logical_and(row + start >= length, lane == 0)
                 kaug[kh, off : off + half, :] = jnp.where(gone, MASKED, 0.0).astype(BF)
@@ -300,7 +326,7 @@
     return jnp.sum(value.reshape(value.shape[0] // 8, 8, value.shape[1]), axis=0)
 
 
-def hidden_kernel(meta, d_normed, hidden, g, gain, w_out, attn, linv, d_hidden, d_attn, small, send, keep, acc):
+def hidden_kernel(meta, d_normed, hidden, g, gain, w_out, attn, linv, d_hidden, d_attn, small, send, keep, acc, gains):
     i, last = pl.program_id(0), pl.num_programs(0) - 1
     dn = d_normed[0].astype(F32)
     h = hidden[0].astype(F32)
@@ -315,17 +341,22 @@
 
     @pl.when(i == 0)
     def _():
-        small[...] = part
+        gains[...] = part
         acc[...] = product
 
     @pl.when(i > 0)
     def _():
-        small[...] += part
+        gains[...] += part
         acc[...] += product
 
     @pl.when(i == last)
     def _():
         split_columns(meta, acc[...], send, keep)
+        line = jnp.sum(gains[...], axis=0, keepdims=True)
+        half = small.shape[1]
+        small[...] = jnp.zeros_like(small)
+        small[2:3, :] = line[:, :half]
+        small[3:4, :] = line[:, half:]
 
 
 def table_sums(strip, hot, base, buckets):
@@ -361,9 +392,10 @@
 
 
 def attn_back_kernel(
-    meta, q, k, v, do, at_ref, pa, pb, normed, wqs, wks, wvs, wqk, wkk, wvk, hot,
-    dq, dk, dv, table, send, keep, gain, strip, dsa, dsb, cat, *, dims, base, buckets
+    meta, q, k, v, do, at_ref, pa, pb, normed, wqs, wks, wvs, wqk, wkk, wvk, hot, gain_attn, small_in, *rest, dims, base, buckets, pair_at, place
 ):
+    before = [] if place[0] else [rest[0]]
+    dq, dk, dv, send, keep, small, gain, strip, dsa, dsb, cat = rest[len(before) :]
     flip = meta[0]
     step = pl.program_id(0)
     th = normed.shape[1]
@@ -410,7 +442,13 @@
             cat[step, at, 0:128] = d_q[got]
             cat[step, at, 128:256] = d_k[got]
             cat[step, at, 256:384] = d_v[got]
-    table[0] = table_sums(strip, hot, base, buckets)
+    @pl.when(step == 0)
+    def _():
+        small[...] = small_in[...]
+
+    sums = table_sums(strip, hot, base, buckets)
+    row = lax.broadcasted_iota(jnp.int32, (small.shape[0], 128), 0) - (4 + 2 * pair_at(step, meta))
+    small[:, 0:128] += jnp.where(row == 0, sums[0:1], jnp.where(row == 1, sums[1:2], 0.0))
 
     @pl.when(step == 1)
     def _():
@@ -418,9 +456,20 @@
         value = dot(flat(normed), both, 0, 0)
         send[...] = value[:, :384].astype(BF)
         keep[...] = value[:, 384:].astype(BF)
-        gain[...] = sum(
+        part = sum(
             value[:, 128 * i : 128 * i + 128] * w[...].astype(F32) for i, w in enumerate((wqs, wks, wvs, wqk, wkk, wvk))
         )
+        for ref in before:
+            part = part + ref[...]
+        gain[...] = part
+        if place[1]:
+            line = lax.dot_general(
+                jnp.ones((8, 128), F32), part, (((1,), (1,)), ((), ())), precision=lax.Precision.HIGHEST,
+                preferred_element_type=F32,
+            )[:1] / gain_attn[...]
+            half = small.shape[1]
+            small[0:1, :] += line[:, :half]
+            small[1:2, :] += line[:, half:]
 
 
 def spread(i, value, first, second):
@@ -469,7 +518,7 @@
     return lax.ppermute(x, axis, [(i, i ^ bit) for i in range(n)])
 
 
-TAIL = 16
+TAIL = 32
 
 
 class Piece:
@@ -504,7 +553,10 @@
 
     every = [piece for piece, _ in work] + pieces
     slots = []
+    received = set()
     for piece in every:
+        for terms in piece.parts:
+            received |= {1 + slot(t[0] if piece.flat else t) for t in terms[1:]}
         slots.append([[(slot(t[0]), t[1]) if piece.flat else (slot(t), 0) for t in terms] for terms in piece.parts])
     small_at, tail_at = [slot(x) for x in small[0]], [slot(x) for x in small[1]]
     messages = {}
@@ -577,6 +629,7 @@
         outs + [sds(x.shape, x.dtype) for x in through],
         nbytes=sum(x.size * 2 for x in ins),
         vmem=30,
+        free=tuple(received),
         after=after,
         aliases={1 + len(ins) + i: len(outs) + i for i in range(len(through))},
     )(meta, *ins, *through)
@@ -595,7 +648,7 @@
         piece.parts, piece.flat = [terms], rows
         piece.left = tuple(b for b in piece.left if b not in bits)
     ends = len(messages) + len(results)
-    return made[len(messages) : ends], (made[ends:], tails), [*made, *passed]
+    return made[len(messages) : ends], (made[ends:], tails), [*made[: len(messages)], *passed]
 
 
 def body(
@@ -619,9 +672,9 @@
 
     me = c if paired else jnp.int32(0)
     flip = me
-    own_a = lax.dynamic_slice_in_dim(lengths_a, c * na, na, 0)
-    own_b = lax.dynamic_slice_in_dim(lengths_b, c * nb, nb, 0)
-    meta = jnp.concatenate([jnp.stack([flip, me, lax.axis_index("rows")]).astype(jnp.int32), own_a, own_b])
+    meta = jnp.concatenate(
+        [jnp.stack([flip, me, lax.axis_index("rows"), c]).astype(jnp.int32), lengths_a, lengths_b]
+    )
     gain1, gain2 = gain_attn[None], gain_ffn[None]
 
     tile = th // 2
@@ -637,18 +690,6 @@
     cut = na * la // 2
 
     def regroup(a, b):
-        if paired:
-            give = call(
-                pick_kernel,
-                (2,),
-                [of_other(shape_a), of_other(shape_b)],
-                pl.BlockSpec((tile, width), lambda i, m: (i, 0)),
-                sds((th, width), BF),
-                nbytes=4 * th * width,
-                vmem=16,
-            )(meta, a, b)
-            return a, b, swap(give, "seq", 1)
-
         def one(x):
             got = lax.all_to_all(x, "seq", 0, 1, tiled=True)
             n, size, _ = got.shape
@@ -666,8 +707,24 @@
         return one(own_a, rest[:cut], na, la), one(own_b, rest[cut:], nb, lb)
 
     received = pl.BlockSpec((tile, width), lambda i, m: (jnp.clip(i - per, 0, per - 1), 0))
-    x_in = regroup(tokens_a, tokens_b)
-    g_in3 = regroup(cotangent_a, cotangent_b)
+    anywhere = pl.BlockSpec(memory_space=pl.ANY)
+    copies = [pltpu.VMEM((2, th, width), BF)] + [pltpu.SemaphoreType.DMA((2 * (na + nb),))] * 2
+    if paired:
+        give = call(
+            functools.partial(pick_kernel, dims=dims),
+            (1,),
+            [anywhere] * 4,
+            [anywhere] * 2,
+            [sds((th, width), BF)] * 2,
+            scratch=copies,
+            nbytes=8 * th * width,
+            vmem=8,
+        )(meta, tokens_a, tokens_b, cotangent_a, cotangent_b)
+        x_in = (tokens_a, tokens_b, swap(give[0], "seq", 1))
+        g_in3 = (cotangent_a, cotangent_b, swap(give[1], "seq", 1))
+    else:
+        x_in = regroup(tokens_a, tokens_b)
+        g_in3 = regroup(cotangent_a, cotangent_b)
     lane = jnp.arange(256, dtype=jnp.int32)
     back_rel = ((-96 - lane + 128 + 512) & 255) - 128
     hot = jnp.logical_and(
@@ -706,7 +763,7 @@
     pa_shape, pb_shape = (head_count, na, la, la), (head_count, nb, lb, lb)
     score_macs = head_count * (na * la * la + nb * lb * lb)
     pa, pb, attn, linv = call(
-        functools.partial(attn_kernel, dims=dims, base=base),
+        functools.partial(attn_kernel, dims=dims, base=base, seqs_a=tokens_a.shape[0]),
         (pairs,),
         [by_pair] * 3 + [pl.BlockSpec((2, strip_len, 128), lambda p, m: (p, 0, 0))],
         [
@@ -787,9 +844,9 @@
         inner = Piece([pair_sum(in_keep, in_send)], every_bit)
         hold = [back_send, in_send]
 
-    small = sds((8, width), F32)
+    small = sds((16, half_w), F32)
     none = ([], [])
-    d_hidden, d_attn, small_ffn, out_send, out_keep = call(
+    d_hidden, d_attn, small_sum, out_send, out_keep = call(
         hidden_kernel,
         row_grid,
         [
@@ -801,10 +858,10 @@
             by_row(width),
             by_row(width),
         ],
-        [by_row(width), by_row(width), whole((8, width)), whole((width, half_w)), whole((width, half_w))],
+        [by_row(width), by_row(width), whole((16, half_w)), whole((width, half_w)), whole((width, half_w))],
         [tok, tok, small, sds((width, half_w), BF), sds((width, half_w), BF)],
-        scratch=[pltpu.VMEM((width, width), F32)],
-        free=(2, 6),
+        scratch=[pltpu.VMEM((width, width), F32), pltpu.VMEM((8, width), F32)],
+        free=(5,),
         vmem=44,
         flops=dense * (ff + 2 * width),
         nbytes=2 * tokens * ff,
@@ -812,7 +869,7 @@
     )(meta, d_normed2, hidden, g, gain2, w_out, attn, linv)
 
     group_count = pairs // 2
-    groups, dqs, tables, gains = [], [], [], []
+    groups, dqs, gains = [], [], []
     for gi in range(group_count):
         if paired:
             if gi == 0:
@@ -841,8 +898,11 @@
         weight_cols = [
             pl.BlockSpec((width, PAIR), lambda s, m, f=pair_at, at=at: (0, f(at, m))) for at in (0, 0, 0, 1, 1, 1)
         ]
-        dq, dk, dv, table, send, keep, gain = call(
-            functools.partial(attn_back_kernel, dims=dims, base=base, buckets=buckets),
+        dq, dk, dv, send, keep, small_sum, gain = call(
+            functools.partial(
+                attn_back_kernel, dims=dims, base=base, buckets=buckets, pair_at=pair_at,
+                place=(gi == 0, gi == group_count - 1),
+            ),
             (2,),
             [by_cols] * 5
             + [
@@ -851,19 +911,20 @@
                 all_tok,
             ]
             + weight_cols
-            + [whole((256, 128))],
+            + [whole((256, 128)), whole((1, width)), whole((16, half_w))]
+            + [whole((width, 128))] * len(gains),
             [to_cols] * 3
             + [
-                pl.BlockSpec((1, 8, 128), lambda s, m: (half_at(s, m), 0, 0)),
                 whole((width, 3 * PAIR)),
                 whole((width, 3 * PAIR)),
+                whole((16, half_w)),
                 whole((width, 128)),
             ],
             [sds((2, th, 2 * PAIR), BF)] * 3
             + [
-                sds((2, 8, 128), F32),
                 sds((width, 3 * PAIR), BF),
                 sds((width, 3 * PAIR), BF),
+                small,
                 sds((width, 128), F32),
             ],
             scratch=[
@@ -876,16 +937,11 @@
         flops=score_macs * 256 * 8 // 3 + dense * width,
             nbytes=2 * score_macs // 3,
             after=hold,
-        )(meta, q, k, v, d_attn, attn, pa, pb, normed, *([w_query, w_key, w_value] * 2), hot)
+        )(meta, q, k, v, d_attn, attn, pa, pb, normed, *([w_query, w_key, w_value] * 2), hot, gain1, small_sum, *gains)
         dqs.append((dq, dk, dv))
-        tables.append(table)
-        gains.append(gain)
+        gains = [gain]
         groups.append((keep, send))
 
-    table_local = jnp.stack([t[:, :2, :buckets] for t in tables], axis=1).reshape(head_count, buckets).T
-    gain_local = jnp.sum(sum(gains), axis=1) / gain_attn
-    small_sum = jnp.concatenate([gain_local, jnp.sum(small_ffn, axis=0), table_local.reshape(-1)])
-    small_sum = jnp.pad(small_sum, (0, 8 * half_w - small_sum.size)).reshape(8, half_w)
     if paired:
         last = Piece([second, pair_sum(*groups[2])], every_bit, carrier=True)
         smalls = [small_sum, swap(small_sum, "seq", 1)]
@@ -963,14 +1019,15 @@
             [grad_a],
             small_state,
         )
-        anywhere = pl.BlockSpec(memory_space=pl.ANY)
         out_a, out_b, grad_a, grad_b = call(
-            place_kernel,
-            (2,),
-            [pl.BlockSpec((tile, width), lambda i, m: (i, 0))] * 2 + [anywhere] * 4,
-            [of_other(shape_a), of_other(shape_b)] * 2,
+            functools.partial(place_kernel, dims=dims),
+            (1,),
+            [anywhere] * 6,
+            [anywhere] * 4,
             [sds(all_a, BF), sds(all_b, BF)] * 2,
-            vmem=24,
+            scratch=copies,
+            vmem=8,
+            free=(1, 2),
             aliases={3: 0, 4: 1, 5: 2, 6: 3},
         )(meta, outs1_got, grads1_got, out_a, out_b, grad_a, grad_b)
     else:
@@ -992,9 +1049,8 @@
             )
             for i in range(3)
         )
-    small_all = small_all.reshape(-1)
-    gain_one, gain_two = small_all[:width], small_all[width : 2 * width]
-    table_sum = small_all[2 * width : 2 * width + buckets * head_count].reshape(buckets, head_count)
+    gain_one, gain_two = small_all[0:2].reshape(width), small_all[2:4].reshape(width)
+    table_sum = small_all[4 : 4 + head_count, :buckets].T
     return (
         out_a, out_b, grad_a, grad_b, gain_one, g_q, g_k, g_v, g_out, table_sum, gain_two, g_in, g_back,
     )

time: 308 us -> 286 us (0.929)
  local copies, waits for them, and re-layouts: 22.6 us -> 3.24 us
  Pallas kernels: 255 us -> 249 us
  waiting for transfers between devices: 0.07 us -> 5.25 us
    unnamed x75 -> x30, local copies, waits for them, and re-layouts: 15.6 us -> 0.09 us
    pallas_call x20 -> x19, Pallas kernels: 255 us -> 249 us  [call(): made(*(place(i, x) for i, x in enumerate((*args, *after))))]
    ppermute x25, waiting for transfers between devices: 0.07 us -> 5.25 us  [swap(): return lax.ppermute(x, axis, [(i, i ^ bit) for i in range(n)])]
  transfers between devices with their start and end apart: 25 -> 25, of which waited for: 0 -> 1; matrix products, arithmetic and copies ran while one was open for 3% -> 1% of each run, Pallas kernels for 55% -> 58%
where the time goes in v1:
time: 286 us; the launch traced here: 281 us
  Pallas kernels  249 us (87%)
  starting transfers between devices  22.2 us (8%)
  waiting for transfers between devices  5.25 us (2%)
  local copies, waits for them, and re-layouts  3.24 us (1%)
    pallas_call x19, Pallas kernels, call(): made(*(place(i, x) for i, x in enumerate((*args, *after))))  249 us
    ppermute x25, starting transfers between devices, swap(): return lax.ppermute(x, axis, [(i, i ^ bit) for i in range(n)])  22.2 us
  transfers between devices with their start and end apart: 25, of which 1 were waited for; matrix products, arithmetic and copies ran while one was open for 1% of the time, Pallas kernels for 58%

profile of v1, /device:TPU:0, one launch (start us, length us, event | category | flops | bytes accessed | tf_op | source)
XLA Modules:
  0.0 280.9 jit_solution(14275452465359452153)
XLA Ops:
  0.6 0.8 concatenate.3.meta
  1.4 3.4 %shard_map.246 = (bf16[1024,768]{1,0:T(8,128)(2,1)}, bf16[1024,768]{1,0:T(8,128)(2,1)}) custom-call(s32[16]{0:T(128)S(1)} %concatenate.3.meta, bf16[4,256,768]{2,1,0:T(8,128)(2,1)} %refs_0_.3, bf16[8,128,768]{2,1,0:T(8,128)(2,1)} %refs_1_.4, bf16[4,256,768]{2,1,0:T(8,128)(2,1)} %refs_4_.4, bf16[8,128,768]{2,1,0:T(8,128)(2,1)} %refs_5_.3), custom_call_target="tpu_custom_call" | custom-call | bytes 6291456 | tf_op jit(solution)/shard_map/pallas_call | solution.py:67
  6.2 3.9 %shard_map.247.refs_7_.refs_3_ = f32[12,896,128]{2,1,0:T(8,128)} custom-call(s32[16]{0:T(128)S(1)} %concatenate.3.meta, f32[3,8,128]{2,1,0:T(8,128)S(1)} %pad.4.refs_0_, f32[256,128]{1,0:T(8,128)S(1)} %fusion.1.refs_1_.refs_14_), custom_call_target="tpu_custom_call" | custom-call | bytes 5505024 | tf_op jit(solution)/shard_map/pallas_call | solution.py:67
  10.1 12.5 %shard_map.248 = (bf16[2,1024,768]{2,1,0:T(8,128)(2,1)}, bf16[2,1024,768]{2,1,0:T(8,128)(2,1)}, bf16[2,1024,768]{2,1,0:T(8,128)(2,1)}, bf16[2,1024,768]{2,1,0:T(8,128)(2,1)}, bf16[2,1024,768]{2,1,0:T(8,128)(2,1)}) custom-call(s32[16]{0:T(128)S(1)} %concatenate.3.meta, bf16[4,256,768]{2,1,0:T(8,128)(2,1)} %refs_0_.3, bf16[8,128,768]{2,1,0:T(8,128)(2,1)} %refs_1_.4, ...), custom_call_target="tpu_custom_call" | custom-call | flops 7247757312 | bytes 15728640 | tf_op jit(solution)/shard_map/pallas_call | solution.py:67
  22.7 21.3 %shard_map.249 = (bf16[12,2,512,512]{3,2,1,0:T(8,128)(2,1)}, bf16[12,4,256,256]{3,2,1,0:T(8,128)(2,1)}, bf16[2,1024,768]{2,1,0:T(8,128)(2,1)}, bf16[2,1024,768]{2,1,0:T(8,128)(2,1)}) custom-call(s32[16]{0:T(128)S(1)} %concatenate.3.meta, bf16[2,1024,768]{2,1,0:T(8,128)(2,1)} %get-tuple-element.97.refs_0_, bf16[2,1024,768]{2,1,0:T(8,128)(2,1)} %get-tuple-element.98.refs_1_, ...), custom_call_target="tpu_custom_call" | custom-call | flops 9663676416 | bytes 18874368 | tf_op jit(solution)/shard_map/pallas_call | solution.py:67
  43.9 75.4 %shard_map.250 = (bf16[2,1024,768]{2,1,0:T(8,128)(2,1)}, bf16[2,1024,768]{2,1,0:T(8,128)(2,1)}, bf16[2,1024,3072]{2,1,0:T(8,128)(2,1)}, bf16[3072,384]{1,0:T(8,1...) custom-call(s32[16]{0:T(128)} %copy-done.6, ...), custom_call_target="tpu_custom_call" | custom-call | flops 50734301184 | bytes 12582912 | tf_op jit(solution)/shard_map/pallas_call | solution.py:67
  119.9 13.5 %shard_map.251 = (bf16[2,1024,768]{2,1,0:T(8,128)(2,1)}, bf16[2,1024,768]{2,1,0:T(8,128)(2,1)}, f32[16,384]{1,0:T(8,128)S(1)}, bf16[768,384]{1,0:T(8,128)(2,1)S(1)}, bf16[768,384]{1,0:T(8,128)(2,1)S(1)}) custom-call(s32[16]{0:T(128)S(1)} %copy-done.7, bf16[2,1024,768]{2,1,0:T(8,128)(2,1)} %get-tuple-element.107.refs_0_, ...), custom_call_target="tpu_custom_call" | custom-call | flops 14495514624 | bytes 12582912 | tf_op jit(solution)/shard_map/pallas_call | solution.py:67
  133.8 5.5 %shard_map.252 = (bf16[3072,384]{1,0:T(8,128)(2,1)}, bf16[1536,384]{1,0:T(8,128)(2,1)}, bf16[1536,384]{1,0:T(8,128)(2,1)}) custom-call(s32[16]{0:T(128)S(1)} %copy-done.7, bf16[2,2,2,2,192,384]{5,4,3,2,1,0:T(8,128)(2,1)S(1)} %bitcast.17, bf16[2,2,2,2,192,384]{5,4,3,2,1,0:T(8,128)(2,1)} %bitcast.29, bf16[2,2,2,2,48,1536]{5,4,3,2,1,0:T(8,128)(2,1)S(1)} %bitcast.18, ...), custom_call_target="tpu_custom_call" | custom-call | bytes 9437184 | tf_op jit(solution)/shard_map/pallas_call | solution.py:67
  139.3 2.7 collective-permute-start.4
  142.0 1.5 collective-permute-start.5
  143.5 21.1 %shard_map.253 = (bf16[2,1024,256]{2,1,0:T(8,128)(2,1)}, bf16[2,1024,256]{2,1,0:T(8,128)(2,1)}, bf16[2,1024,256]{2,1,0:T(8,128)(2,1)}, bf16[768,384]{1,0:T(8,128...) custom-call(s32[16]{0:T(128)S(1)} %copy-done.7, ...), custom_call_target="tpu_custom_call" | custom-call | flops 8858370048 | bytes 6291456 | tf_op jit(solution)/shard_map/pallas_call | solution.py:67
  164.8 21.4 %shard_map.254 = (bf16[2,1024,256]{2,1,0:T(8,128)(2,1)}, bf16[2,1024,256]{2,1,0:T(8,128)(2,1)}, bf16[2,1024,256]{2,1,0:T(8,128)(2,1)}, bf16[768,384]{1,0:T(8,128...) custom-call(s32[16]{0:T(128)S(1)} %copy-done.7, ...), custom_call_target="tpu_custom_call" | custom-call | flops 8858370048 | bytes 6291456 | tf_op jit(solution)/shard_map/pallas_call | solution.py:67
  186.7 4.4 %shard_map.255 = (bf16[2304,384]{1,0:T(8,128)(2,1)}, bf16[768,384]{1,0:T(8,128)(2,1)S(1)}, bf16[768,384]{1,0:T(8,128)(2,1)S(1)}, bf16[768,384]{1,0:T(8,128)(2,1)S(1)}) custom-call(s32[16]{0:T(128)S(1)} %copy-done.7, bf16[1536,384]{1,0:T(8,128)(2,1)S(1)} %collective-permute-done.4.refs_0_, bf16[3072,384]{1,0:T(8,128)(2,1)} %get-tuple-element.113.refs_17_.refs_1_, ...), custom_call_target="tpu_custom_call" | custom-call | bytes 7077888 | tf_op jit(solution)/shard_map/pallas_call | solution.py:67
  191.1 1.6 collective-permute-start.10
  193.7 22.5 %shard_map.256 = (bf16[2,1024,256]{2,1,0:T(8,128)(2,1)}, bf16[2,1024,256]{2,1,0:T(8,128)(2,1)}, bf16[2,1024,256]{2,1,0:T(8,128)(2,1)}, bf16[768,384]{1,0:T(8,128...) custom-call(s32[16]{0:T(128)S(1)} %copy-done.7, ...), custom_call_target="tpu_custom_call" | custom-call | flops 8858370048 | bytes 6291456 | tf_op jit(solution)/shard_map/pallas_call | solution.py:67
  216.4 2.7 shard_map.257
  219.7 1.6 collective-permute-start.12
  221.3 8.3 %shard_map.258.refs_9_.refs_8_.refs_6_ = bf16[1024,768]{1,0:T(8,128)(2,1)} custom-call(s32[16]{0:T(128)S(1)} %copy-done.7, bf16[2,1024,256]{2,1,0:T(8,128)(2,1)} %get-tuple-element.141.refs_0_, bf16[2,1024,256]{2,1,0:T(8,128)(2,1)} %get-tuple-element.125.refs_7_.refs_1_, bf16[2,1024,256]{2,1,0:T(8,128)(2,1)} %get-tuple-element.133.refs_4_.refs_2_, ...), custom_call_target="tpu_custom_call" | custom-call | flops 3623878656 | bytes 11010048 | tf_op jit(solution)/shard_map/pallas_call | solution.py:67
  229.7 5.2 %collective-permute-done.11.refs_0_ = bf16[768,384]{1,0:T(8,128)(2,1)S(1)} collective-permute-done((bf16[768,384]{1,0:T(8,128)(2,1)S(1)}, bf16[768,384]{1,0:T(8,128)(2,1)S(1)}, u32[]{:S(2)}, u32[]{:S(2)}) %collective-permute-start.11) | collective-permute-done | bytes 589856 | tf_op jit(solution)/shard_map/ppermute | solution.py:518
  234.9 1.1 shard_map.259
  236.0 1.6 collective-permute-start.16
  237.6 1.5 collective-permute-start.17
  239.5 2.6 collective-permute-start.19
  242.1 15.1 %shard_map.260 = (bf16[1024,768]{1,0:T(8,128)(2,1)}, bf16[4,256,768]{2,1,0:T(8,128)(2,1)}, bf16[8,128,768]{2,1,0:T(8,128)(2,1)}) custom-call(s32[16]{0:T(128)S(1)} %copy-done.7, bf16[2,1024,3072]{2,1,0:T(8,128)(2,1)} %get-tuple-element.155.refs_0_, bf16[3072,768]{1,0:T(8,128)(2,1)S(1)} %bitcast.28, bf16[2,1024,768]{2,1,0:T(8,128)(2,1)} %get-tuple-element.108.refs_1_.refs_2_, ...), custom_call_target="tpu_custom_call" | custom-call | flops 9663676416 | bytes 12582912 | tf_op jit(solution)/shard_map/pallas_call | solution.py:67
  257.3 1.5 shard_map.261
  260.3 3.5 %collective-permute-start.24 = (bf16[128,384]{1,0:T(8,128)(2,1)S(1)}, bf16[128,384]{1,0:T(8,128)(2,1)S(1)}, u32[]{:S(2)}, u32[]{:S(2)}) collective-permute-start(bf16[128,384]{1,0:T(8,128)(2,1)S(1)} %get-tuple-element.164.refs_18_), channel_id=1, source_target_pairs={{0,24},{2,26},{4,28},{6,30},{8,16},{10,18},{12,20},{14,22},{16,8},... | collective-permute-start | bytes 294920 | tf_op jit(solution)/shard_map/ppermute | solution.py:518
  263.7 8.7 %shard_map.262 = (bf16[4,256,768]{2,1,0:T(8,128)(2,1)}, bf16[8,128,768]{2,1,0:T(8,128)(2,1)}) custom-call(s32[16]{0:T(128)S(1)} %copy-done.7, bf16[2,1024,256]{2,1,0:T(8,128)(2,1)} %get-tuple-element.141.refs_0_, bf16[2,1024,256]{2,1,0:T(8,128)(2,1)} %get-tuple-element.125.refs_7_.refs_1_, bf16[2,1024,256]{2,1,0:T(8,128)(2,1)} %get-tuple-element.133.refs_4_.refs_2_, ...), custom_call_target="tpu_custom_call" | custom-call | flops 3623878656 | bytes 11010048 | tf_op jit(solution)/shard_map/pallas_call | solution.py:67
  272.4 1.3 shard_map.264
  273.7 0.6 reshape.121
  274.3 0.6 reshape.122
  274.9 0.6 slice_bitcast_fusion
  275.5 5.2 %shard_map.263 = (bf16[4,256,768]{2,1,0:T(8,128)(2,1)}, bf16[8,128,768]{2,1,0:T(8,128)(2,1)}, bf16[4,256,768]{2,1,0:T(8,128)(2,1)}, bf16[8,128,768]{2,1,0:T(8,128)(2,1)}) custom-call(s32[16]{0:T(128)S(1)} %copy-done.7, ...), custom_call_target="tpu_custom_call", output_to_operand_aliasing={{0}: (3, {}), {1}: (4, {}), {2}: (5, {}), {3}: (6, {})} | custom-call | tf_op jit(solution)/shard_map/pallas_call | solution.py:67
  (80 shorter events, 6.6 us)
Async XLA Ops:
  1.4 21.3 %copy-start.6 = (s32[16]{0:T(128)}, s32[16]{0:T(128)S(1)}, u32[]{:S(2)}) copy-start(s32[16]{0:T(128)S(1)} %concatenate.3.meta) | copy-start | bytes 196
  4.8 5.3 %collective-permute-start = (bf16[1024,768]{1,0:T(8,128)(2,1)}, bf16[1024,768]{1,0:T(8,128)(2,1)}, u32[]{:S(2)}, u32[]{:S(2)}) collective-permute-start(bf16[1024,768]{1,0:T(8,128)(2,1)} %get-tuple-element.96), channel_id=1, source_target_pairs={{0,1},{1,0},{2,3},{3,2},{4,5},{5,4},{6,7},{7,6},{8,9},{9,8},{10,11... | collective-permute-start | bytes 4718600 | tf_op jit(solution)/shard_map/ppermute | solution.py:518
  5.3 38.6 %collective-permute-start.1 = (bf16[1024,768]{1,0:T(8,128)(2,1)}, bf16[1024,768]{1,0:T(8,128)(2,1)}, u32[]{:S(2)}, u32[]{:S(2)}) collective-permute-start(bf16[1024,768]{1,0:T(8,128)(2,1)} %get-tuple-element.102), channel_id=1, source_target_pairs={{0,1},{1,0},{2,3},{3,2},{4,5},{5,4},{6,7},{7,6},{8,9},{9,8},{10,11... | collective-permute-start | bytes 4718600 | tf_op jit(solution)/shard_map/ppermute | solution.py:518
  43.9 76.0 %copy-start.7 = (s32[16]{0:T(128)S(1)}, s32[16]{0:T(128)}, u32[]{:S(2)}) copy-start(s32[16]{0:T(128)} %copy-done.6) | copy-start | bytes 196
  43.9 76.0 %copy-start.8 = (f32[1,768]{1,0:T(1,128)S(1)}, f32[1,768]{1,0:T(1,128)}, u32[]{:S(2)}) copy-start(f32[1,768]{1,0:T(1,128)} %broadcast_in_dim.14.refs_3_) | copy-start | bytes 9220
  43.9 76.0 %copy-start.9 = (bf16[768,768]{1,0:T(8,128)(2,1)S(1)}, bf16[768,768]{1,0:T(8,128)(2,1)}, u32[]{:S(2)}) copy-start(bf16[768,768]{1,0:T(8,128)(2,1)} %refs_4_.5) | copy-start | bytes 3538948
  119.4 14.4 %collective-permute-start.2 = (bf16[3072,384]{1,0:T(8,128)(2,1)}, bf16[3072,384]{1,0:T(8,128)(2,1)S(1)}, u32[]{:S(2)}, u32[]{:S(2)}) collective-permute-start(bf16[3072,384]{1,0:T(8,128)(2,1)} %get-tuple-element.103.refs_7_), channel_id=1, source_target_pairs={{0,1},{1,0},{2,3},{3,2},{4,5},{5,4},{6,7},{7,6},{8,9},{9,8},{10,11... | collective-permute-start | bytes 7077896 | tf_op jit(solution)/shard_map/ppermute | solution.py:518
  119.7 14.1 %collective-permute-start.3 = (bf16[768,1536]{1,0:T(8,128)(2,1)}, bf16[768,1536]{1,0:T(8,128)(2,1)S(1)}, u32[]{:S(2)}, u32[]{:S(2)}) collective-permute-start(bf16[768,1536]{1,0:T(8,128)(2,1)} %get-tuple-element.105.refs_8_), channel_id=1, source_target_pairs={{0,1},{1,0},{2,3},{3,2},{4,5},{5,4},{6,7},{7,6},{8,9},{9,8},{10,11... | collective-permute-start | bytes 7077896 | tf_op jit(solution)/shard_map/ppermute | solution.py:518
  133.5 53.2 %collective-permute-start.6 = (bf16[768,384]{1,0:T(8,128)(2,1)S(1)}, bf16[768,384]{1,0:T(8,128)(2,1)S(1)}, u32[]{:S(2)}, u32[]{:S(2)}) collective-permute-start(bf16[768,384]{1,0:T(8,128)(2,1)S(1)} %get-tuple-element.115.refs_20_), channel_id=1, source_target_pairs={{0,1},{1,0},{2,3},{3,2},{4,5},{5,4},{6,7},{7,6},{8,9},{9,8},{10,11... | collective-permute-start | bytes 1769480 | tf_op jit(solution)/shard_map/ppermute | solution.py:518
  139.3 47.3 %collective-permute-start.4 = (bf16[1536,384]{1,0:T(8,128)(2,1)}, bf16[1536,384]{1,0:T(8,128)(2,1)S(1)}, u32[]{:S(2)}, u32[]{:S(2)}) collective-permute-start(bf16[1536,384]{1,0:T(8,128)(2,1)} %get-tuple-element.112.refs_18_), channel_id=1, source_target_pairs={{0,2},{2,0},{4,6},{6,4},{8,10},{10,8},{12,14},{14,12},{16,18},{18,... | collective-permute-start | bytes 3538952 | tf_op jit(solution)/shard_map/ppermute | solution.py:518
  142.0 44.7 %collective-permute-start.5 = (bf16[1536,384]{1,0:T(8,128)(2,1)}, bf16[1536,384]{1,0:T(8,128)(2,1)S(1)}, u32[]{:S(2)}, u32[]{:S(2)}) collective-permute-start(bf16[1536,384]{1,0:T(8,128)(2,1)} %get-tuple-element.114.refs_19_), channel_id=1, source_target_pairs={{0,4},{2,6},{4,0},{6,2},{8,12},{10,14},{12,8},{14,10},{16,20},{18,... | collective-permute-start | bytes 3538952 | tf_op jit(solution)/shard_map/ppermute | solution.py:518
  164.7 22.0 %collective-permute-start.7 = (bf16[768,384]{1,0:T(8,128)(2,1)S(1)}, bf16[768,384]{1,0:T(8,128)(2,1)S(1)}, u32[]{:S(2)}, u32[]{:S(2)}) collective-permute-start(bf16[768,384]{1,0:T(8,128)(2,1)S(1)} %get-tuple-element.120.refs_18_), channel_id=1, source_target_pairs={{0,1},{1,0},{2,3},{3,2},{4,5},{5,4},{6,7},{7,6},{8,9},{9,8},{10,11... | collective-permute-start | bytes 1769480 | tf_op jit(solution)/shard_map/ppermute | solution.py:518
  186.2 43.5 %collective-permute-start.13 = (bf16[768,384]{1,0:T(8,128)(2,1)S(1)}, bf16[768,384]{1,0:T(8,128)(2,1)S(1)}, u32[]{:S(2)}, u32[]{:S(2)}) collective-permute-start(bf16[768,384]{1,0:T(8,128)(2,1)S(1)} %get-tuple-element.132.refs_22_), channel_id=1, source_target_pairs={{0,1},{1,0},{2,3},{3,2},{4,5},{5,4},{6,7},{7,6},{8,9},{9,8},{10,11... | collective-permute-start | bytes 1769480 | tf_op jit(solution)/shard_map/ppermute | solution.py:518
  186.7 55.4 %slice-start = ((s8[4718592]{0:T(1024)(128)(4,1)}), s8[4194304]{0:T(1024)(128)(4,1)S(1)}, s32[]{:S(2)}) async-start(s8[4718592]{0:T(1024)(128)(4,1)} %bitcast.27), calls=%async_computation | async-start | bytes 8388608
  191.1 25.2 %collective-permute-start.10 = (bf16[768,384]{1,0:T(8,128)(2,1)S(1)}, bf16[768,384]{1,0:T(8,128)(2,1)S(1)}, u32[]{:S(2)}, u32[]{:S(2)}) collective-permute-start(bf16[768,384]{1,0:T(8,128)(2,1)S(1)} %get-tuple-element.129.refs_21_), channel_id=1, source_target_pairs={{0,8},{2,10},{4,12},{6,14},{8,0},{10,2},{12,4},{14,6},{16,24},{18,... | collective-permute-start | bytes 1769480 | tf_op jit(solution)/shard_map/ppermute | solution.py:518
  192.7 23.6 %collective-permute-start.8 = (bf16[768,384]{1,0:T(8,128)(2,1)S(1)}, bf16[768,384]{1,0:T(8,128)(2,1)S(1)}, u32[]{:S(2)}, u32[]{:S(2)}) collective-permute-start(bf16[768,384]{1,0:T(8,128)(2,1)S(1)} %get-tuple-element.126.refs_19_), channel_id=1, source_target_pairs={{0,4},{2,6},{4,0},{6,2},{8,12},{10,14},{12,8},{14,10},{16,20},{18,... | collective-permute-start | bytes 1769480 | tf_op jit(solution)/shard_map/ppermute | solution.py:518
  193.2 23.1 %collective-permute-start.9 = (bf16[768,384]{1,0:T(8,128)(2,1)S(1)}, bf16[768,384]{1,0:T(8,128)(2,1)S(1)}, u32[]{:S(2)}, u32[]{:S(2)}) collective-permute-start(bf16[768,384]{1,0:T(8,128)(2,1)S(1)} %get-tuple-element.128.refs_20_), channel_id=1, source_target_pairs={{0,2},{2,0},{4,6},{6,4},{8,10},{10,8},{12,14},{14,12},{16,18},{18,... | collective-permute-start | bytes 1769480 | tf_op jit(solution)/shard_map/ppermute | solution.py:518
  193.7 48.4 %slice-start.1 = ((s8[4718592]{0:T(1024)(128)(4,1)}), s8[524288]{0:T(1024)(128)(4,1)S(1)}, s32[]{:S(2)}) async-start(s8[4718592]{0:T(1024)(128)(4,1)} %bitcast.27), calls=%async_computation.1 | async-start | bytes 1048576
  216.2 13.4 %collective-permute-start.14 = (bf16[768,384]{1,0:T(8,128)(2,1)S(1)}, bf16[768,384]{1,0:T(8,128)(2,1)S(1)}, u32[]{:S(2)}, u32[]{:S(2)}) collective-permute-start(bf16[768,384]{1,0:T(8,128)(2,1)S(1)} %get-tuple-element.137.refs_18_), channel_id=1, source_target_pairs={{0,1},{1,0},{2,3},{3,2},{4,5},{5,4},{6,7},{7,6},{8,9},{9,8},{10,11... | collective-permute-start | bytes 1769480 | tf_op jit(solution)/shard_map/ppermute | solution.py:518
  216.3 5.0 %copy-start.1 = (bf16[768,768]{1,0:T(8,128)(2,1)S(1)}, bf16[768,768]{1,0:T(8,128)(2,1)}, u32[]{:S(2)}) copy-start(bf16[768,768]{1,0:T(8,128)(2,1)} %refs_9_.9) | copy-start | bytes 3538948
  219.1 15.8 %collective-permute-start.11 = (bf16[768,384]{1,0:T(8,128)(2,1)S(1)}, bf16[768,384]{1,0:T(8,128)(2,1)S(1)}, u32[]{:S(2)}, u32[]{:S(2)}) collective-permute-start(bf16[768,384]{1,0:T(8,128)(2,1)S(1)} %get-tuple-element.134.refs_16_), channel_id=1, source_target_pairs={{0,8},{2,10},{4,12},{6,14},{8,0},{10,2},{12,4},{14,6},{16,24},{18,... | collective-permute-start | bytes 1769480 | tf_op jit(solution)/shard_map/ppermute | solution.py:518
  219.2 10.5 %collective-permute-start.15 = (f32[16,384]{1,0:T(8,128)S(1)}, f32[16,384]{1,0:T(8,128)S(1)}, u32[]{:S(2)}, u32[]{:S(2)}) collective-permute-start(f32[16,384]{1,0:T(8,128)S(1)} %get-tuple-element.140.refs_19_.refs_7_), channel_id=1, source_target_pairs={{0,1},{1,0},{2,3},{3,2},{4,5},{5,4},{6,7},{7,6},{8,9},{9,8},{10,11... | collective-permute-start | bytes 73736 | tf_op jit(solution)/shard_map/ppermute | solution.py:518
  219.7 10.0 %collective-permute-start.12 = (bf16[384,384]{1,0:T(8,128)(2,1)S(1)}, bf16[384,384]{1,0:T(8,128)(2,1)S(1)}, u32[]{:S(2)}, u32[]{:S(2)}) collective-permute-start(bf16[384,384]{1,0:T(8,128)(2,1)S(1)} %get-tuple-element.136.refs_17_), channel_id=1, source_target_pairs={{0,2},{2,0},{4,6},{6,4},{8,10},{10,8},{12,14},{14,12},{16,18},{18,... | collective-permute-start | bytes 884744 | tf_op jit(solution)/shard_map/ppermute | solution.py:518
  236.0 21.3 %collective-permute-start.16 = (bf16[608,384]{1,0:T(8,128)(2,1)S(1)}, bf16[608,384]{1,0:T(8,128)(2,1)S(1)}, u32[]{:S(2)}, u32[]{:S(2)}) collective-permute-start(bf16[608,384]{1,0:T(8,128)(2,1)S(1)} %get-tuple-element.149.refs_5_), channel_id=1, source_target_pairs={{0,4},{2,6},{4,0},{6,2},{8,12},{10,14},{12,8},{14,10},{16,20},{18,... | collective-permute-start | bytes 1400840 | tf_op jit(solution)/shard_map/ppermute | solution.py:518
  237.6 19.7 %collective-permute-start.17 = (bf16[416,384]{1,0:T(8,128)(2,1)S(1)}, bf16[416,384]{1,0:T(8,128)(2,1)S(1)}, u32[]{:S(2)}, u32[]{:S(2)}) collective-permute-start(bf16[416,384]{1,0:T(8,128)(2,1)S(1)} %get-tuple-element.151.refs_6_), channel_id=1, source_target_pairs={{0,2},{2,0},{4,6},{6,4},{8,10},{10,8},{12,14},{14,12},{16,18},{18,... | collective-permute-start | bytes 958472 | tf_op jit(solution)/shard_map/ppermute | solution.py:518
  239.0 18.2 %collective-permute-start.18 = (bf16[416,384]{1,0:T(8,128)(2,1)S(1)}, bf16[416,384]{1,0:T(8,128)(2,1)S(1)}, u32[]{:S(2)}, u32[]{:S(2)}) collective-permute-start(bf16[416,384]{1,0:T(8,128)(2,1)S(1)} %get-tuple-element.152.refs_7_), channel_id=1, source_target_pairs={{0,6},{2,4},{4,2},{6,0},{8,14},{10,12},{12,10},{14,8},{16,22},{18,... | collective-permute-start | bytes 958472 | tf_op jit(solution)/shard_map/ppermute | solution.py:518
  239.5 17.8 %collective-permute-start.19 = (bf16[384,384]{1,0:T(8,128)(2,1)S(1)}, bf16[384,384]{1,0:T(8,128)(2,1)S(1)}, u32[]{:S(2)}, u32[]{:S(2)}) collective-permute-start(bf16[384,384]{1,0:T(8,128)(2,1)S(1)} %get-tuple-element.153.refs_4_), channel_id=1, source_target_pairs={{0,16},{2,18},{4,20},{6,22},{8,24},{10,26},{12,28},{14,30},{16,0},... | collective-permute-start | bytes 884744 | tf_op jit(solution)/shard_map/ppermute | solution.py:518
  258.8 16.7 %collective-permute-start.20 = (bf16[1024,768]{1,0:T(8,128)(2,1)}, bf16[1024,768]{1,0:T(8,128)(2,1)S(1)}, u32[]{:S(2)}, u32[]{:S(2)}) collective-permute-start(bf16[1024,768]{1,0:T(8,128)(2,1)} %get-tuple-element.157.refs_20_), channel_id=1, source_target_pairs={{0,1},{1,0},{2,3},{3,2},{4,5},{5,4},{6,7},{7,6},{8,9},{9,8},{10,11... | collective-permute-start | bytes 4718600 | tf_op jit(solution)/shard_map/ppermute | solution.py:518
  258.8 16.7 %collective-permute-start.21 = (bf16[1024,768]{1,0:T(8,128)(2,1)}, bf16[1024,768]{1,0:T(8,128)(2,1)S(1)}, u32[]{:S(2)}, u32[]{:S(2)}) collective-permute-start(bf16[1024,768]{1,0:T(8,128)(2,1)} %get-tuple-element.158.refs_19_), channel_id=1, source_target_pairs={{0,1},{1,0},{2,3},{3,2},{4,5},{5,4},{6,7},{7,6},{8,9},{9,8},{10,11... | collective-permute-start | bytes 4718600 | tf_op jit(solution)/shard_map/ppermute | solution.py:518
  259.3 13.1 %collective-permute-start.22 = (bf16[224,384]{1,0:T(8,128)(2,1)S(1)}, bf16[224,384]{1,0:T(8,128)(2,1)S(1)}, u32[]{:S(2)}, u32[]{:S(2)}) collective-permute-start(bf16[224,384]{1,0:T(8,128)(2,1)S(1)} %get-tuple-element.162.refs_16_), channel_id=1, source_target_pairs={{0,16},{2,18},{4,20},{6,22},{8,24},{10,26},{12,28},{14,30},{16,0},... | collective-permute-start | bytes 516104 | tf_op jit(solution)/shard_map/ppermute | solution.py:518
  259.8 12.6 %collective-permute-start.23 = (bf16[128,384]{1,0:T(8,128)(2,1)S(1)}, bf16[128,384]{1,0:T(8,128)(2,1)S(1)}, u32[]{:S(2)}, u32[]{:S(2)}) collective-permute-start(bf16[128,384]{1,0:T(8,128)(2,1)S(1)} %get-tuple-element.163.refs_17_), channel_id=1, source_target_pairs={{0,8},{2,10},{4,12},{6,14},{8,0},{10,2},{12,4},{14,6},{16,24},{18,... | collective-permute-start | bytes 294920 | tf_op jit(solution)/shard_map/ppermute | solution.py:518
  260.3 12.2 %collective-permute-start.24 = (bf16[128,384]{1,0:T(8,128)(2,1)S(1)}, bf16[128,384]{1,0:T(8,128)(2,1)S(1)}, u32[]{:S(2)}, u32[]{:S(2)}) collective-permute-start(bf16[128,384]{1,0:T(8,128)(2,1)S(1)} %get-tuple-element.164.refs_18_), channel_id=1, source_target_pairs={{0,24},{2,26},{4,28},{6,30},{8,16},{10,18},{12,20},{14,22},{16,8},... | collective-permute-start | bytes 294920 | tf_op jit(solution)/shard_map/ppermute | solution.py:518
  (8 other events, 33.8 us)

commit v2 on v1

--- a/solution.py
+++ b/solution.py
@@ -97,7 +97,15 @@
         strip[h, near1:, :] = jnp.broadcast_to(plus, (strip.shape[1] - near1, 128))
 
 
-def moved(copies, held, arrive, leave):
+def moved(copies, sems):
+    started = [pltpu.make_async_copy(src, dst, sems.at[i]) for i, (src, dst) in enumerate(copies)]
+    for one in started:
+        one.start()
+    for one in started:
+        one.wait()
+
+
+def moved_on(copies, held, arrive, leave):
     first = [pltpu.make_async_copy(src, held.at[at], arrive.at[i]) for i, (src, at, _) in enumerate(copies)]
     then = [pltpu.make_async_copy(held.at[at], dst, leave.at[i]) for i, (_, at, dst) in enumerate(copies)]
     for one in first:
@@ -117,7 +125,7 @@
 
 def pick_kernel(meta, ta, tb, ca, cb, out_x, out_g, held, arrive, leave, *, dims):
     first = [(1 - meta[1]) * n for n in (dims[0], dims[2])]
-    moved(
+    moved_on(
         [
             (pair[kind].at[first[kind] + s], (i, rows), out.at[rows])
             for i, (pair, out) in enumerate((((ta, tb), out_x), ((ca, cb), out_g)))
@@ -129,19 +137,15 @@
     )
 
 
-def place_kernel(
-    meta, out_got, grad_got, a0, b0, a1, b1, out_a, out_b, grad_a, grad_b, held, arrive, leave, *, dims
-):
+def place_kernel(meta, out_got, grad_got, a0, b0, a1, b1, out_a, out_b, grad_a, grad_b, sems, *, dims):
     first = [(1 - meta[1]) * n for n in (dims[0], dims[2])]
     moved(
         [
-            (got.at[rows], (i, rows), pair[kind].at[first[kind] + s])
-            for i, (got, pair) in enumerate(((out_got, (out_a, out_b)), (grad_got, (grad_a, grad_b))))
+            (got.at[rows], pair[kind].at[first[kind] + s])
+            for got, pair in ((out_got, (out_a, out_b)), (grad_got, (grad_a, grad_b)))
             for kind, s, rows in flat_rows(dims)
         ],
-        held,
-        arrive,
-        leave,
+        sems,
     )
 
 
@@ -463,10 +467,10 @@
             part = part + ref[...]
         gain[...] = part
         if place[1]:
-            line = lax.dot_general(
-                jnp.ones((8, 128), F32), part, (((1,), (1,)), ((), ())), precision=lax.Precision.HIGHEST,
-                preferred_element_type=F32,
-            )[:1] / gain_attn[...]
+            high = part.astype(BF)
+            low = (part - high.astype(F32)).astype(BF)
+            ones = jnp.ones((16, 128), BF)
+            line = (dot(ones, high, 1, 1) + dot(ones, low, 1, 1))[:1] / gain_attn[...]
             half = small.shape[1]
             small[0:1, :] += line[:, :half]
             small[1:2, :] += line[:, half:]
@@ -708,7 +712,8 @@
 
     received = pl.BlockSpec((tile, width), lambda i, m: (jnp.clip(i - per, 0, per - 1), 0))
     anywhere = pl.BlockSpec(memory_space=pl.ANY)
-    copies = [pltpu.VMEM((2, th, width), BF)] + [pltpu.SemaphoreType.DMA((2 * (na + nb),))] * 2
+    copies = [pltpu.SemaphoreType.DMA((2 * (na + nb),))]
+    in_vmem = pl.BlockSpec(memory_space=pltpu.VMEM)
     if paired:
         give = call(
             functools.partial(pick_kernel, dims=dims),
@@ -716,7 +721,7 @@
             [anywhere] * 4,
             [anywhere] * 2,
             [sds((th, width), BF)] * 2,
-            scratch=copies,
+            scratch=[pltpu.VMEM((2, th, width), BF)] + copies * 2,
             nbytes=8 * th * width,
             vmem=8,
         )(meta, tokens_a, tokens_b, cotangent_a, cotangent_b)
@@ -753,7 +758,7 @@
         [by_row(width)] * 5,
         [tok] * 5,
         vmem=30,
-        free=(5, 6, 7),
+        free=(3, 5, 6, 7),
         flops=3 * dense * width,
         nbytes=10 * tokens * width,
         after=[strip],
@@ -827,8 +832,8 @@
         ],
         flops=dense * (5 * ff + width),
         nbytes=2 * tokens * ff,
-        vmem=60,
-        free=(3, 8, 9),
+        vmem=52,
+        free=(3, 7, 8, 9),
     )(meta, attn, x, w_out, gain2, *g_in3, w_in, w_back)
 
     bit_count = nrows.bit_length() - 1
@@ -882,7 +887,7 @@
             else:
                 first = Piece(first, every_bit)
                 _, _, hold = shuttle(
-                    meta, half_w, [(back, (1,)), (inner, (0,)), (first, (2,))], none, [dqs[1][0]]
+                    meta, half_w, [(back, (1,)), (inner, (2,)), (first, (0,))], none, [dqs[1][0]]
                 )
                 second = pair_sum(*groups[1])
                 hold.append(groups[1][1])
@@ -933,7 +938,8 @@
                 pltpu.VMEM((2, lb, lb), BF),
                 pltpu.VMEM((2, tokens, 3 * PAIR), BF),
             ],
-            vmem=44,
+            free=(8, 9, 10, 11, 12, 13, 14),
+            vmem=40,
         flops=score_macs * 256 * 8 // 3 + dense * width,
             nbytes=2 * score_macs // 3,
             after=hold,
@@ -945,7 +951,7 @@
     if paired:
         last = Piece([second, pair_sum(*groups[2])], every_bit, carrier=True)
         smalls = [small_sum, swap(small_sum, "seq", 1)]
-        _, _, hold = shuttle(meta, half_w, [(back, (2,)), (inner, (2,)), (first, (0,))], none, [dqs[2][0]])
+        _, _, hold = shuttle(meta, half_w, [(back, (2,)), (inner, (0,)), (first, (1,))], none, [dqs[2][0]])
         hold += [groups[2][1], small_sum]
 
     def token_grads(part):
@@ -971,7 +977,7 @@
         _, small_state, hold = shuttle(
             meta,
             half_w,
-            [(back, (3,)), (inner, (3,)), (first, (1,)), (last, low_bits)],
+            [(back, (3,)), (inner, (3,)), (first, (2,)), (last, low_bits)],
             none,
             [grads1],
             (smalls, ()),
@@ -1022,7 +1028,7 @@
         out_a, out_b, grad_a, grad_b = call(
             functools.partial(place_kernel, dims=dims),
             (1,),
-            [anywhere] * 6,
+            [in_vmem] * 2 + [anywhere] * 4,
             [anywhere] * 4,
             [sds(all_a, BF), sds(all_b, BF)] * 2,
             scratch=copies,

time: 286 us -> 273 us (0.955)
  Pallas kernels: 249 us -> 238 us
  waiting for transfers between devices: 5.25 us -> 0.52 us
  starting transfers between devices: 22.2 us -> 25.4 us
    pallas_call x19, Pallas kernels: 249 us -> 238 us  [call(): made(*(place(i, x) for i, x in enumerate((*args, *after))))]
    ppermute x25 -> x27, waiting for transfers between devices: 5.25 us -> 0.52 us  [swap(): return lax.ppermute(x, axis, [(i, i ^ bit) for i in range(n)])]
    ppermute x25 -> x27, starting transfers between devices: 22.2 us -> 25.4 us  [swap(): return lax.ppermute(x, axis, [(i, i ^ bit) for i in range(n)])]
  transfers between devices with their start and end apart: 25 -> 27, of which waited for: 1 -> 1; matrix products, arithmetic and copies ran while one was open for 1% -> 1% of each run, Pallas kernels for 58% -> 58%
where the time goes in v2:
time: 273 us; the launch traced here: 268 us
  Pallas kernels  238 us (87%)
  starting transfers between devices  25.4 us (9%)
    pallas_call x19, Pallas kernels, call(): made(*(place(i, x) for i, x in enumerate((*args, *after))))  238 us
    ppermute x27, starting transfers between devices, swap(): return lax.ppermute(x, axis, [(i, i ^ bit) for i in range(n)])  25.4 us
  transfers between devices with their start and end apart: 27, of which 1 were waited for; matrix products, arithmetic and copies ran while one was open for 1% of the time, Pallas kernels for 58%

profile of v2, /device:TPU:0, one launch (start us, length us, event | category | flops | bytes accessed | tf_op | source)
XLA Modules:
  0.0 268.1 jit_solution(9309112471197172317)
XLA Ops:
  0.6 0.8 concatenate.3.meta
  1.4 3.4 %shard_map.246 = (bf16[1024,768]{1,0:T(8,128)(2,1)}, bf16[1024,768]{1,0:T(8,128)(2,1)}) custom-call(s32[16]{0:T(128)S(1)} %concatenate.3.meta, bf16[4,256,768]{2,1,0:T(8,128)(2,1)} %refs_0_.3, bf16[8,128,768]{2,1,0:T(8,128)(2,1)} %refs_1_.4, bf16[4,256,768]{2,1,0:T(8,128)(2,1)} %refs_4_.4, bf16[8,128,768]{2,1,0:T(8,128)(2,1)} %refs_5_.3), custom_call_target="tpu_custom_call" | custom-call | bytes 6291456 | tf_op jit(solution)/shard_map/pallas_call | solution.py:67
  5.7 3.9 %shard_map.247.refs_7_.refs_3_ = f32[12,896,128]{2,1,0:T(8,128)} custom-call(s32[16]{0:T(128)S(1)} %concatenate.3.meta, f32[3,8,128]{2,1,0:T(8,128)S(1)} %pad.4.refs_0_, f32[256,128]{1,0:T(8,128)S(1)} %fusion.1.refs_1_.refs_14_), custom_call_target="tpu_custom_call" | custom-call | bytes 5505024 | tf_op jit(solution)/shard_map/pallas_call | solution.py:67
  10.1 12.3 %shard_map.248 = (bf16[2,1024,768]{2,1,0:T(8,128)(2,1)}, bf16[2,1024,768]{2,1,0:T(8,128)(2,1)}, bf16[2,1024,768]{2,1,0:T(8,128)(2,1)}, bf16[2,1024,768]{2,1,0:T(8,128)(2,1)}, bf16[2,1024,768]{2,1,0:T(8,128)(2,1)}) custom-call(s32[16]{0:T(128)S(1)} %concatenate.3.meta, bf16[4,256,768]{2,1,0:T(8,128)(2,1)} %refs_0_.3, bf16[8,128,768]{2,1,0:T(8,128)(2,1)} %refs_1_.4, ...), custom_call_target="tpu_custom_call" | custom-call | flops 7247757312 | bytes 15728640 | tf_op jit(solution)/shard_map/pallas_call | solution.py:67
  22.3 21.3 %shard_map.249 = (bf16[12,2,512,512]{3,2,1,0:T(8,128)(2,1)}, bf16[12,4,256,256]{3,2,1,0:T(8,128)(2,1)}, bf16[2,1024,768]{2,1,0:T(8,128)(2,1)}, bf16[2,1024,768]{2,1,0:T(8,128)(2,1)}) custom-call(s32[16]{0:T(128)S(1)} %concatenate.3.meta, bf16[2,1024,768]{2,1,0:T(8,128)(2,1)} %get-tuple-element.99.refs_0_, bf16[2,1024,768]{2,1,0:T(8,128)(2,1)} %get-tuple-element.100.refs_1_, ...), custom_call_target="tpu_custom_call" | custom-call | flops 9663676416 | bytes 18874368 | tf_op jit(solution)/shard_map/pallas_call | solution.py:67
  43.6 74.5 %shard_map.250 = (bf16[2,1024,768]{2,1,0:T(8,128)(2,1)}, bf16[2,1024,768]{2,1,0:T(8,128)(2,1)}, bf16[2,1024,3072]{2,1,0:T(8,128)(2,1)}, bf16[3072,384]{1,0:T(8,1...) custom-call(s32[16]{0:T(128)S(1)} %concatenate.3.meta, ...), custom_call_target="tpu_custom_call" | custom-call | flops 50734301184 | bytes 12582912 | tf_op jit(solution)/shard_map/pallas_call | solution.py:67
  118.8 13.6 %shard_map.251 = (bf16[2,1024,768]{2,1,0:T(8,128)(2,1)}, bf16[2,1024,768]{2,1,0:T(8,128)(2,1)}, f32[16,384]{1,0:T(8,128)S(1)}, bf16[768,384]{1,0:T(8,128)(2,1)S(1)}, bf16[768,384]{1,0:T(8,128)(2,1)S(1)}) custom-call(s32[16]{0:T(128)S(1)} %concatenate.3.meta, bf16[2,1024,768]{2,1,0:T(8,128)(2,1)} %get-tuple-element.109.refs_0_, ...), custom_call_target="tpu_custom_call" | custom-call | flops 14495514624 | bytes 12582912 | tf_op jit(solution)/shard_map/pallas_call | solution.py:67
  132.5 5.8 %shard_map.252 = (bf16[3072,384]{1,0:T(8,128)(2,1)}, bf16[1536,384]{1,0:T(8,128)(2,1)}, bf16[1536,384]{1,0:T(8,128)(2,1)}) custom-call(s32[16]{0:T(128)S(1)} %concatenate.3.meta, bf16[2,2,2,2,192,384]{5,4,3,2,1,0:T(8,128)(2,1)S(1)} %bitcast.17, bf16[2,2,2,2,192,384]{5,4,3,2,1,0:T(8,128)(2,1)} %bitcast.29, bf16[2,2,2,2,48,1536]{5,4,3,2,1,0:T(8,128)(2,1)S(1)} %bitcast.18, ...), custom_call_target="tpu_custom_call" | custom-call | bytes 9437184 | tf_op jit(solution)/shard_map/pallas_call | solution.py:67
  138.4 2.7 %collective-permute-start.4 = (bf16[1536,384]{1,0:T(8,128)(2,1)}, bf16[1536,384]{1,0:T(8,128)(2,1)S(1)}, u32[]{:S(2)}, u32[]{:S(2)}) collective-permute-start(bf16[1536,384]{1,0:T(8,128)(2,1)} %get-tuple-element.114.refs_18_), channel_id=1, source_target_pairs={{0,2},{2,0},{4,6},{6,4},{8,10},{10,8},{12,14},{14,12},{16,18},{18,... | collective-permute-start | bytes 3538952 | tf_op jit(solution)/shard_map/ppermute | solution.py:522
  141.1 1.5 collective-permute-start.5
  142.6 19.1 %shard_map.253 = (bf16[2,1024,256]{2,1,0:T(8,128)(2,1)}, bf16[2,1024,256]{2,1,0:T(8,128)(2,1)}, bf16[2,1024,256]{2,1,0:T(8,128)(2,1)}, bf16[768,384]{1,0:T(8,128...) custom-call(s32[16]{0:T(128)S(1)} %concatenate.3.meta, ...), custom_call_target="tpu_custom_call" | custom-call | flops 8858370048 | bytes 6291456 | tf_op jit(solution)/shard_map/pallas_call | solution.py:67
  161.7 19.3 %shard_map.254 = (bf16[2,1024,256]{2,1,0:T(8,128)(2,1)}, bf16[2,1024,256]{2,1,0:T(8,128)(2,1)}, bf16[2,1024,256]{2,1,0:T(8,128)(2,1)}, bf16[768,384]{1,0:T(8,128...) custom-call(s32[16]{0:T(128)S(1)} %concatenate.3.meta, ...), custom_call_target="tpu_custom_call" | custom-call | flops 8858370048 | bytes 6291456 | tf_op jit(solution)/shard_map/pallas_call | solution.py:67
  181.5 4.4 %shard_map.255 = (bf16[2304,384]{1,0:T(8,128)(2,1)}, bf16[768,384]{1,0:T(8,128)(2,1)S(1)}, bf16[768,384]{1,0:T(8,128)(2,1)S(1)}, bf16[768,384]{1,0:T(8,128)(2,1)S(1)}) custom-call(s32[16]{0:T(128)S(1)} %concatenate.3.meta, bf16[1536,384]{1,0:T(8,128)(2,1)S(1)} %collective-permute-done.4.refs_0_, bf16[3072,384]{1,0:T(8,128)(2,1)} %get-tuple-element.115.refs_17_.refs_1_, ...), custom_call_target="tpu_custom_call" | custom-call | bytes 7077888 | tf_op jit(solution)/shard_map/pallas_call | solution.py:67
  186.4 2.1 collective-permute-start.9
  188.5 19.9 %shard_map.256 = (bf16[2,1024,256]{2,1,0:T(8,128)(2,1)}, bf16[2,1024,256]{2,1,0:T(8,128)(2,1)}, bf16[2,1024,256]{2,1,0:T(8,128)(2,1)}, bf16[768,384]{1,0:T(8,128...) custom-call(s32[16]{0:T(128)S(1)} %concatenate.3.meta, ...), custom_call_target="tpu_custom_call" | custom-call | flops 8858370048 | bytes 6291456 | tf_op jit(solution)/shard_map/pallas_call | solution.py:67
  208.9 2.4 shard_map.257
  211.4 1.9 collective-permute-start.12
  213.3 1.5 collective-permute-start.13
  214.8 8.3 %shard_map.258.refs_10_.refs_9_.refs_7_ = bf16[1024,768]{1,0:T(8,128)(2,1)} custom-call(s32[16]{0:T(128)S(1)} %concatenate.3.meta, bf16[2,1024,256]{2,1,0:T(8,128)(2,1)} %get-tuple-element.144.refs_0_, bf16[2,1024,256]{2,1,0:T(8,128)(2,1)} %get-tuple-element.127.refs_7_.refs_1_, bf16[2,1024,256]{2,1,0:T(8,128)(2,1)} %get-tuple-element.135.refs_4_.refs_2_, ...), custom_call_target="tpu_custom_call" | custom-call | flops 3623878656 | bytes 11010048 | tf_op jit(solution)/shard_map/pallas_call | solution.py:67
  223.2 1.1 shard_map.259
  224.3 0.6 collective-permute-start.18
  225.1 2.8 %collective-permute-start.20 = (bf16[416,384]{1,0:T(8,128)(2,1)S(1)}, bf16[416,384]{1,0:T(8,128)(2,1)S(1)}, u32[]{:S(2)}, u32[]{:S(2)}) collective-permute-start(bf16[416,384]{1,0:T(8,128)(2,1)S(1)} %get-tuple-element.156.refs_8_), channel_id=1, source_target_pairs={{0,6},{2,4},{4,2},{6,0},{8,14},{10,12},{12,10},{14,8},{16,22},{18,... | collective-permute-start | bytes 958472 | tf_op jit(solution)/shard_map/ppermute | solution.py:522
  227.9 2.6 collective-permute-start.21
  230.5 1.6 collective-permute-start.17
  232.1 15.2 %shard_map.260 = (bf16[1024,768]{1,0:T(8,128)(2,1)}, bf16[4,256,768]{2,1,0:T(8,128)(2,1)}, bf16[8,128,768]{2,1,0:T(8,128)(2,1)}) custom-call(s32[16]{0:T(128)S(1)} %concatenate.3.meta, bf16[2,1024,3072]{2,1,0:T(8,128)(2,1)} %get-tuple-element.159.refs_0_, bf16[3072,768]{1,0:T(8,128)(2,1)S(1)} %bitcast.28, ...), custom_call_target="tpu_custom_call" | custom-call | flops 9663676416 | bytes 12582912 | tf_op jit(solution)/shard_map/pallas_call | solution.py:67
  247.3 1.5 shard_map.261
  250.2 3.6 %collective-permute-start.26 = (bf16[128,384]{1,0:T(8,128)(2,1)S(1)}, bf16[128,384]{1,0:T(8,128)(2,1)S(1)}, u32[]{:S(2)}, u32[]{:S(2)}) collective-permute-start(bf16[128,384]{1,0:T(8,128)(2,1)S(1)} %get-tuple-element.168.refs_18_), channel_id=1, source_target_pairs={{0,24},{2,26},{4,28},{6,30},{8,16},{10,18},{12,20},{14,22},{16,8},... | collective-permute-start | bytes 294920 | tf_op jit(solution)/shard_map/ppermute | solution.py:522
  253.8 8.7 %shard_map.262 = (bf16[4,256,768]{2,1,0:T(8,128)(2,1)}, bf16[8,128,768]{2,1,0:T(8,128)(2,1)}) custom-call(s32[16]{0:T(128)S(1)} %concatenate.3.meta, bf16[2,1024,256]{2,1,0:T(8,128)(2,1)} %get-tuple-element.144.refs_0_, bf16[2,1024,256]{2,1,0:T(8,128)(2,1)} %get-tuple-element.127.refs_7_.refs_1_, bf16[2,1024,256]{2,1,0:T(8,128)(2,1)} %get-tuple-element.135.refs_4_.refs_2_, ...), custom_call_target="tpu_custom_call" | custom-call | flops 3623878656 | bytes 11010048 | tf_op jit(solution)/shard_map/pallas_call | solution.py:67
  262.5 1.3 shard_map.264
  263.8 0.6 reshape.121
  265.0 0.6 slice_bitcast_fusion
  265.6 2.3 shard_map.263
  (74 shorter events, 5.7 us)
Async XLA Ops:
  4.8 5.2 %collective-permute-start = (bf16[1024,768]{1,0:T(8,128)(2,1)}, bf16[1024,768]{1,0:T(8,128)(2,1)S(1)}, u32[]{:S(2)}, u32[]{:S(2)}) collective-permute-start(bf16[1024,768]{1,0:T(8,128)(2,1)} %get-tuple-element.98), channel_id=1, source_target_pairs={{0,1},{1,0},{2,3},{3,2},{4,5},{5,4},{6,7},{7,6},{8,9},{9,8},{10,11... | collective-permute-start | bytes 4718600 | tf_op jit(solution)/shard_map/ppermute | solution.py:522
  5.3 38.3 %collective-permute-start.1 = (bf16[1024,768]{1,0:T(8,128)(2,1)}, bf16[1024,768]{1,0:T(8,128)(2,1)}, u32[]{:S(2)}, u32[]{:S(2)}) collective-permute-start(bf16[1024,768]{1,0:T(8,128)(2,1)} %get-tuple-element.104), channel_id=1, source_target_pairs={{0,1},{1,0},{2,3},{3,2},{4,5},{5,4},{6,7},{7,6},{8,9},{9,8},{10,11... | collective-permute-start | bytes 4718600 | tf_op jit(solution)/shard_map/ppermute | solution.py:522
  5.6 4.4 %copy-start = (bf16[768,768]{1,0:T(8,128)(2,1)S(1)}, bf16[768,768]{1,0:T(8,128)(2,1)}, u32[]{:S(2)}) copy-start(bf16[768,768]{1,0:T(8,128)(2,1)} %refs_9_.9) | copy-start | bytes 3538948
  22.3 21.3 %copy-start.4 = (bf16[768,768]{1,0:T(8,128)(2,1)S(1)}, bf16[768,768]{1,0:T(8,128)(2,1)}, u32[]{:S(2)}) copy-start(bf16[768,768]{1,0:T(8,128)(2,1)} %refs_4_.5) | copy-start | bytes 3538948
  118.2 14.4 %collective-permute-start.2 = (bf16[3072,384]{1,0:T(8,128)(2,1)}, bf16[3072,384]{1,0:T(8,128)(2,1)S(1)}, u32[]{:S(2)}, u32[]{:S(2)}) collective-permute-start(bf16[3072,384]{1,0:T(8,128)(2,1)} %get-tuple-element.105.refs_7_), channel_id=1, source_target_pairs={{0,1},{1,0},{2,3},{3,2},{4,5},{5,4},{6,7},{7,6},{8,9},{9,8},{10,11... | collective-permute-start | bytes 7077896 | tf_op jit(solution)/shard_map/ppermute | solution.py:522
  118.5 14.1 %collective-permute-start.3 = (bf16[768,1536]{1,0:T(8,128)(2,1)}, bf16[768,1536]{1,0:T(8,128)(2,1)S(1)}, u32[]{:S(2)}, u32[]{:S(2)}) collective-permute-start(bf16[768,1536]{1,0:T(8,128)(2,1)} %get-tuple-element.107.refs_8_), channel_id=1, source_target_pairs={{0,1},{1,0},{2,3},{3,2},{4,5},{5,4},{6,7},{7,6},{8,9},{9,8},{10,11... | collective-permute-start | bytes 7077896 | tf_op jit(solution)/shard_map/ppermute | solution.py:522
  132.3 49.1 %collective-permute-start.6 = (bf16[768,384]{1,0:T(8,128)(2,1)S(1)}, bf16[768,384]{1,0:T(8,128)(2,1)S(1)}, u32[]{:S(2)}, u32[]{:S(2)}) collective-permute-start(bf16[768,384]{1,0:T(8,128)(2,1)S(1)} %get-tuple-element.117.refs_20_), channel_id=1, source_target_pairs={{0,1},{1,0},{2,3},{3,2},{4,5},{5,4},{6,7},{7,6},{8,9},{9,8},{10,11... | collective-permute-start | bytes 1769480 | tf_op jit(solution)/shard_map/ppermute | solution.py:522
  132.5 10.1 %copy-start.3 = (bf16[2,1024,768]{2,1,0:T(8,128)(2,1)S(1)}, bf16[2,1024,768]{2,1,0:T(8,128)(2,1)}, u32[]{:S(2)}) copy-start(bf16[2,1024,768]{2,1,0:T(8,128)(2,1)} %get-tuple-element.120.refs_7_) | copy-start | bytes 9437188
  138.4 43.1 %collective-permute-start.4 = (bf16[1536,384]{1,0:T(8,128)(2,1)}, bf16[1536,384]{1,0:T(8,128)(2,1)S(1)}, u32[]{:S(2)}, u32[]{:S(2)}) collective-permute-start(bf16[1536,384]{1,0:T(8,128)(2,1)} %get-tuple-element.114.refs_18_), channel_id=1, source_target_pairs={{0,2},{2,0},{4,6},{6,4},{8,10},{10,8},{12,14},{14,12},{16,18},{18,... | collective-permute-start | bytes 3538952 | tf_op jit(solution)/shard_map/ppermute | solution.py:522
  141.1 40.4 %collective-permute-start.5 = (bf16[1536,384]{1,0:T(8,128)(2,1)}, bf16[1536,384]{1,0:T(8,128)(2,1)S(1)}, u32[]{:S(2)}, u32[]{:S(2)}) collective-permute-start(bf16[1536,384]{1,0:T(8,128)(2,1)} %get-tuple-element.116.refs_19_), channel_id=1, source_target_pairs={{0,4},{2,6},{4,0},{6,2},{8,12},{10,14},{12,8},{14,10},{16,20},{18,... | collective-permute-start | bytes 3538952 | tf_op jit(solution)/shard_map/ppermute | solution.py:522
  161.7 19.8 %collective-permute-start.7 = (bf16[768,384]{1,0:T(8,128)(2,1)S(1)}, bf16[768,384]{1,0:T(8,128)(2,1)S(1)}, u32[]{:S(2)}, u32[]{:S(2)}) collective-permute-start(bf16[768,384]{1,0:T(8,128)(2,1)S(1)} %get-tuple-element.122.refs_18_), channel_id=1, source_target_pairs={{0,1},{1,0},{2,3},{3,2},{4,5},{5,4},{6,7},{7,6},{8,9},{9,8},{10,11... | collective-permute-start | bytes 1769480 | tf_op jit(solution)/shard_map/ppermute | solution.py:522
  181.0 32.4 %collective-permute-start.14 = (bf16[768,384]{1,0:T(8,128)(2,1)S(1)}, bf16[768,384]{1,0:T(8,128)(2,1)S(1)}, u32[]{:S(2)}, u32[]{:S(2)}) collective-permute-start(bf16[768,384]{1,0:T(8,128)(2,1)S(1)} %get-tuple-element.134.refs_22_), channel_id=1, source_target_pairs={{0,1},{1,0},{2,3},{3,2},{4,5},{5,4},{6,7},{7,6},{8,9},{9,8},{10,11... | collective-permute-start | bytes 1769480 | tf_op jit(solution)/shard_map/ppermute | solution.py:522
  181.5 50.6 %slice-start = ((s8[4718592]{0:T(1024)(128)(4,1)}), s8[4194304]{0:T(1024)(128)(4,1)S(1)}, s32[]{:S(2)}) async-start(s8[4718592]{0:T(1024)(128)(4,1)} %bitcast.27), calls=%async_computation | async-start | bytes 8388608
  185.9 22.5 %collective-permute-start.10 = (bf16[768,384]{1,0:T(8,128)(2,1)S(1)}, bf16[768,384]{1,0:T(8,128)(2,1)S(1)}, u32[]{:S(2)}, u32[]{:S(2)}) collective-permute-start(bf16[768,384]{1,0:T(8,128)(2,1)S(1)} %get-tuple-element.131.refs_21_), channel_id=1, source_target_pairs={{0,2},{2,0},{4,6},{6,4},{8,10},{10,8},{12,14},{14,12},{16,18},{18,... | collective-permute-start | bytes 1769480 | tf_op jit(solution)/shard_map/ppermute | solution.py:522
  186.4 22.5 %collective-permute-start.8 = (bf16[768,384]{1,0:T(8,128)(2,1)S(1)}, bf16[768,384]{1,0:T(8,128)(2,1)S(1)}, u32[]{:S(2)}, u32[]{:S(2)}) collective-permute-start(bf16[768,384]{1,0:T(8,128)(2,1)S(1)} %get-tuple-element.128.refs_19_), channel_id=1, source_target_pairs={{0,4},{2,6},{4,0},{6,2},{8,12},{10,14},{12,8},{14,10},{16,20},{18,... | collective-permute-start | bytes 1769480 | tf_op jit(solution)/shard_map/ppermute | solution.py:522
  186.4 22.5 %collective-permute-start.9 = (bf16[768,384]{1,0:T(8,128)(2,1)S(1)}, bf16[768,384]{1,0:T(8,128)(2,1)S(1)}, u32[]{:S(2)}, u32[]{:S(2)}) collective-permute-start(bf16[768,384]{1,0:T(8,128)(2,1)S(1)} %get-tuple-element.130.refs_20_), channel_id=1, source_target_pairs={{0,8},{2,10},{4,12},{6,14},{8,0},{10,2},{12,4},{14,6},{16,24},{18,... | collective-permute-start | bytes 1769480 | tf_op jit(solution)/shard_map/ppermute | solution.py:522
  188.5 43.6 %slice-start.1 = ((s8[4718592]{0:T(1024)(128)(4,1)}), s8[524288]{0:T(1024)(128)(4,1)S(1)}, s32[]{:S(2)}) async-start(s8[4718592]{0:T(1024)(128)(4,1)} %bitcast.27), calls=%async_computation.1 | async-start | bytes 1048576
  208.4 14.8 %collective-permute-start.15 = (bf16[768,384]{1,0:T(8,128)(2,1)S(1)}, bf16[768,384]{1,0:T(8,128)(2,1)S(1)}, u32[]{:S(2)}, u32[]{:S(2)}) collective-permute-start(bf16[768,384]{1,0:T(8,128)(2,1)S(1)} %get-tuple-element.140.refs_19_), channel_id=1, source_target_pairs={{0,1},{1,0},{2,3},{3,2},{4,5},{5,4},{6,7},{7,6},{8,9},{9,8},{10,11... | collective-permute-start | bytes 1769480 | tf_op jit(solution)/shard_map/ppermute | solution.py:522
  208.4 14.8 %collective-permute-start.16 = (f32[16,384]{1,0:T(8,128)S(1)}, f32[16,384]{1,0:T(8,128)S(1)}, u32[]{:S(2)}, u32[]{:S(2)}) collective-permute-start(f32[16,384]{1,0:T(8,128)S(1)} %get-tuple-element.143.refs_20_.refs_8_), channel_id=1, source_target_pairs={{0,1},{1,0},{2,3},{3,2},{4,5},{5,4},{6,7},{7,6},{8,9},{9,8},{10,11... | collective-permute-start | bytes 73736 | tf_op jit(solution)/shard_map/ppermute | solution.py:522
  211.3 11.9 %collective-permute-start.11 = (bf16[384,384]{1,0:T(8,128)(2,1)S(1)}, bf16[384,384]{1,0:T(8,128)(2,1)S(1)}, u32[]{:S(2)}, u32[]{:S(2)}) collective-permute-start(bf16[384,384]{1,0:T(8,128)(2,1)S(1)} %get-tuple-element.136.refs_16_), channel_id=1, source_target_pairs={{0,8},{2,10},{4,12},{6,14},{8,0},{10,2},{12,4},{14,6},{16,24},{18,... | collective-permute-start | bytes 884744 | tf_op jit(solution)/shard_map/ppermute | solution.py:522
  211.4 11.8 %collective-permute-start.12 = (bf16[384,384]{1,0:T(8,128)(2,1)S(1)}, bf16[384,384]{1,0:T(8,128)(2,1)S(1)}, u32[]{:S(2)}, u32[]{:S(2)}) collective-permute-start(bf16[384,384]{1,0:T(8,128)(2,1)S(1)} %get-tuple-element.138.refs_17_), channel_id=1, source_target_pairs={{0,2},{2,0},{4,6},{6,4},{8,10},{10,8},{12,14},{14,12},{16,18},{18,... | collective-permute-start | bytes 884744 | tf_op jit(solution)/shard_map/ppermute | solution.py:522
  213.3 9.9 %collective-permute-start.13 = (bf16[384,384]{1,0:T(8,128)(2,1)S(1)}, bf16[384,384]{1,0:T(8,128)(2,1)S(1)}, u32[]{:S(2)}, u32[]{:S(2)}) collective-permute-start(bf16[384,384]{1,0:T(8,128)(2,1)S(1)} %get-tuple-element.139.refs_18_), channel_id=1, source_target_pairs={{0,4},{2,6},{4,0},{6,2},{8,12},{10,14},{12,8},{14,10},{16,20},{18,... | collective-permute-start | bytes 884744 | tf_op jit(solution)/shard_map/ppermute | solution.py:522
  224.3 23.0 %collective-permute-start.18 = (bf16[416,384]{1,0:T(8,128)(2,1)S(1)}, bf16[416,384]{1,0:T(8,128)(2,1)S(1)}, u32[]{:S(2)}, u32[]{:S(2)}) collective-permute-start(bf16[416,384]{1,0:T(8,128)(2,1)S(1)} %get-tuple-element.154.refs_6_), channel_id=1, source_target_pairs={{0,2},{2,0},{4,6},{6,4},{8,10},{10,8},{12,14},{14,12},{16,18},{18,... | collective-permute-start | bytes 958472 | tf_op jit(solution)/shard_map/ppermute | solution.py:522
  224.9 22.4 %collective-permute-start.19 = (bf16[416,384]{1,0:T(8,128)(2,1)S(1)}, bf16[416,384]{1,0:T(8,128)(2,1)S(1)}, u32[]{:S(2)}, u32[]{:S(2)}) collective-permute-start(bf16[416,384]{1,0:T(8,128)(2,1)S(1)} %get-tuple-element.155.refs_7_), channel_id=1, source_target_pairs={{0,4},{2,6},{4,0},{6,2},{8,12},{10,14},{12,8},{14,10},{16,20},{18,... | collective-permute-start | bytes 958472 | tf_op jit(solution)/shard_map/ppermute | solution.py:522
  225.1 22.3 %collective-permute-start.20 = (bf16[416,384]{1,0:T(8,128)(2,1)S(1)}, bf16[416,384]{1,0:T(8,128)(2,1)S(1)}, u32[]{:S(2)}, u32[]{:S(2)}) collective-permute-start(bf16[416,384]{1,0:T(8,128)(2,1)S(1)} %get-tuple-element.156.refs_8_), channel_id=1, source_target_pairs={{0,6},{2,4},{4,2},{6,0},{8,14},{10,12},{12,10},{14,8},{16,22},{18,... | collective-permute-start | bytes 958472 | tf_op jit(solution)/shard_map/ppermute | solution.py:522
  227.9 19.4 %collective-permute-start.21 = (bf16[384,384]{1,0:T(8,128)(2,1)S(1)}, bf16[384,384]{1,0:T(8,128)(2,1)S(1)}, u32[]{:S(2)}, u32[]{:S(2)}) collective-permute-start(bf16[384,384]{1,0:T(8,128)(2,1)S(1)} %get-tuple-element.157.refs_4_), channel_id=1, source_target_pairs={{0,16},{2,18},{4,20},{6,22},{8,24},{10,26},{12,28},{14,30},{16,0},... | collective-permute-start | bytes 884744 | tf_op jit(solution)/shard_map/ppermute | solution.py:522
  230.5 16.8 %collective-permute-start.17 = (bf16[192,384]{1,0:T(8,128)(2,1)S(1)}, bf16[192,384]{1,0:T(8,128)(2,1)S(1)}, u32[]{:S(2)}, u32[]{:S(2)}) collective-permute-start(bf16[192,384]{1,0:T(8,128)(2,1)S(1)} %get-tuple-element.152.refs_5_), channel_id=1, source_target_pairs={{0,8},{2,10},{4,12},{6,14},{8,0},{10,2},{12,4},{14,6},{16,24},{18,... | collective-permute-start | bytes 442376 | tf_op jit(solution)/shard_map/ppermute | solution.py:522
  248.9 16.7 %collective-permute-start.22 = (bf16[1024,768]{1,0:T(8,128)(2,1)}, bf16[1024,768]{1,0:T(8,128)(2,1)S(1)}, u32[]{:S(2)}, u32[]{:S(2)}) collective-permute-start(bf16[1024,768]{1,0:T(8,128)(2,1)} %get-tuple-element.161.refs_20_), channel_id=1, source_target_pairs={{0,1},{1,0},{2,3},{3,2},{4,5},{5,4},{6,7},{7,6},{8,9},{9,8},{10,11... | collective-permute-start | bytes 4718600 | tf_op jit(solution)/shard_map/ppermute | solution.py:522
  248.9 16.7 %collective-permute-start.23 = (bf16[1024,768]{1,0:T(8,128)(2,1)}, bf16[1024,768]{1,0:T(8,128)(2,1)S(1)}, u32[]{:S(2)}, u32[]{:S(2)}) collective-permute-start(bf16[1024,768]{1,0:T(8,128)(2,1)} %get-tuple-element.162.refs_19_), channel_id=1, source_target_pairs={{0,1},{1,0},{2,3},{3,2},{4,5},{5,4},{6,7},{7,6},{8,9},{9,8},{10,11... | collective-permute-start | bytes 4718600 | tf_op jit(solution)/shard_map/ppermute | solution.py:522
  249.4 13.1 %collective-permute-start.24 = (bf16[224,384]{1,0:T(8,128)(2,1)S(1)}, bf16[224,384]{1,0:T(8,128)(2,1)S(1)}, u32[]{:S(2)}, u32[]{:S(2)}) collective-permute-start(bf16[224,384]{1,0:T(8,128)(2,1)S(1)} %get-tuple-element.166.refs_16_), channel_id=1, source_target_pairs={{0,16},{2,18},{4,20},{6,22},{8,24},{10,26},{12,28},{14,30},{16,0},... | collective-permute-start | bytes 516104 | tf_op jit(solution)/shard_map/ppermute | solution.py:522
  249.7 12.8 %collective-permute-start.25 = (bf16[128,384]{1,0:T(8,128)(2,1)S(1)}, bf16[128,384]{1,0:T(8,128)(2,1)S(1)}, u32[]{:S(2)}, u32[]{:S(2)}) collective-permute-start(bf16[128,384]{1,0:T(8,128)(2,1)S(1)} %get-tuple-element.167.refs_17_), channel_id=1, source_target_pairs={{0,8},{2,10},{4,12},{6,14},{8,0},{10,2},{12,4},{14,6},{16,24},{18,... | collective-permute-start | bytes 294920 | tf_op jit(solution)/shard_map/ppermute | solution.py:522
  250.2 12.3 %collective-permute-start.26 = (bf16[128,384]{1,0:T(8,128)(2,1)S(1)}, bf16[128,384]{1,0:T(8,128)(2,1)S(1)}, u32[]{:S(2)}, u32[]{:S(2)}) collective-permute-start(bf16[128,384]{1,0:T(8,128)(2,1)S(1)} %get-tuple-element.168.refs_18_), channel_id=1, source_target_pairs={{0,24},{2,26},{4,28},{6,30},{8,16},{10,18},{12,20},{14,22},{16,8},... | collective-permute-start | bytes 294920 | tf_op jit(solution)/shard_map/ppermute | solution.py:522
  (5 other events, 20.8 us)

commit v3 on v2

--- a/solution.py
+++ b/solution.py
@@ -633,7 +633,7 @@
         outs + [sds(x.shape, x.dtype) for x in through],
         nbytes=sum(x.size * 2 for x in ins),
         vmem=30,
-        free=tuple(received),
+        free=tuple(range(1, 1 + len(ins))),
         after=after,
         aliases={1 + len(ins) + i: len(outs) + i for i in range(len(through))},
     )(meta, *ins, *through)
@@ -797,7 +797,7 @@
     mix_rows = pl.BlockSpec((1, tile, width), lambda i, m: (mix_at(i) // per, mix_at(i) % per, 0))
     unit_rows = pl.BlockSpec((fb, half_w), lambda i, m: (unit_at(i, m), 0))
     hidden, g, low, back_send, back_keep, in_send, in_keep, d_normed2 = call(
-        functools.partial(ffn_kernel, mixes=mixes, chunk=min(512, th)),
+        functools.partial(ffn_kernel, mixes=mixes, chunk=th),
         (mixes + nf,),
         [
             mix_rows,
@@ -867,7 +867,7 @@
         [tok, tok, small, sds((width, half_w), BF), sds((width, half_w), BF)],
         scratch=[pltpu.VMEM((width, width), F32), pltpu.VMEM((8, width), F32)],
         free=(5,),
-        vmem=44,
+        vmem=34,
         flops=dense * (ff + 2 * width),
         nbytes=2 * tokens * ff,
         after=hold,
@@ -965,7 +965,7 @@
             + [of_part(width), of_part(width), whole((1, width))],
             [pl.BlockSpec((tile, width), lambda i, m: (i, 0))] if part else own,
             [sds((th, width), BF)] if part else [sds(all_a, BF), sds(all_b, BF)],
-            vmem=28,
+            vmem=24,
             free=(10, 11, 12),
             flops=3 * dense * width // 2,
             nbytes=7 * tokens * width,
@@ -990,7 +990,7 @@
         [out_rows(ff), whole((ff, width)), out_rows(width)],
         [pl.BlockSpec((tile, width), lambda i, m: (jnp.minimum(i, per - 1), 0)), of_core(shape_a), of_core(shape_b)],
         [sds((th, width), BF), sds(all_a, BF), sds(all_b, BF)],
-        vmem=34,
+        vmem=30,
         free=(2,),
         flops=dense * ff,
         nbytes=2 * tokens * ff,

time: 273 us -> 269 us (0.985)
  Pallas kernels: 238 us -> 232 us
    pallas_call x19, Pallas kernels: 238 us -> 232 us  [call(): made(*(place(i, x) for i, x in enumerate((*args, *after))))]
  transfers between devices with their start and end apart: 27 -> 27, of which waited for: 1 -> 1; matrix products, arithmetic and copies ran while one was open for 1% -> 1% of each run, Pallas kernels for 58% -> 57%
where the time goes in v3:
time: 269 us; the launch traced here: 264 us
  Pallas kernels  232 us (86%)
  starting transfers between devices  25.4 us (9%)
  local copies, waits for them, and re-layouts  4.97 us (2%)
    pallas_call x19, Pallas kernels, call(): made(*(place(i, x) for i, x in enumerate((*args, *after))))  232 us
    ppermute x27, starting transfers between devices, swap(): return lax.ppermute(x, axis, [(i, i ^ bit) for i in range(n)])  25.4 us
  transfers between devices with their start and end apart: 27, of which 1 were waited for; matrix products, arithmetic and copies ran while one was open for 1% of the time, Pallas kernels for 57%

profile of v3, /device:TPU:0, one launch (start us, length us, event | category | flops | bytes accessed | tf_op | source)
XLA Modules:
  0.0 264.1 jit_solution(14664618418869288103)
XLA Ops:
  0.6 0.8 concatenate.3.meta
  1.4 3.4 %shard_map.246 = (bf16[1024,768]{1,0:T(8,128)(2,1)}, bf16[1024,768]{1,0:T(8,128)(2,1)}) custom-call(s32[16]{0:T(128)S(1)} %concatenate.3.meta, bf16[4,256,768]{2,1,0:T(8,128)(2,1)} %refs_0_.3, bf16[8,128,768]{2,1,0:T(8,128)(2,1)} %refs_1_.4, bf16[4,256,768]{2,1,0:T(8,128)(2,1)} %refs_4_.4, bf16[8,128,768]{2,1,0:T(8,128)(2,1)} %refs_5_.3), custom_call_target="tpu_custom_call" | custom-call | bytes 6291456 | tf_op jit(solution)/shard_map/pallas_call | solution.py:67
  5.7 3.9 %shard_map.247.refs_7_.refs_3_ = f32[12,896,128]{2,1,0:T(8,128)} custom-call(s32[16]{0:T(128)S(1)} %concatenate.3.meta, f32[3,8,128]{2,1,0:T(8,128)S(1)} %pad.4.refs_0_, f32[256,128]{1,0:T(8,128)S(1)} %fusion.1.refs_1_.refs_14_), custom_call_target="tpu_custom_call" | custom-call | bytes 5505024 | tf_op jit(solution)/shard_map/pallas_call | solution.py:67
  10.1 12.3 %shard_map.248 = (bf16[2,1024,768]{2,1,0:T(8,128)(2,1)}, bf16[2,1024,768]{2,1,0:T(8,128)(2,1)}, bf16[2,1024,768]{2,1,0:T(8,128)(2,1)}, bf16[2,1024,768]{2,1,0:T(8,128)(2,1)}, bf16[2,1024,768]{2,1,0:T(8,128)(2,1)}) custom-call(s32[16]{0:T(128)S(1)} %concatenate.3.meta, bf16[4,256,768]{2,1,0:T(8,128)(2,1)} %refs_0_.3, bf16[8,128,768]{2,1,0:T(8,128)(2,1)} %refs_1_.4, ...), custom_call_target="tpu_custom_call" | custom-call | flops 7247757312 | bytes 15728640 | tf_op jit(solution)/shard_map/pallas_call | solution.py:67
  22.4 21.2 %shard_map.249 = (bf16[12,2,512,512]{3,2,1,0:T(8,128)(2,1)}, bf16[12,4,256,256]{3,2,1,0:T(8,128)(2,1)}, bf16[2,1024,768]{2,1,0:T(8,128)(2,1)}, bf16[2,1024,768]{2,1,0:T(8,128)(2,1)}) custom-call(s32[16]{0:T(128)S(1)} %concatenate.3.meta, bf16[2,1024,768]{2,1,0:T(8,128)(2,1)} %get-tuple-element.99.refs_0_, bf16[2,1024,768]{2,1,0:T(8,128)(2,1)} %get-tuple-element.100.refs_1_, ...), custom_call_target="tpu_custom_call" | custom-call | flops 9663676416 | bytes 18874368 | tf_op jit(solution)/shard_map/pallas_call | solution.py:67
  43.6 73.9 %shard_map.250 = (bf16[2,1024,768]{2,1,0:T(8,128)(2,1)}, bf16[2,1024,768]{2,1,0:T(8,128)(2,1)}, bf16[2,1024,3072]{2,1,0:T(8,128)(2,1)}, bf16[3072,384]{1,0:T(8,1...) custom-call(s32[16]{0:T(128)S(1)} %concatenate.3.meta, ...), custom_call_target="tpu_custom_call" | custom-call | flops 50734301184 | bytes 12582912 | tf_op jit(solution)/shard_map/pallas_call | solution.py:67
  118.0 14.0 %shard_map.251 = (bf16[2,1024,768]{2,1,0:T(8,128)(2,1)}, bf16[2,1024,768]{2,1,0:T(8,128)(2,1)}, f32[16,384]{1,0:T(8,128)S(1)}, bf16[768,384]{1,0:T(8,128)(2,1)S(1)}, bf16[768,384]{1,0:T(8,128)(2,1)S(1)}) custom-call(s32[16]{0:T(128)S(1)} %concatenate.3.meta, bf16[2,1024,768]{2,1,0:T(8,128)(2,1)} %get-tuple-element.109.refs_0_, ...), custom_call_target="tpu_custom_call" | custom-call | flops 14495514624 | bytes 12582912 | tf_op jit(solution)/shard_map/pallas_call | solution.py:67
  132.4 3.2 %shard_map.252 = (bf16[3072,384]{1,0:T(8,128)(2,1)}, bf16[1536,384]{1,0:T(8,128)(2,1)}, bf16[1536,384]{1,0:T(8,128)(2,1)}) custom-call(s32[16]{0:T(128)S(1)} %concatenate.3.meta, bf16[2,2,2,2,192,384]{5,4,3,2,1,0:T(8,128)(2,1)S(1)} %bitcast.19, bf16[2,2,2,2,192,384]{5,4,3,2,1,0:T(8,128)(2,1)S(1)} %bitcast.17, bf16[2,2,2,2,48,1536]{5,4,3,2,1,0:T(8,128)(2,1)S(1)} %bitcast.20, ...), custom_call_target="tpu_custom_call" | custom-call | bytes 9437184 | tf_op jit(solution)/shard_map/pallas_call | solution.py:67
  135.6 2.6 collective-permute-start.4
  138.2 1.5 collective-permute-start.5
  139.7 19.1 %shard_map.253 = (bf16[2,1024,256]{2,1,0:T(8,128)(2,1)}, bf16[2,1024,256]{2,1,0:T(8,128)(2,1)}, bf16[2,1024,256]{2,1,0:T(8,128)(2,1)}, bf16[768,384]{1,0:T(8,128...) custom-call(s32[16]{0:T(128)S(1)} %concatenate.3.meta, ...), custom_call_target="tpu_custom_call" | custom-call | flops 8858370048 | bytes 6291456 | tf_op jit(solution)/shard_map/pallas_call | solution.py:67
  158.8 19.3 %shard_map.254 = (bf16[2,1024,256]{2,1,0:T(8,128)(2,1)}, bf16[2,1024,256]{2,1,0:T(8,128)(2,1)}, bf16[2,1024,256]{2,1,0:T(8,128)(2,1)}, bf16[768,384]{1,0:T(8,128...) custom-call(s32[16]{0:T(128)S(1)} %concatenate.3.meta, ...), custom_call_target="tpu_custom_call" | custom-call | flops 8858370048 | bytes 6291456 | tf_op jit(solution)/shard_map/pallas_call | solution.py:67
  178.6 2.4 shard_map.255
  181.6 2.1 collective-permute-start.9
  183.7 19.9 %shard_map.256 = (bf16[2,1024,256]{2,1,0:T(8,128)(2,1)}, bf16[2,1024,256]{2,1,0:T(8,128)(2,1)}, bf16[2,1024,256]{2,1,0:T(8,128)(2,1)}, bf16[768,384]{1,0:T(8,128...) custom-call(s32[16]{0:T(128)S(1)} %concatenate.3.meta, ...), custom_call_target="tpu_custom_call" | custom-call | flops 8858370048 | bytes 6291456 | tf_op jit(solution)/shard_map/pallas_call | solution.py:67
  204.1 1.0 shard_map.257
  205.2 1.9 collective-permute-start.12
  207.1 1.5 collective-permute-start.13
  208.6 8.3 %shard_map.258.refs_10_.refs_9_.refs_7_ = bf16[1024,768]{1,0:T(8,128)(2,1)} custom-call(s32[16]{0:T(128)S(1)} %concatenate.3.meta, bf16[2,1024,256]{2,1,0:T(8,128)(2,1)} %get-tuple-element.144.refs_0_, bf16[2,1024,256]{2,1,0:T(8,128)(2,1)} %get-tuple-element.127.refs_7_.refs_1_, bf16[2,1024,256]{2,1,0:T(8,128)(2,1)} %get-tuple-element.135.refs_4_.refs_2_, ...), custom_call_target="tpu_custom_call" | custom-call | flops 3623878656 | bytes 11010048 | tf_op jit(solution)/shard_map/pallas_call | solution.py:67
  217.0 1.1 shard_map.259
  218.0 0.6 collective-permute-start.18
  218.8 2.8 %collective-permute-start.20 = (bf16[416,384]{1,0:T(8,128)(2,1)S(1)}, bf16[416,384]{1,0:T(8,128)(2,1)S(1)}, u32[]{:S(2)}, u32[]{:S(2)}) collective-permute-start(bf16[416,384]{1,0:T(8,128)(2,1)S(1)} %get-tuple-element.156.refs_8_), channel_id=1, source_target_pairs={{0,6},{2,4},{4,2},{6,0},{8,14},{10,12},{12,10},{14,8},{16,22},{18,... | collective-permute-start | bytes 958472 | tf_op jit(solution)/shard_map/ppermute | solution.py:522
  221.6 2.6 collective-permute-start.21
  224.2 1.6 collective-permute-start.17
  225.8 2.3 copy-done.8
  228.1 15.1 %shard_map.260 = (bf16[1024,768]{1,0:T(8,128)(2,1)}, bf16[4,256,768]{2,1,0:T(8,128)(2,1)}, bf16[8,128,768]{2,1,0:T(8,128)(2,1)}) custom-call(s32[16]{0:T(128)S(1)} %concatenate.3.meta, bf16[2,1024,3072]{2,1,0:T(8,128)(2,1)} %get-tuple-element.159.refs_0_, bf16[3072,768]{1,0:T(8,128)(2,1)S(1)} %copy-done.8, ...), custom_call_target="tpu_custom_call" | custom-call | flops 9663676416 | bytes 12582912 | tf_op jit(solution)/shard_map/pallas_call | solution.py:67
  243.3 1.5 shard_map.261
  246.1 3.6 %collective-permute-start.26 = (bf16[128,384]{1,0:T(8,128)(2,1)S(1)}, bf16[128,384]{1,0:T(8,128)(2,1)S(1)}, u32[]{:S(2)}, u32[]{:S(2)}) collective-permute-start(bf16[128,384]{1,0:T(8,128)(2,1)S(1)} %get-tuple-element.168.refs_18_), channel_id=1, source_target_pairs={{0,24},{2,26},{4,28},{6,30},{8,16},{10,18},{12,20},{14,22},{16,8},... | collective-permute-start | bytes 294920 | tf_op jit(solution)/shard_map/ppermute | solution.py:522
  249.7 8.7 %shard_map.262 = (bf16[4,256,768]{2,1,0:T(8,128)(2,1)}, bf16[8,128,768]{2,1,0:T(8,128)(2,1)}) custom-call(s32[16]{0:T(128)S(1)} %concatenate.3.meta, bf16[2,1024,256]{2,1,0:T(8,128)(2,1)} %get-tuple-element.144.refs_0_, bf16[2,1024,256]{2,1,0:T(8,128)(2,1)} %get-tuple-element.127.refs_7_.refs_1_, bf16[2,1024,256]{2,1,0:T(8,128)(2,1)} %get-tuple-element.135.refs_4_.refs_2_, ...), custom_call_target="tpu_custom_call" | custom-call | flops 3623878656 | bytes 11010048 | tf_op jit(solution)/shard_map/pallas_call | solution.py:67
  258.5 1.3 shard_map.264
  259.7 0.6 reshape.121
  261.6 2.3 shard_map.263
  (79 shorter events, 6.5 us)
Async XLA Ops:
  4.8 5.2 %collective-permute-start = (bf16[1024,768]{1,0:T(8,128)(2,1)}, bf16[1024,768]{1,0:T(8,128)(2,1)S(1)}, u32[]{:S(2)}, u32[]{:S(2)}) collective-permute-start(bf16[1024,768]{1,0:T(8,128)(2,1)} %get-tuple-element.98), channel_id=1, source_target_pairs={{0,1},{1,0},{2,3},{3,2},{4,5},{5,4},{6,7},{7,6},{8,9},{9,8},{10,11... | collective-permute-start | bytes 4718600 | tf_op jit(solution)/shard_map/ppermute | solution.py:522
  5.3 38.2 %collective-permute-start.1 = (bf16[1024,768]{1,0:T(8,128)(2,1)}, bf16[1024,768]{1,0:T(8,128)(2,1)}, u32[]{:S(2)}, u32[]{:S(2)}) collective-permute-start(bf16[1024,768]{1,0:T(8,128)(2,1)} %get-tuple-element.104), channel_id=1, source_target_pairs={{0,1},{1,0},{2,3},{3,2},{4,5},{5,4},{6,7},{7,6},{8,9},{9,8},{10,11... | collective-permute-start | bytes 4718600 | tf_op jit(solution)/shard_map/ppermute | solution.py:522
  22.4 21.2 %copy-start.9 = (bf16[768,768]{1,0:T(8,128)(2,1)S(1)}, bf16[768,768]{1,0:T(8,128)(2,1)}, u32[]{:S(2)}) copy-start(bf16[768,768]{1,0:T(8,128)(2,1)} %refs_4_.5) | copy-start | bytes 3538948
  117.5 14.9 %collective-permute-start.2 = (bf16[3072,384]{1,0:T(8,128)(2,1)}, bf16[3072,384]{1,0:T(8,128)(2,1)S(1)}, u32[]{:S(2)}, u32[]{:S(2)}) collective-permute-start(bf16[3072,384]{1,0:T(8,128)(2,1)} %get-tuple-element.105.refs_7_), channel_id=1, source_target_pairs={{0,1},{1,0},{2,3},{3,2},{4,5},{5,4},{6,7},{7,6},{8,9},{9,8},{10,11... | collective-permute-start | bytes 7077896 | tf_op jit(solution)/shard_map/ppermute | solution.py:522
  117.9 14.5 %collective-permute-start.3 = (bf16[768,1536]{1,0:T(8,128)(2,1)}, bf16[768,1536]{1,0:T(8,128)(2,1)S(1)}, u32[]{:S(2)}, u32[]{:S(2)}) collective-permute-start(bf16[768,1536]{1,0:T(8,128)(2,1)} %get-tuple-element.107.refs_8_), channel_id=1, source_target_pairs={{0,1},{1,0},{2,3},{3,2},{4,5},{5,4},{6,7},{7,6},{8,9},{9,8},{10,11... | collective-permute-start | bytes 7077896 | tf_op jit(solution)/shard_map/ppermute | solution.py:522
  118.0 14.4 %copy-start.6 = (bf16[3072,384]{1,0:T(8,128)(2,1)S(1)}, bf16[3072,384]{1,0:T(8,128)(2,1)}, u32[]{:S(2)}) copy-start(bf16[3072,384]{1,0:T(8,128)(2,1)} %get-tuple-element.106) | copy-start | bytes 7077892
  118.0 14.4 %copy-start.7 = (bf16[768,1536]{1,0:T(8,128)(2,1)S(1)}, bf16[768,1536]{1,0:T(8,128)(2,1)}, u32[]{:S(2)}) copy-start(bf16[768,1536]{1,0:T(8,128)(2,1)} %get-tuple-element.108) | copy-start | bytes 7077892
  132.0 46.6 %collective-permute-start.6 = (bf16[768,384]{1,0:T(8,128)(2,1)S(1)}, bf16[768,384]{1,0:T(8,128)(2,1)S(1)}, u32[]{:S(2)}, u32[]{:S(2)}) collective-permute-start(bf16[768,384]{1,0:T(8,128)(2,1)S(1)} %get-tuple-element.117.refs_20_), channel_id=1, source_target_pairs={{0,1},{1,0},{2,3},{3,2},{4,5},{5,4},{6,7},{7,6},{8,9},{9,8},{10,11... | collective-permute-start | bytes 1769480 | tf_op jit(solution)/shard_map/ppermute | solution.py:522
  135.6 43.0 %collective-permute-start.4 = (bf16[1536,384]{1,0:T(8,128)(2,1)}, bf16[1536,384]{1,0:T(8,128)(2,1)S(1)}, u32[]{:S(2)}, u32[]{:S(2)}) collective-permute-start(bf16[1536,384]{1,0:T(8,128)(2,1)} %get-tuple-element.114.refs_18_), channel_id=1, source_target_pairs={{0,2},{2,0},{4,6},{6,4},{8,10},{10,8},{12,14},{14,12},{16,18},{18,... | collective-permute-start | bytes 3538952 | tf_op jit(solution)/shard_map/ppermute | solution.py:522
  138.2 40.4 %collective-permute-start.5 = (bf16[1536,384]{1,0:T(8,128)(2,1)}, bf16[1536,384]{1,0:T(8,128)(2,1)S(1)}, u32[]{:S(2)}, u32[]{:S(2)}) collective-permute-start(bf16[1536,384]{1,0:T(8,128)(2,1)} %get-tuple-element.116.refs_19_), channel_id=1, source_target_pairs={{0,4},{2,6},{4,0},{6,2},{8,12},{10,14},{12,8},{14,10},{16,20},{18,... | collective-permute-start | bytes 3538952 | tf_op jit(solution)/shard_map/ppermute | solution.py:522
  158.8 19.8 %collective-permute-start.7 = (bf16[768,384]{1,0:T(8,128)(2,1)S(1)}, bf16[768,384]{1,0:T(8,128)(2,1)S(1)}, u32[]{:S(2)}, u32[]{:S(2)}) collective-permute-start(bf16[768,384]{1,0:T(8,128)(2,1)S(1)} %get-tuple-element.122.refs_18_), channel_id=1, source_target_pairs={{0,1},{1,0},{2,3},{3,2},{4,5},{5,4},{6,7},{7,6},{8,9},{9,8},{10,11... | collective-permute-start | bytes 1769480 | tf_op jit(solution)/shard_map/ppermute | solution.py:522
  158.8 19.8 %copy-start.4 = (bf16[3072,384]{1,0:T(8,128)(2,1)S(1)}, bf16[3072,384]{1,0:T(8,128)(2,1)}, u32[]{:S(2)}) copy-start(bf16[3072,384]{1,0:T(8,128)(2,1)} %get-tuple-element.115.refs_17_.refs_1_) | copy-start | bytes 7077892
  178.1 29.0 %collective-permute-start.14 = (bf16[768,384]{1,0:T(8,128)(2,1)S(1)}, bf16[768,384]{1,0:T(8,128)(2,1)S(1)}, u32[]{:S(2)}, u32[]{:S(2)}) collective-permute-start(bf16[768,384]{1,0:T(8,128)(2,1)S(1)} %get-tuple-element.134.refs_22_), channel_id=1, source_target_pairs={{0,1},{1,0},{2,3},{3,2},{4,5},{5,4},{6,7},{7,6},{8,9},{9,8},{10,11... | collective-permute-start | bytes 1769480 | tf_op jit(solution)/shard_map/ppermute | solution.py:522
  181.0 22.6 %collective-permute-start.10 = (bf16[768,384]{1,0:T(8,128)(2,1)S(1)}, bf16[768,384]{1,0:T(8,128)(2,1)S(1)}, u32[]{:S(2)}, u32[]{:S(2)}) collective-permute-start(bf16[768,384]{1,0:T(8,128)(2,1)S(1)} %get-tuple-element.131.refs_21_), channel_id=1, source_target_pairs={{0,2},{2,0},{4,6},{6,4},{8,10},{10,8},{12,14},{14,12},{16,18},{18,... | collective-permute-start | bytes 1769480 | tf_op jit(solution)/shard_map/ppermute | solution.py:522
  181.6 22.5 %collective-permute-start.8 = (bf16[768,384]{1,0:T(8,128)(2,1)S(1)}, bf16[768,384]{1,0:T(8,128)(2,1)S(1)}, u32[]{:S(2)}, u32[]{:S(2)}) collective-permute-start(bf16[768,384]{1,0:T(8,128)(2,1)S(1)} %get-tuple-element.128.refs_19_), channel_id=1, source_target_pairs={{0,4},{2,6},{4,0},{6,2},{8,12},{10,14},{12,8},{14,10},{16,20},{18,... | collective-permute-start | bytes 1769480 | tf_op jit(solution)/shard_map/ppermute | solution.py:522
  181.6 22.5 %collective-permute-start.9 = (bf16[768,384]{1,0:T(8,128)(2,1)S(1)}, bf16[768,384]{1,0:T(8,128)(2,1)S(1)}, u32[]{:S(2)}, u32[]{:S(2)}) collective-permute-start(bf16[768,384]{1,0:T(8,128)(2,1)S(1)} %get-tuple-element.130.refs_20_), channel_id=1, source_target_pairs={{0,8},{2,10},{4,12},{6,14},{8,0},{10,2},{12,4},{14,6},{16,24},{18,... | collective-permute-start | bytes 1769480 | tf_op jit(solution)/shard_map/ppermute | solution.py:522
  183.7 20.4 %copy-start.5 = (bf16[2304,384]{1,0:T(8,128)(2,1)S(1)}, bf16[2304,384]{1,0:T(8,128)(2,1)}, u32[]{:S(2)}) copy-start(bf16[2304,384]{1,0:T(8,128)(2,1)} %get-tuple-element.129.refs_18_.refs_1_) | copy-start | bytes 5308420
  203.6 13.3 %collective-permute-start.15 = (bf16[768,384]{1,0:T(8,128)(2,1)S(1)}, bf16[768,384]{1,0:T(8,128)(2,1)S(1)}, u32[]{:S(2)}, u32[]{:S(2)}) collective-permute-start(bf16[768,384]{1,0:T(8,128)(2,1)S(1)} %get-tuple-element.140.refs_19_), channel_id=1, source_target_pairs={{0,1},{1,0},{2,3},{3,2},{4,5},{5,4},{6,7},{7,6},{8,9},{9,8},{10,11... | collective-permute-start | bytes 1769480 | tf_op jit(solution)/shard_map/ppermute | solution.py:522
  203.6 13.3 %collective-permute-start.16 = (f32[16,384]{1,0:T(8,128)S(1)}, f32[16,384]{1,0:T(8,128)S(1)}, u32[]{:S(2)}, u32[]{:S(2)}) collective-permute-start(f32[16,384]{1,0:T(8,128)S(1)} %get-tuple-element.143.refs_20_.refs_8_), channel_id=1, source_target_pairs={{0,1},{1,0},{2,3},{3,2},{4,5},{5,4},{6,7},{7,6},{8,9},{9,8},{10,11... | collective-permute-start | bytes 73736 | tf_op jit(solution)/shard_map/ppermute | solution.py:522
  205.1 11.8 %collective-permute-start.11 = (bf16[384,384]{1,0:T(8,128)(2,1)S(1)}, bf16[384,384]{1,0:T(8,128)(2,1)S(1)}, u32[]{:S(2)}, u32[]{:S(2)}) collective-permute-start(bf16[384,384]{1,0:T(8,128)(2,1)S(1)} %get-tuple-element.136.refs_16_), channel_id=1, source_target_pairs={{0,8},{2,10},{4,12},{6,14},{8,0},{10,2},{12,4},{14,6},{16,24},{18,... | collective-permute-start | bytes 884744 | tf_op jit(solution)/shard_map/ppermute | solution.py:522
  205.2 11.8 %collective-permute-start.12 = (bf16[384,384]{1,0:T(8,128)(2,1)S(1)}, bf16[384,384]{1,0:T(8,128)(2,1)S(1)}, u32[]{:S(2)}, u32[]{:S(2)}) collective-permute-start(bf16[384,384]{1,0:T(8,128)(2,1)S(1)} %get-tuple-element.138.refs_17_), channel_id=1, source_target_pairs={{0,2},{2,0},{4,6},{6,4},{8,10},{10,8},{12,14},{14,12},{16,18},{18,... | collective-permute-start | bytes 884744 | tf_op jit(solution)/shard_map/ppermute | solution.py:522
  207.1 9.9 %collective-permute-start.13 = (bf16[384,384]{1,0:T(8,128)(2,1)S(1)}, bf16[384,384]{1,0:T(8,128)(2,1)S(1)}, u32[]{:S(2)}, u32[]{:S(2)}) collective-permute-start(bf16[384,384]{1,0:T(8,128)(2,1)S(1)} %get-tuple-element.139.refs_18_), channel_id=1, source_target_pairs={{0,4},{2,6},{4,0},{6,2},{8,12},{10,14},{12,8},{14,10},{16,20},{18,... | collective-permute-start | bytes 884744 | tf_op jit(solution)/shard_map/ppermute | solution.py:522
  218.0 25.2 %collective-permute-start.18 = (bf16[416,384]{1,0:T(8,128)(2,1)S(1)}, bf16[416,384]{1,0:T(8,128)(2,1)S(1)}, u32[]{:S(2)}, u32[]{:S(2)}) collective-permute-start(bf16[416,384]{1,0:T(8,128)(2,1)S(1)} %get-tuple-element.154.refs_6_), channel_id=1, source_target_pairs={{0,2},{2,0},{4,6},{6,4},{8,10},{10,8},{12,14},{14,12},{16,18},{18,... | collective-permute-start | bytes 958472 | tf_op jit(solution)/shard_map/ppermute | solution.py:522
  218.7 24.6 %collective-permute-start.19 = (bf16[416,384]{1,0:T(8,128)(2,1)S(1)}, bf16[416,384]{1,0:T(8,128)(2,1)S(1)}, u32[]{:S(2)}, u32[]{:S(2)}) collective-permute-start(bf16[416,384]{1,0:T(8,128)(2,1)S(1)} %get-tuple-element.155.refs_7_), channel_id=1, source_target_pairs={{0,4},{2,6},{4,0},{6,2},{8,12},{10,14},{12,8},{14,10},{16,20},{18,... | collective-permute-start | bytes 958472 | tf_op jit(solution)/shard_map/ppermute | solution.py:522
  218.8 24.5 %collective-permute-start.20 = (bf16[416,384]{1,0:T(8,128)(2,1)S(1)}, bf16[416,384]{1,0:T(8,128)(2,1)S(1)}, u32[]{:S(2)}, u32[]{:S(2)}) collective-permute-start(bf16[416,384]{1,0:T(8,128)(2,1)S(1)} %get-tuple-element.156.refs_8_), channel_id=1, source_target_pairs={{0,6},{2,4},{4,2},{6,0},{8,14},{10,12},{12,10},{14,8},{16,22},{18,... | collective-permute-start | bytes 958472 | tf_op jit(solution)/shard_map/ppermute | solution.py:522
  221.6 21.7 %collective-permute-start.21 = (bf16[384,384]{1,0:T(8,128)(2,1)S(1)}, bf16[384,384]{1,0:T(8,128)(2,1)S(1)}, u32[]{:S(2)}, u32[]{:S(2)}) collective-permute-start(bf16[384,384]{1,0:T(8,128)(2,1)S(1)} %get-tuple-element.157.refs_4_), channel_id=1, source_target_pairs={{0,16},{2,18},{4,20},{6,22},{8,24},{10,26},{12,28},{14,30},{16,0},... | collective-permute-start | bytes 884744 | tf_op jit(solution)/shard_map/ppermute | solution.py:522
  224.2 19.0 %collective-permute-start.17 = (bf16[192,384]{1,0:T(8,128)(2,1)S(1)}, bf16[192,384]{1,0:T(8,128)(2,1)S(1)}, u32[]{:S(2)}, u32[]{:S(2)}) collective-permute-start(bf16[192,384]{1,0:T(8,128)(2,1)S(1)} %get-tuple-element.152.refs_5_), channel_id=1, source_target_pairs={{0,8},{2,10},{4,12},{6,14},{8,0},{10,2},{12,4},{14,6},{16,24},{18,... | collective-permute-start | bytes 442376 | tf_op jit(solution)/shard_map/ppermute | solution.py:522
  244.8 16.7 %collective-permute-start.22 = (bf16[1024,768]{1,0:T(8,128)(2,1)}, bf16[1024,768]{1,0:T(8,128)(2,1)S(1)}, u32[]{:S(2)}, u32[]{:S(2)}) collective-permute-start(bf16[1024,768]{1,0:T(8,128)(2,1)} %get-tuple-element.161.refs_20_), channel_id=1, source_target_pairs={{0,1},{1,0},{2,3},{3,2},{4,5},{5,4},{6,7},{7,6},{8,9},{9,8},{10,11... | collective-permute-start | bytes 4718600 | tf_op jit(solution)/shard_map/ppermute | solution.py:522
  244.8 16.7 %collective-permute-start.23 = (bf16[1024,768]{1,0:T(8,128)(2,1)}, bf16[1024,768]{1,0:T(8,128)(2,1)S(1)}, u32[]{:S(2)}, u32[]{:S(2)}) collective-permute-start(bf16[1024,768]{1,0:T(8,128)(2,1)} %get-tuple-element.162.refs_19_), channel_id=1, source_target_pairs={{0,1},{1,0},{2,3},{3,2},{4,5},{5,4},{6,7},{7,6},{8,9},{9,8},{10,11... | collective-permute-start | bytes 4718600 | tf_op jit(solution)/shard_map/ppermute | solution.py:522
  245.3 13.1 %collective-permute-start.24 = (bf16[224,384]{1,0:T(8,128)(2,1)S(1)}, bf16[224,384]{1,0:T(8,128)(2,1)S(1)}, u32[]{:S(2)}, u32[]{:S(2)}) collective-permute-start(bf16[224,384]{1,0:T(8,128)(2,1)S(1)} %get-tuple-element.166.refs_16_), channel_id=1, source_target_pairs={{0,16},{2,18},{4,20},{6,22},{8,24},{10,26},{12,28},{14,30},{16,0},... | collective-permute-start | bytes 516104 | tf_op jit(solution)/shard_map/ppermute | solution.py:522
  245.7 12.8 %collective-permute-start.25 = (bf16[128,384]{1,0:T(8,128)(2,1)S(1)}, bf16[128,384]{1,0:T(8,128)(2,1)S(1)}, u32[]{:S(2)}, u32[]{:S(2)}) collective-permute-start(bf16[128,384]{1,0:T(8,128)(2,1)S(1)} %get-tuple-element.167.refs_17_), channel_id=1, source_target_pairs={{0,8},{2,10},{4,12},{6,14},{8,0},{10,2},{12,4},{14,6},{16,24},{18,... | collective-permute-start | bytes 294920 | tf_op jit(solution)/shard_map/ppermute | solution.py:522
  246.1 12.3 %collective-permute-start.26 = (bf16[128,384]{1,0:T(8,128)(2,1)S(1)}, bf16[128,384]{1,0:T(8,128)(2,1)S(1)}, u32[]{:S(2)}, u32[]{:S(2)}) collective-permute-start(bf16[128,384]{1,0:T(8,128)(2,1)S(1)} %get-tuple-element.168.refs_18_), channel_id=1, source_target_pairs={{0,24},{2,26},{4,28},{6,30},{8,16},{10,18},{12,20},{14,22},{16,8},... | collective-permute-start | bytes 294920 | tf_op jit(solution)/shard_map/ppermute | solution.py:522
  (8 other events, 34.9 us)

commit v4 on v3

--- a/solution.py
+++ b/solution.py
@@ -991,7 +991,6 @@
         [pl.BlockSpec((tile, width), lambda i, m: (jnp.minimum(i, per - 1), 0)), of_core(shape_a), of_core(shape_b)],
         [sds((th, width), BF), sds(all_a, BF), sds(all_b, BF)],
         vmem=30,
-        free=(2,),
         flops=dense * ff,
         nbytes=2 * tokens * ff,
         after=hold,

time: 269 us -> 268 us (level)
  no operation moved by 1% of the time
where the time goes in v4:
time: 268 us; the launch traced here: 263 us
  Pallas kernels  233 us (87%)
  starting transfers between devices  25.4 us (9%)
    pallas_call x19, Pallas kernels, call(): made(*(place(i, x) for i, x in enumerate((*args, *after))))  233 us
    ppermute x27, starting transfers between devices, swap(): return lax.ppermute(x, axis, [(i, i ^ bit) for i in range(n)])  25.4 us
  transfers between devices with their start and end apart: 27, of which 1 were waited for; matrix products, arithmetic and copies ran while one was open for 1% of the time, Pallas kernels for 57%

profile of v4, /device:TPU:0, one launch (start us, length us, event | category | flops | bytes accessed | tf_op | source)
XLA Modules:
  0.0 263.2 jit_solution(13809697049266267379)
XLA Ops:
  0.6 0.8 concatenate.3.meta
  1.4 3.4 %shard_map.246 = (bf16[1024,768]{1,0:T(8,128)(2,1)}, bf16[1024,768]{1,0:T(8,128)(2,1)}) custom-call(s32[16]{0:T(128)S(1)} %concatenate.3.meta, bf16[4,256,768]{2,1,0:T(8,128)(2,1)} %refs_0_.3, bf16[8,128,768]{2,1,0:T(8,128)(2,1)} %refs_1_.4, bf16[4,256,768]{2,1,0:T(8,128)(2,1)} %refs_4_.4, bf16[8,128,768]{2,1,0:T(8,128)(2,1)} %refs_5_.3), custom_call_target="tpu_custom_call" | custom-call | bytes 6291456 | tf_op jit(solution)/shard_map/pallas_call | solution.py:67
  5.7 3.9 %shard_map.247.refs_7_.refs_3_ = f32[12,896,128]{2,1,0:T(8,128)} custom-call(s32[16]{0:T(128)S(1)} %concatenate.3.meta, f32[3,8,128]{2,1,0:T(8,128)S(1)} %pad.4.refs_0_, f32[256,128]{1,0:T(8,128)S(1)} %fusion.1.refs_1_.refs_14_), custom_call_target="tpu_custom_call" | custom-call | bytes 5505024 | tf_op jit(solution)/shard_map/pallas_call | solution.py:67
  10.1 12.3 %shard_map.248 = (bf16[2,1024,768]{2,1,0:T(8,128)(2,1)}, bf16[2,1024,768]{2,1,0:T(8,128)(2,1)}, bf16[2,1024,768]{2,1,0:T(8,128)(2,1)}, bf16[2,1024,768]{2,1,0:T(8,128)(2,1)}, bf16[2,1024,768]{2,1,0:T(8,128)(2,1)}) custom-call(s32[16]{0:T(128)S(1)} %concatenate.3.meta, bf16[4,256,768]{2,1,0:T(8,128)(2,1)} %refs_0_.3, bf16[8,128,768]{2,1,0:T(8,128)(2,1)} %refs_1_.4, ...), custom_call_target="tpu_custom_call" | custom-call | flops 7247757312 | bytes 15728640 | tf_op jit(solution)/shard_map/pallas_call | solution.py:67
  22.3 21.3 %shard_map.249 = (bf16[12,2,512,512]{3,2,1,0:T(8,128)(2,1)}, bf16[12,4,256,256]{3,2,1,0:T(8,128)(2,1)}, bf16[2,1024,768]{2,1,0:T(8,128)(2,1)}, bf16[2,1024,768]{2,1,0:T(8,128)(2,1)}) custom-call(s32[16]{0:T(128)S(1)} %concatenate.3.meta, bf16[2,1024,768]{2,1,0:T(8,128)(2,1)} %get-tuple-element.99.refs_0_, bf16[2,1024,768]{2,1,0:T(8,128)(2,1)} %get-tuple-element.100.refs_1_, ...), custom_call_target="tpu_custom_call" | custom-call | flops 9663676416 | bytes 18874368 | tf_op jit(solution)/shard_map/pallas_call | solution.py:67
  43.6 73.9 %shard_map.250 = (bf16[2,1024,768]{2,1,0:T(8,128)(2,1)}, bf16[2,1024,768]{2,1,0:T(8,128)(2,1)}, bf16[2,1024,3072]{2,1,0:T(8,128)(2,1)}, bf16[3072,384]{1,0:T(8,1...) custom-call(s32[16]{0:T(128)S(1)} %concatenate.3.meta, ...), custom_call_target="tpu_custom_call" | custom-call | flops 50734301184 | bytes 12582912 | tf_op jit(solution)/shard_map/pallas_call | solution.py:67
  118.1 14.0 %shard_map.251 = (bf16[2,1024,768]{2,1,0:T(8,128)(2,1)}, bf16[2,1024,768]{2,1,0:T(8,128)(2,1)}, f32[16,384]{1,0:T(8,128)S(1)}, bf16[768,384]{1,0:T(8,128)(2,1)S(1)}, bf16[768,384]{1,0:T(8,128)(2,1)S(1)}) custom-call(s32[16]{0:T(128)S(1)} %concatenate.3.meta, bf16[2,1024,768]{2,1,0:T(8,128)(2,1)} %get-tuple-element.109.refs_0_, ...), custom_call_target="tpu_custom_call" | custom-call | flops 14495514624 | bytes 12582912 | tf_op jit(solution)/shard_map/pallas_call | solution.py:67
  132.3 3.2 %shard_map.252 = (bf16[3072,384]{1,0:T(8,128)(2,1)}, bf16[1536,384]{1,0:T(8,128)(2,1)}, bf16[1536,384]{1,0:T(8,128)(2,1)}) custom-call(s32[16]{0:T(128)S(1)} %concatenate.3.meta, bf16[2,2,2,2,192,384]{5,4,3,2,1,0:T(8,128)(2,1)S(1)} %bitcast.19, bf16[2,2,2,2,192,384]{5,4,3,2,1,0:T(8,128)(2,1)S(1)} %bitcast.17, bf16[2,2,2,2,48,1536]{5,4,3,2,1,0:T(8,128)(2,1)S(1)} %bitcast.20, ...), custom_call_target="tpu_custom_call" | custom-call | bytes 9437184 | tf_op jit(solution)/shard_map/pallas_call | solution.py:67
  135.5 2.7 %collective-permute-start.4 = (bf16[1536,384]{1,0:T(8,128)(2,1)}, bf16[1536,384]{1,0:T(8,128)(2,1)S(1)}, u32[]{:S(2)}, u32[]{:S(2)}) collective-permute-start(bf16[1536,384]{1,0:T(8,128)(2,1)} %get-tuple-element.114.refs_18_), channel_id=1, source_target_pairs={{0,2},{2,0},{4,6},{6,4},{8,10},{10,8},{12,14},{14,12},{16,18},{18,... | collective-permute-start | bytes 3538952 | tf_op jit(solution)/shard_map/ppermute | solution.py:522
  138.2 1.5 collective-permute-start.5
  139.7 19.1 %shard_map.253 = (bf16[2,1024,256]{2,1,0:T(8,128)(2,1)}, bf16[2,1024,256]{2,1,0:T(8,128)(2,1)}, bf16[2,1024,256]{2,1,0:T(8,128)(2,1)}, bf16[768,384]{1,0:T(8,128...) custom-call(s32[16]{0:T(128)S(1)} %concatenate.3.meta, ...), custom_call_target="tpu_custom_call" | custom-call | flops 8858370048 | bytes 6291456 | tf_op jit(solution)/shard_map/pallas_call | solution.py:67
  158.8 19.3 %shard_map.254 = (bf16[2,1024,256]{2,1,0:T(8,128)(2,1)}, bf16[2,1024,256]{2,1,0:T(8,128)(2,1)}, bf16[2,1024,256]{2,1,0:T(8,128)(2,1)}, bf16[768,384]{1,0:T(8,128...) custom-call(s32[16]{0:T(128)S(1)} %concatenate.3.meta, ...), custom_call_target="tpu_custom_call" | custom-call | flops 8858370048 | bytes 6291456 | tf_op jit(solution)/shard_map/pallas_call | solution.py:67
  178.6 2.4 shard_map.255
  181.6 2.1 collective-permute-start.9
  183.7 19.9 %shard_map.256 = (bf16[2,1024,256]{2,1,0:T(8,128)(2,1)}, bf16[2,1024,256]{2,1,0:T(8,128)(2,1)}, bf16[2,1024,256]{2,1,0:T(8,128)(2,1)}, bf16[768,384]{1,0:T(8,128...) custom-call(s32[16]{0:T(128)S(1)} %concatenate.3.meta, ...), custom_call_target="tpu_custom_call" | custom-call | flops 8858370048 | bytes 6291456 | tf_op jit(solution)/shard_map/pallas_call | solution.py:67
  204.1 1.0 shard_map.257
  205.1 1.9 collective-permute-start.12
  207.1 1.5 collective-permute-start.13
  208.6 8.3 %shard_map.258.refs_10_.refs_9_.refs_7_ = bf16[1024,768]{1,0:T(8,128)(2,1)} custom-call(s32[16]{0:T(128)S(1)} %concatenate.3.meta, bf16[2,1024,256]{2,1,0:T(8,128)(2,1)} %get-tuple-element.144.refs_0_, bf16[2,1024,256]{2,1,0:T(8,128)(2,1)} %get-tuple-element.127.refs_7_.refs_1_, bf16[2,1024,256]{2,1,0:T(8,128)(2,1)} %get-tuple-element.135.refs_4_.refs_2_, ...), custom_call_target="tpu_custom_call" | custom-call | flops 3623878656 | bytes 11010048 | tf_op jit(solution)/shard_map/pallas_call | solution.py:67
  217.0 1.1 shard_map.259
  218.8 2.8 %collective-permute-start.20 = (bf16[416,384]{1,0:T(8,128)(2,1)S(1)}, bf16[416,384]{1,0:T(8,128)(2,1)S(1)}, u32[]{:S(2)}, u32[]{:S(2)}) collective-permute-start(bf16[416,384]{1,0:T(8,128)(2,1)S(1)} %get-tuple-element.156.refs_8_), channel_id=1, source_target_pairs={{0,6},{2,4},{4,2},{6,0},{8,14},{10,12},{12,10},{14,8},{16,22},{18,... | collective-permute-start | bytes 958472 | tf_op jit(solution)/shard_map/ppermute | solution.py:522
  221.6 2.6 collective-permute-start.21
  224.2 1.6 collective-permute-start.17
  225.8 16.6 %shard_map.260 = (bf16[1024,768]{1,0:T(8,128)(2,1)}, bf16[4,256,768]{2,1,0:T(8,128)(2,1)}, bf16[8,128,768]{2,1,0:T(8,128)(2,1)}) custom-call(s32[16]{0:T(128)S(1)} %concatenate.3.meta, bf16[2,1024,3072]{2,1,0:T(8,128)(2,1)} %get-tuple-element.159.refs_0_, bf16[3072,768]{1,0:T(8,128)(2,1)} %refs_1_.5, ...), custom_call_target="tpu_custom_call" | custom-call | flops 9663676416 | bytes 12582912 | tf_op jit(solution)/shard_map/pallas_call | solution.py:67
  242.4 1.5 shard_map.261
  245.3 3.6 %collective-permute-start.26 = (bf16[128,384]{1,0:T(8,128)(2,1)S(1)}, bf16[128,384]{1,0:T(8,128)(2,1)S(1)}, u32[]{:S(2)}, u32[]{:S(2)}) collective-permute-start(bf16[128,384]{1,0:T(8,128)(2,1)S(1)} %get-tuple-element.168.refs_18_), channel_id=1, source_target_pairs={{0,24},{2,26},{4,28},{6,30},{8,16},{10,18},{12,20},{14,22},{16,8},... | collective-permute-start | bytes 294920 | tf_op jit(solution)/shard_map/ppermute | solution.py:522
  248.9 8.7 %shard_map.262 = (bf16[4,256,768]{2,1,0:T(8,128)(2,1)}, bf16[8,128,768]{2,1,0:T(8,128)(2,1)}) custom-call(s32[16]{0:T(128)S(1)} %concatenate.3.meta, bf16[2,1024,256]{2,1,0:T(8,128)(2,1)} %get-tuple-element.144.refs_0_, bf16[2,1024,256]{2,1,0:T(8,128)(2,1)} %get-tuple-element.127.refs_7_.refs_1_, bf16[2,1024,256]{2,1,0:T(8,128)(2,1)} %get-tuple-element.135.refs_4_.refs_2_, ...), custom_call_target="tpu_custom_call" | custom-call | flops 3623878656 | bytes 11010048 | tf_op jit(solution)/shard_map/pallas_call | solution.py:67
  257.6 1.3 shard_map.264
  258.9 0.6 reshape.121
  259.5 0.6 reshape.122
  260.1 0.6 slice_bitcast_fusion
  260.7 2.3 shard_map.263
  (77 shorter events, 5.8 us)
Async XLA Ops:
  4.8 5.2 %collective-permute-start = (bf16[1024,768]{1,0:T(8,128)(2,1)}, bf16[1024,768]{1,0:T(8,128)(2,1)S(1)}, u32[]{:S(2)}, u32[]{:S(2)}) collective-permute-start(bf16[1024,768]{1,0:T(8,128)(2,1)} %get-tuple-element.98), channel_id=1, source_target_pairs={{0,1},{1,0},{2,3},{3,2},{4,5},{5,4},{6,7},{7,6},{8,9},{9,8},{10,11... | collective-permute-start | bytes 4718600 | tf_op jit(solution)/shard_map/ppermute | solution.py:522
  5.3 38.3 %collective-permute-start.1 = (bf16[1024,768]{1,0:T(8,128)(2,1)}, bf16[1024,768]{1,0:T(8,128)(2,1)}, u32[]{:S(2)}, u32[]{:S(2)}) collective-permute-start(bf16[1024,768]{1,0:T(8,128)(2,1)} %get-tuple-element.104), channel_id=1, source_target_pairs={{0,1},{1,0},{2,3},{3,2},{4,5},{5,4},{6,7},{7,6},{8,9},{9,8},{10,11... | collective-permute-start | bytes 4718600 | tf_op jit(solution)/shard_map/ppermute | solution.py:522
  22.3 21.3 %copy-start.8 = (bf16[768,768]{1,0:T(8,128)(2,1)S(1)}, bf16[768,768]{1,0:T(8,128)(2,1)}, u32[]{:S(2)}) copy-start(bf16[768,768]{1,0:T(8,128)(2,1)} %refs_4_.5) | copy-start | bytes 3538948
  117.5 14.8 %collective-permute-start.2 = (bf16[3072,384]{1,0:T(8,128)(2,1)}, bf16[3072,384]{1,0:T(8,128)(2,1)S(1)}, u32[]{:S(2)}, u32[]{:S(2)}) collective-permute-start(bf16[3072,384]{1,0:T(8,128)(2,1)} %get-tuple-element.105.refs_7_), channel_id=1, source_target_pairs={{0,1},{1,0},{2,3},{3,2},{4,5},{5,4},{6,7},{7,6},{8,9},{9,8},{10,11... | collective-permute-start | bytes 7077896 | tf_op jit(solution)/shard_map/ppermute | solution.py:522
  117.8 14.5 %collective-permute-start.3 = (bf16[768,1536]{1,0:T(8,128)(2,1)}, bf16[768,1536]{1,0:T(8,128)(2,1)S(1)}, u32[]{:S(2)}, u32[]{:S(2)}) collective-permute-start(bf16[768,1536]{1,0:T(8,128)(2,1)} %get-tuple-element.107.refs_8_), channel_id=1, source_target_pairs={{0,1},{1,0},{2,3},{3,2},{4,5},{5,4},{6,7},{7,6},{8,9},{9,8},{10,11... | collective-permute-start | bytes 7077896 | tf_op jit(solution)/shard_map/ppermute | solution.py:522
  118.1 14.2 %copy-start.6 = (bf16[3072,384]{1,0:T(8,128)(2,1)S(1)}, bf16[3072,384]{1,0:T(8,128)(2,1)}, u32[]{:S(2)}) copy-start(bf16[3072,384]{1,0:T(8,128)(2,1)} %get-tuple-element.106) | copy-start | bytes 7077892
  118.1 14.2 %copy-start.7 = (bf16[768,1536]{1,0:T(8,128)(2,1)S(1)}, bf16[768,1536]{1,0:T(8,128)(2,1)}, u32[]{:S(2)}) copy-start(bf16[768,1536]{1,0:T(8,128)(2,1)} %get-tuple-element.108) | copy-start | bytes 7077892
  132.1 46.5 %collective-permute-start.6 = (bf16[768,384]{1,0:T(8,128)(2,1)S(1)}, bf16[768,384]{1,0:T(8,128)(2,1)S(1)}, u32[]{:S(2)}, u32[]{:S(2)}) collective-permute-start(bf16[768,384]{1,0:T(8,128)(2,1)S(1)} %get-tuple-element.117.refs_20_), channel_id=1, source_target_pairs={{0,1},{1,0},{2,3},{3,2},{4,5},{5,4},{6,7},{7,6},{8,9},{9,8},{10,11... | collective-permute-start | bytes 1769480 | tf_op jit(solution)/shard_map/ppermute | solution.py:522
  135.5 43.1 %collective-permute-start.4 = (bf16[1536,384]{1,0:T(8,128)(2,1)}, bf16[1536,384]{1,0:T(8,128)(2,1)S(1)}, u32[]{:S(2)}, u32[]{:S(2)}) collective-permute-start(bf16[1536,384]{1,0:T(8,128)(2,1)} %get-tuple-element.114.refs_18_), channel_id=1, source_target_pairs={{0,2},{2,0},{4,6},{6,4},{8,10},{10,8},{12,14},{14,12},{16,18},{18,... | collective-permute-start | bytes 3538952 | tf_op jit(solution)/shard_map/ppermute | solution.py:522
  138.2 40.4 %collective-permute-start.5 = (bf16[1536,384]{1,0:T(8,128)(2,1)}, bf16[1536,384]{1,0:T(8,128)(2,1)S(1)}, u32[]{:S(2)}, u32[]{:S(2)}) collective-permute-start(bf16[1536,384]{1,0:T(8,128)(2,1)} %get-tuple-element.116.refs_19_), channel_id=1, source_target_pairs={{0,4},{2,6},{4,0},{6,2},{8,12},{10,14},{12,8},{14,10},{16,20},{18,... | collective-permute-start | bytes 3538952 | tf_op jit(solution)/shard_map/ppermute | solution.py:522
  158.8 19.8 %collective-permute-start.7 = (bf16[768,384]{1,0:T(8,128)(2,1)S(1)}, bf16[768,384]{1,0:T(8,128)(2,1)S(1)}, u32[]{:S(2)}, u32[]{:S(2)}) collective-permute-start(bf16[768,384]{1,0:T(8,128)(2,1)S(1)} %get-tuple-element.122.refs_18_), channel_id=1, source_target_pairs={{0,1},{1,0},{2,3},{3,2},{4,5},{5,4},{6,7},{7,6},{8,9},{9,8},{10,11... | collective-permute-start | bytes 1769480 | tf_op jit(solution)/shard_map/ppermute | solution.py:522
  158.8 19.8 %copy-start.4 = (bf16[3072,384]{1,0:T(8,128)(2,1)S(1)}, bf16[3072,384]{1,0:T(8,128)(2,1)}, u32[]{:S(2)}) copy-start(bf16[3072,384]{1,0:T(8,128)(2,1)} %get-tuple-element.115.refs_17_.refs_1_) | copy-start | bytes 7077892
  178.1 28.9 %collective-permute-start.14 = (bf16[768,384]{1,0:T(8,128)(2,1)S(1)}, bf16[768,384]{1,0:T(8,128)(2,1)S(1)}, u32[]{:S(2)}, u32[]{:S(2)}) collective-permute-start(bf16[768,384]{1,0:T(8,128)(2,1)S(1)} %get-tuple-element.134.refs_22_), channel_id=1, source_target_pairs={{0,1},{1,0},{2,3},{3,2},{4,5},{5,4},{6,7},{7,6},{8,9},{9,8},{10,11... | collective-permute-start | bytes 1769480 | tf_op jit(solution)/shard_map/ppermute | solution.py:522
  181.0 22.5 %collective-permute-start.10 = (bf16[768,384]{1,0:T(8,128)(2,1)S(1)}, bf16[768,384]{1,0:T(8,128)(2,1)S(1)}, u32[]{:S(2)}, u32[]{:S(2)}) collective-permute-start(bf16[768,384]{1,0:T(8,128)(2,1)S(1)} %get-tuple-element.131.refs_21_), channel_id=1, source_target_pairs={{0,2},{2,0},{4,6},{6,4},{8,10},{10,8},{12,14},{14,12},{16,18},{18,... | collective-permute-start | bytes 1769480 | tf_op jit(solution)/shard_map/ppermute | solution.py:522
  181.6 22.5 %collective-permute-start.8 = (bf16[768,384]{1,0:T(8,128)(2,1)S(1)}, bf16[768,384]{1,0:T(8,128)(2,1)S(1)}, u32[]{:S(2)}, u32[]{:S(2)}) collective-permute-start(bf16[768,384]{1,0:T(8,128)(2,1)S(1)} %get-tuple-element.128.refs_19_), channel_id=1, source_target_pairs={{0,4},{2,6},{4,0},{6,2},{8,12},{10,14},{12,8},{14,10},{16,20},{18,... | collective-permute-start | bytes 1769480 | tf_op jit(solution)/shard_map/ppermute | solution.py:522
  181.6 22.5 %collective-permute-start.9 = (bf16[768,384]{1,0:T(8,128)(2,1)S(1)}, bf16[768,384]{1,0:T(8,128)(2,1)S(1)}, u32[]{:S(2)}, u32[]{:S(2)}) collective-permute-start(bf16[768,384]{1,0:T(8,128)(2,1)S(1)} %get-tuple-element.130.refs_20_), channel_id=1, source_target_pairs={{0,8},{2,10},{4,12},{6,14},{8,0},{10,2},{12,4},{14,6},{16,24},{18,... | collective-permute-start | bytes 1769480 | tf_op jit(solution)/shard_map/ppermute | solution.py:522
  183.7 20.4 %copy-start.5 = (bf16[2304,384]{1,0:T(8,128)(2,1)S(1)}, bf16[2304,384]{1,0:T(8,128)(2,1)}, u32[]{:S(2)}) copy-start(bf16[2304,384]{1,0:T(8,128)(2,1)} %get-tuple-element.129.refs_18_.refs_1_) | copy-start | bytes 5308420
  203.5 13.4 %collective-permute-start.15 = (bf16[768,384]{1,0:T(8,128)(2,1)S(1)}, bf16[768,384]{1,0:T(8,128)(2,1)S(1)}, u32[]{:S(2)}, u32[]{:S(2)}) collective-permute-start(bf16[768,384]{1,0:T(8,128)(2,1)S(1)} %get-tuple-element.140.refs_19_), channel_id=1, source_target_pairs={{0,1},{1,0},{2,3},{3,2},{4,5},{5,4},{6,7},{7,6},{8,9},{9,8},{10,11... | collective-permute-start | bytes 1769480 | tf_op jit(solution)/shard_map/ppermute | solution.py:522
  203.6 13.3 %collective-permute-start.16 = (f32[16,384]{1,0:T(8,128)S(1)}, f32[16,384]{1,0:T(8,128)S(1)}, u32[]{:S(2)}, u32[]{:S(2)}) collective-permute-start(f32[16,384]{1,0:T(8,128)S(1)} %get-tuple-element.143.refs_20_.refs_8_), channel_id=1, source_target_pairs={{0,1},{1,0},{2,3},{3,2},{4,5},{5,4},{6,7},{7,6},{8,9},{9,8},{10,11... | collective-permute-start | bytes 73736 | tf_op jit(solution)/shard_map/ppermute | solution.py:522
  205.1 11.9 %collective-permute-start.11 = (bf16[384,384]{1,0:T(8,128)(2,1)S(1)}, bf16[384,384]{1,0:T(8,128)(2,1)S(1)}, u32[]{:S(2)}, u32[]{:S(2)}) collective-permute-start(bf16[384,384]{1,0:T(8,128)(2,1)S(1)} %get-tuple-element.136.refs_16_), channel_id=1, source_target_pairs={{0,8},{2,10},{4,12},{6,14},{8,0},{10,2},{12,4},{14,6},{16,24},{18,... | collective-permute-start | bytes 884744 | tf_op jit(solution)/shard_map/ppermute | solution.py:522
  205.1 11.8 %collective-permute-start.12 = (bf16[384,384]{1,0:T(8,128)(2,1)S(1)}, bf16[384,384]{1,0:T(8,128)(2,1)S(1)}, u32[]{:S(2)}, u32[]{:S(2)}) collective-permute-start(bf16[384,384]{1,0:T(8,128)(2,1)S(1)} %get-tuple-element.138.refs_17_), channel_id=1, source_target_pairs={{0,2},{2,0},{4,6},{6,4},{8,10},{10,8},{12,14},{14,12},{16,18},{18,... | collective-permute-start | bytes 884744 | tf_op jit(solution)/shard_map/ppermute | solution.py:522
  207.1 9.9 %collective-permute-start.13 = (bf16[384,384]{1,0:T(8,128)(2,1)S(1)}, bf16[384,384]{1,0:T(8,128)(2,1)S(1)}, u32[]{:S(2)}, u32[]{:S(2)}) collective-permute-start(bf16[384,384]{1,0:T(8,128)(2,1)S(1)} %get-tuple-element.139.refs_18_), channel_id=1, source_target_pairs={{0,4},{2,6},{4,0},{6,2},{8,12},{10,14},{12,8},{14,10},{16,20},{18,... | collective-permute-start | bytes 884744 | tf_op jit(solution)/shard_map/ppermute | solution.py:522
  218.0 24.4 %collective-permute-start.18 = (bf16[416,384]{1,0:T(8,128)(2,1)S(1)}, bf16[416,384]{1,0:T(8,128)(2,1)S(1)}, u32[]{:S(2)}, u32[]{:S(2)}) collective-permute-start(bf16[416,384]{1,0:T(8,128)(2,1)S(1)} %get-tuple-element.154.refs_6_), channel_id=1, source_target_pairs={{0,2},{2,0},{4,6},{6,4},{8,10},{10,8},{12,14},{14,12},{16,18},{18,... | collective-permute-start | bytes 958472 | tf_op jit(solution)/shard_map/ppermute | solution.py:522
  218.6 23.8 %collective-permute-start.19 = (bf16[416,384]{1,0:T(8,128)(2,1)S(1)}, bf16[416,384]{1,0:T(8,128)(2,1)S(1)}, u32[]{:S(2)}, u32[]{:S(2)}) collective-permute-start(bf16[416,384]{1,0:T(8,128)(2,1)S(1)} %get-tuple-element.155.refs_7_), channel_id=1, source_target_pairs={{0,4},{2,6},{4,0},{6,2},{8,12},{10,14},{12,8},{14,10},{16,20},{18,... | collective-permute-start | bytes 958472 | tf_op jit(solution)/shard_map/ppermute | solution.py:522
  218.8 23.7 %collective-permute-start.20 = (bf16[416,384]{1,0:T(8,128)(2,1)S(1)}, bf16[416,384]{1,0:T(8,128)(2,1)S(1)}, u32[]{:S(2)}, u32[]{:S(2)}) collective-permute-start(bf16[416,384]{1,0:T(8,128)(2,1)S(1)} %get-tuple-element.156.refs_8_), channel_id=1, source_target_pairs={{0,6},{2,4},{4,2},{6,0},{8,14},{10,12},{12,10},{14,8},{16,22},{18,... | collective-permute-start | bytes 958472 | tf_op jit(solution)/shard_map/ppermute | solution.py:522
  221.6 20.8 %collective-permute-start.21 = (bf16[384,384]{1,0:T(8,128)(2,1)S(1)}, bf16[384,384]{1,0:T(8,128)(2,1)S(1)}, u32[]{:S(2)}, u32[]{:S(2)}) collective-permute-start(bf16[384,384]{1,0:T(8,128)(2,1)S(1)} %get-tuple-element.157.refs_4_), channel_id=1, source_target_pairs={{0,16},{2,18},{4,20},{6,22},{8,24},{10,26},{12,28},{14,30},{16,0},... | collective-permute-start | bytes 884744 | tf_op jit(solution)/shard_map/ppermute | solution.py:522
  224.2 18.2 %collective-permute-start.17 = (bf16[192,384]{1,0:T(8,128)(2,1)S(1)}, bf16[192,384]{1,0:T(8,128)(2,1)S(1)}, u32[]{:S(2)}, u32[]{:S(2)}) collective-permute-start(bf16[192,384]{1,0:T(8,128)(2,1)S(1)} %get-tuple-element.152.refs_5_), channel_id=1, source_target_pairs={{0,8},{2,10},{4,12},{6,14},{8,0},{10,2},{12,4},{14,6},{16,24},{18,... | collective-permute-start | bytes 442376 | tf_op jit(solution)/shard_map/ppermute | solution.py:522
  244.0 16.7 %collective-permute-start.22 = (bf16[1024,768]{1,0:T(8,128)(2,1)}, bf16[1024,768]{1,0:T(8,128)(2,1)S(1)}, u32[]{:S(2)}, u32[]{:S(2)}) collective-permute-start(bf16[1024,768]{1,0:T(8,128)(2,1)} %get-tuple-element.161.refs_20_), channel_id=1, source_target_pairs={{0,1},{1,0},{2,3},{3,2},{4,5},{5,4},{6,7},{7,6},{8,9},{9,8},{10,11... | collective-permute-start | bytes 4718600 | tf_op jit(solution)/shard_map/ppermute | solution.py:522
  244.0 16.7 %collective-permute-start.23 = (bf16[1024,768]{1,0:T(8,128)(2,1)}, bf16[1024,768]{1,0:T(8,128)(2,1)S(1)}, u32[]{:S(2)}, u32[]{:S(2)}) collective-permute-start(bf16[1024,768]{1,0:T(8,128)(2,1)} %get-tuple-element.162.refs_19_), channel_id=1, source_target_pairs={{0,1},{1,0},{2,3},{3,2},{4,5},{5,4},{6,7},{7,6},{8,9},{9,8},{10,11... | collective-permute-start | bytes 4718600 | tf_op jit(solution)/shard_map/ppermute | solution.py:522
  244.5 13.1 %collective-permute-start.24 = (bf16[224,384]{1,0:T(8,128)(2,1)S(1)}, bf16[224,384]{1,0:T(8,128)(2,1)S(1)}, u32[]{:S(2)}, u32[]{:S(2)}) collective-permute-start(bf16[224,384]{1,0:T(8,128)(2,1)S(1)} %get-tuple-element.166.refs_16_), channel_id=1, source_target_pairs={{0,16},{2,18},{4,20},{6,22},{8,24},{10,26},{12,28},{14,30},{16,0},... | collective-permute-start | bytes 516104 | tf_op jit(solution)/shard_map/ppermute | solution.py:522
  244.8 12.8 %collective-permute-start.25 = (bf16[128,384]{1,0:T(8,128)(2,1)S(1)}, bf16[128,384]{1,0:T(8,128)(2,1)S(1)}, u32[]{:S(2)}, u32[]{:S(2)}) collective-permute-start(bf16[128,384]{1,0:T(8,128)(2,1)S(1)} %get-tuple-element.167.refs_17_), channel_id=1, source_target_pairs={{0,8},{2,10},{4,12},{6,14},{8,0},{10,2},{12,4},{14,6},{16,24},{18,... | collective-permute-start | bytes 294920 | tf_op jit(solution)/shard_map/ppermute | solution.py:522
  245.3 12.3 %collective-permute-start.26 = (bf16[128,384]{1,0:T(8,128)(2,1)S(1)}, bf16[128,384]{1,0:T(8,128)(2,1)S(1)}, u32[]{:S(2)}, u32[]{:S(2)}) collective-permute-start(bf16[128,384]{1,0:T(8,128)(2,1)S(1)} %get-tuple-element.168.refs_18_), channel_id=1, source_target_pairs={{0,24},{2,26},{4,28},{6,30},{8,16},{10,18},{12,20},{14,22},{16,8},... | collective-permute-start | bytes 294920 | tf_op jit(solution)/shard_map/ppermute | solution.py:522
  (7 other events, 32.6 us)
